TPU v7x, 256 devices: a whole 4x4x8 slice. The times are simulated.
256 devices in a mesh: spatial: 16 (over z, core), head: 4 (over x), dp: 4 (over y).
Axes of the slice: x: 4, y: 4, z: 8, core: 2. Of those that a mesh axis runs over, the one named last changes fastest.
Arguments:
- tokens: bfloat16 [4, 4096, 1024], P('dp', 'spatial'), may hold values from -6 to 6
- neighbours: int32 [4, 64, 27], P('dp', 'spatial'), may hold values from -1 to 63, as said below
- counts: int32 [4, 64], P('dp'), may hold values from 1 to 64, as said below
- w_qkv: bfloat16 [3, 1024, 1024], P(None, None, 'head'), may hold values from -0.1875 to 0.1875
- w_out: bfloat16 [1024, 1024], P('head'), may hold values from -0.1875 to 0.1875
- cotangent: bfloat16 [4, 4096, 1024], P('dp', 'spatial'), may hold values from -6 to 6
Outputs:
- layer_out: bfloat16 [4, 4096, 1024], P('dp', 'spatial', 'head')
- grad_tokens: bfloat16 [4, 4096, 1024], P('dp', 'spatial', 'head')
- grad_qkv: float32 [3, 1024, 1024], P(None, None, 'head')
- grad_out: float32 [1024, 1024], P('head')
Inputs may be any that keep to these rules, and one draw needn't show every extreme that they name: neighbours[s, b, 0] = b; every other entry is -1 (an empty slot) or a block c with 0 < |c - b| <= 4; no block appears twice in a row; in every scene some block lists the block exactly 4 after it. `counts`: the occupied tokens of a block fill its first slots.
All inputs are finite; a program needn't handle non-finite values.
Results may differ from a plain program's by a relative error of at most 0.012.
The roundings to bfloat16 on the way count: a program that leaves them out, or rounds other values in their place, can miss the bound.
Values may be sent and summed in bfloat16 or wider, within the bound.
No kernel may reach another device: no remote copies, remote signals or barrier semaphores. Data moves between devices by JAX's collectives and lax.ppermute only.
A program may use at most 192 MiB of HBM per device.

v0:
```python
import jax
import jax.numpy as jnp
from jax import lax
from jax.sharding import PartitionSpec as P

HD = 64
BLOCK = 64
NBR = 27


def extended(x, sides, width):
    for axis, dim in sides:
        peers, length = (lax.axis_size(axis), x.shape[dim])
        up = [(i, (i + 1) % peers) for i in range(peers - 1)]
        down = [(j, i) for i, j in up]
        last = lax.slice_in_dim(x, length - width, length, axis=dim)
        leading = lax.slice_in_dim(x, 0, width, axis=dim)
        before = lax.ppermute(last, axis, up)
        after = lax.ppermute(leading, axis, down)
        x = jnp.concatenate([before, x, after], axis=dim)
    return x


def per_device(tokens, neighbours, counts, w_qkv, w_out, cotangent):
    inputs = tokens[0]
    block_ids = neighbours[0]
    occupied = counts[0]
    scene_cot = cotangent[0]
    tok_rows = inputs.shape[0]
    blocks = tok_rows // BLOCK
    width = w_qkv.shape[2]
    heads_here = width // HD
    factor = HD ** (-0.5)
    queries = jnp.dot(inputs, w_qkv[0], preferred_element_type=jnp.float32).astype(jnp.bfloat16)
    keys_loc = jnp.dot(inputs, w_qkv[1], preferred_element_type=jnp.float32).astype(jnp.bfloat16)
    values_loc = jnp.dot(inputs, w_qkv[2], preferred_element_type=jnp.float32).astype(jnp.bfloat16)
    paired = jnp.concatenate([keys_loc, values_loc], axis=1)
    window = extended(paired, (("spatial", 0),), tok_rows)
    win_keys = window[:, :width].reshape(3 * blocks, BLOCK, heads_here, HD)
    win_values = window[:, width:].reshape(3 * blocks, BLOCK, heads_here, HD)
    window_base = lax.axis_index("spatial") * blocks - blocks
    upstream = jnp.dot(scene_cot, w_out.T, preferred_element_type=jnp.float32).astype(jnp.bfloat16)
    q_blocks = queries.reshape(blocks, BLOCK, heads_here, HD)
    up_blocks = upstream.reshape(blocks, BLOCK, heads_here, HD)
    group_size = min(blocks, 8)
    slots = jnp.arange(BLOCK, dtype=jnp.int32)
    table = jnp.arange(occupied.shape[0], dtype=jnp.int32)

    def one_group(running, group_idx):
        key_grad, value_grad = running
        clipped = jnp.maximum(block_ids, 0)
        looked = jnp.sum(jnp.where(clipped[:, :, None] == table, occupied, 0), axis=-1)
        usable = (block_ids >= 0)[:, :, None] & (slots[None, None, :] < looked[:, :, None])
        usable = usable.reshape(group_size, NBR * BLOCK)
        window_idx = jnp.clip(block_ids - window_base, 0, 3 * blocks - 1)
        near_keys = win_keys[window_idx].reshape(group_size, NBR * BLOCK, heads_here, HD)
        near_values = win_values[window_idx].reshape(group_size, NBR * BLOCK, heads_here, HD)
        scores = (
            jnp.einsum("gqhd,gkhd->ghqk", q_blocks, near_keys, preferred_element_type=jnp.float32)
            * factor
        )
        weights = jnp.where(usable[:, None, None, :], jnp.exp(scores), 0.0)
        probs = weights / jnp.sum(weights, axis=-1, keepdims=True)
        probs_low = probs.astype(jnp.bfloat16)
        attended = jnp.einsum(
            "ghqk,gkhd->gqhd", probs_low, near_values, preferred_element_type=jnp.float32
        ).astype(jnp.bfloat16)
        dprob = jnp.einsum(
            "gqhd,gkhd->ghqk", up_blocks, near_values, preferred_element_type=jnp.float32
        )
        spread = jnp.sum(probs * dprob, axis=-1, keepdims=True)
        dscore = (probs * (dprob - spread) * factor).astype(jnp.bfloat16)
        query_grad = jnp.einsum(
            "ghqk,gkhd->gqhd", dscore, near_keys, preferred_element_type=jnp.float32
        ).astype(jnp.bfloat16)
        key_part = jnp.einsum(
            "ghqk,gqhd->gkhd", dscore, q_blocks, preferred_element_type=jnp.float32
        )
        value_part = jnp.einsum(
            "ghqk,gqhd->gkhd", probs_low, up_blocks, preferred_element_type=jnp.float32
        )
        key_grad = key_grad.at[window_idx].add(
            key_part.reshape(group_size, NBR, BLOCK, heads_here, HD)
        )
        value_grad = value_grad.at[window_idx].add(
            value_part.reshape(group_size, NBR, BLOCK, heads_here, HD)
        )
        return ((key_grad, value_grad), (attended, query_grad))

    empty = jnp.zeros((3 * blocks, BLOCK, heads_here, HD), jnp.float32)
    steps_idx = jnp.arange(blocks // group_size, dtype=jnp.int32)
    (key_grad, value_grad), (attended, query_grad) = lax.scan(one_group, (empty, empty), steps_idx)
    attended = attended.reshape(tok_rows, width)
    query_grad = query_grad.reshape(tok_rows, width)
    feat_width = inputs.shape[1] // lax.axis_size("head")
    feat_begin = lax.axis_index("head") * feat_width
    input_slice = lax.dynamic_slice_in_dim(inputs, feat_begin, feat_width, 1)
    cot_slice = lax.dynamic_slice_in_dim(scene_cot, feat_begin, feat_width, 1)
    partial_out = jnp.dot(attended, w_out, preferred_element_type=jnp.float32)
    summed_out = lax.psum_scatter(partial_out, "head", scatter_dimension=1, tiled=True)
    layer_out = (input_slice.astype(jnp.float32) + summed_out).astype(jnp.bfloat16)
    stacked = jnp.concatenate(
        [key_grad.reshape(3 * tok_rows, width), value_grad.reshape(3 * tok_rows, width)], axis=1
    )
    rim_rows = jnp.concatenate([stacked[:tok_rows], stacked[2 * tok_rows :]], axis=0)
    arrived = extended(rim_rows, (("spatial", 0),), tok_rows)
    own_grads = stacked[tok_rows : 2 * tok_rows] + arrived[:tok_rows] + arrived[3 * tok_rows :]
    key_low = own_grads[:, :width].astype(jnp.bfloat16)
    value_low = own_grads[:, width:].astype(jnp.bfloat16)
    inner = jnp.dot(query_grad, w_qkv[0].T, preferred_element_type=jnp.float32)
    inner = inner + jnp.dot(key_low, w_qkv[1].T, preferred_element_type=jnp.float32)
    inner = inner + jnp.dot(value_low, w_qkv[2].T, preferred_element_type=jnp.float32)
    summed_in = lax.psum_scatter(inner, "head", scatter_dimension=1, tiled=True)
    grad_tokens = (cot_slice.astype(jnp.float32) + summed_in).astype(jnp.bfloat16)
    qkv_terms = jnp.stack(
        [
            jnp.einsum("td,tw->dw", inputs, which_grad, preferred_element_type=jnp.float32)
            for which_grad in (query_grad, key_low, value_low)
        ]
    )
    out_term = jnp.einsum("tw,td->wd", attended, scene_cot, preferred_element_type=jnp.float32)
    qkv_grad, out_grad = lax.psum((qkv_terms, out_term), ("spatial", "dp"))
    return (layer_out[None], grad_tokens[None], qkv_grad, out_grad)


def solution(mesh):
    in_specs = (
        P("dp", "spatial", None),
        P("dp", "spatial", None),
        P("dp", None),
        P(None, None, "head"),
        P("head", None),
        P("dp", "spatial", None),
    )
    out_specs = (
        P("dp", "spatial", "head"),
        P("dp", "spatial", "head"),
        P(None, None, "head"),
        P("head", None),
    )
    return jax.shard_map(
        per_device, mesh=mesh, in_specs=in_specs, out_specs=out_specs, check_vma=False
    )
```

profile of v0, /device:TPU:1, one launch (start us, length us, event | category | flops | bytes accessed | tf_op | source)
XLA Modules:
  0.0 487.2 jit_solution(80543166588312614)
XLA Ops:
  8.1 1.6 convolution_convert_fusion.2
  9.7 1.5 convolution_convert_fusion.3
  11.2 5.2 %collective-permute-start.1 = (bf16[256,512]{0,1:T(8,128)(2,1)S(1)}, bf16[256,512]{0,1:T(8,128)(2,1)S(1)}, u32[]{:S(2)}, u32[]{:S(2)}) collective-permute-start(bf16[256,512]{0,1:T(8,128)(2,1)S(1)} %pad_maximum_fusion.2), channel_id=1, source_target_pairs={{16,0},{32,16},{48,32},{64,48},{80,64},{96,80},{112,96},{128,112},... | collective-permute-start | bytes 786440 | tf_op jit(solution)/shard_map/ppermute | solution.py:19
  16.4 1.9 collective-permute-start
  18.3 0.7 compare_bitcast_fusion
  19.0 0.7 maximum_bitcast_fusion
  19.7 1.5 convolution_convert_fusion.1
  21.2 0.7 compare_select_fusion
  22.3 1.3 select_reduce_fusion
  24.1 0.2 copy.54
  24.3 1.4 convolution_convert_fusion
  25.9 0.2 copy.58
  26.2 0.6 reshape.189
  26.8 1.0 copy.39
  27.9 6.1 %gather_fusion = bf16[108,64,4,64]{3,1,2,0:T(8,128)(2,1)} fusion(bf16[12,64,4,64]{3,1,2,0:T(8,128)(2,1)S(1)} %copy.39, s32[1024]{0:T(1024)S(1)} %pad_clamp_fusion), kind=kCustom, calls=%fused_computation | custom fusion | bytes 7078320 | tf_op jit(solution)/shard_map/while/body/eval_jaxpr/gather | solution.py:57
  34.0 10.6 %copy.40 = bf16[108,64,4,64]{1,0,3,2:T(8,128)(2,1)} copy(bf16[108,64,4,64]{3,1,2,0:T(8,128)(2,1)} %gather_fusion) | data formatting | bytes 7077888 | tf_op jit(solution)/shard_map/while/body/eval_jaxpr/gather | solution.py:57
  44.6 11.0 %reshape.136 = bf16[4,1728,4,64]{1,0,3,2:T(4,128)(2,1)} reshape(bf16[108,64,4,64]{1,0,3,2:T(8,128)(2,1)} %copy.40) | data formatting | bytes 7077888 | tf_op jit(solution)/shard_map/while/body/eval_jaxpr/reshape | solution.py:57
  55.6 0.6 reshape.190
  56.2 0.9 copy.44
  57.1 6.1 %gather_fusion.1 = bf16[108,64,4,64]{3,1,2,0:T(8,128)(2,1)} fusion(bf16[12,64,4,64]{3,1,2,0:T(8,128)(2,1)S(1)} %copy.44, s32[1024]{0:T(1024)S(1)} %pad_clamp_fusion), kind=kCustom, calls=%fused_computation.1 | custom fusion | bytes 7078320 | tf_op jit(solution)/shard_map/while/body/eval_jaxpr/gather | solution.py:56
  63.2 10.6 %copy.45 = bf16[108,64,4,64]{1,0,3,2:T(8,128)(2,1)} copy(bf16[108,64,4,64]{3,1,2,0:T(8,128)(2,1)} %gather_fusion.1) | data formatting | bytes 7077888 | tf_op jit(solution)/shard_map/while/body/eval_jaxpr/gather | solution.py:56
  73.8 11.0 %reshape.139 = bf16[4,1728,4,64]{1,0,3,2:T(4,128)(2,1)} reshape(bf16[108,64,4,64]{1,0,3,2:T(8,128)(2,1)} %copy.45) | data formatting | bytes 7077888 | tf_op jit(solution)/shard_map/while/body/eval_jaxpr/reshape | solution.py:56
  84.8 6.3 %fusion.11 = f32[4,4,64,1728]{3,2,1,0:T(8,128)} fusion(bf16[4,64,4,64]{1,3,2,0:T(8,128)(2,1)S(1)} %copy.58, bf16[4,1728,4,64]{1,0,3,2:T(4,128)(2,1)} %reshape.136), kind=kOutput, calls=%fused_computation.14 | convolution fusion | flops 226492416 | bytes 10747904 | tf_op jit(solution)/shard_map/while/body/eval_jaxpr/gqhd,gkhd->ghqk/dot_general | solution.py:68
  91.1 2.3 fusion.3
  93.4 2.2 fusion.30
  95.5 0.8 copy-done.4
  96.3 3.9 convolution_bitcast_fusion
  100.3 0.2 copy.49
  100.5 0.2 reshape.140
  100.7 1.3 fusion.84
  102.0 17.3 %convolution_bitcast_fusion.1 = f32[4,1728,4,64]{1,3,2,0:T(8,128)} fusion(bf16[4,64,4,64]{1,3,2,0:T(8,128)(2,1)S(1)} %copy.54, f32[4,4,64,1728]{3,2,1,0:T(8,128)} %fusion.11, f32[4,4,64,1728]{3,2,1,0:T(8,128)} %copy-done.4, f32[4,4,64]{2,1,0:T(4,128)S(1)} %get-tuple-element.91, pred[4,1728]{1,0:T(4,128)(4,1)S(1)} %compare_and_fusion), kind=kOutput, calls=%fused_computation.12 | convolution fusion | flops 245959360 | bytes 21375744 | tf_op jit(solution)/shard_map/while/body/eval_jaxpr/ghqk,gqhd->gkhd/dot_general | solution.py:76
  119.3 10.8 %copy.55 = f32[4,1728,4,64]{1,0,3,2:T(4,128)} copy(f32[4,1728,4,64]{1,3,2,0:T(8,128)} %convolution_bitcast_fusion.1) | data formatting | bytes 14155776 | tf_op jit(solution)/shard_map/while/body/eval_jaxpr/ghqk,gqhd->gkhd/transpose | solution.py:76
  130.1 13.1 %reshape.169 = f32[108,64,4,64]{1,0,3,2:T(8,128)} reshape(f32[4,1728,4,64]{1,0,3,2:T(4,128)} %copy.55) | data formatting | bytes 14155776 | tf_op jit(solution)/shard_map/while/body/eval_jaxpr/reshape | solution.py:83
  143.2 15.3 %copy.56 = f32[108,64,4,64]{3,1,2,0:T(8,128)} copy(f32[108,64,4,64]{1,0,3,2:T(8,128)} %reshape.169) | data formatting | bytes 14155776 | tf_op jit(solution)/shard_map/while/body/eval_jaxpr/reshape | solution.py:83
  158.6 21.0 %scatter_fusion = f32[12,64,4,64]{3,1,2,0:T(8,128)S(1)} fusion(f32[12,64,4,64]{3,1,2,0:T(8,128)S(1)} %broadcast_in_dim.71.clone, s32[108]{0:T(128)S(1)} %reshape.151, f32[108,64,4,64]{3,1,2,0:T(8,128)} %copy.56), kind=kCustom, calls=%fused_computation.2 | custom fusion | flops 1769472 | bytes 21234096 | tf_op jit(solution)/shard_map/while/body/eval_jaxpr/scatter-add | solution.py:82
  179.6 2.2 copy.57
  181.7 2.6 reshape.144
  184.4 10.7 %copy.59 = f32[4,1728,4,64]{1,0,3,2:T(4,128)} copy(f32[4,1728,4,64]{1,3,2,0:T(8,128)} %convolution_bitcast_fusion) | data formatting | bytes 14155776 | tf_op jit(solution)/shard_map/while/body/eval_jaxpr/ghqk,gqhd->gkhd/transpose | solution.py:79
  195.1 13.1 %reshape.177 = f32[108,64,4,64]{1,0,3,2:T(8,128)} reshape(f32[4,1728,4,64]{1,0,3,2:T(4,128)} %copy.59) | data formatting | bytes 14155776 | tf_op jit(solution)/shard_map/while/body/eval_jaxpr/reshape | solution.py:86
  208.2 15.3 %copy.60 = f32[108,64,4,64]{3,1,2,0:T(8,128)} copy(f32[108,64,4,64]{1,0,3,2:T(8,128)} %reshape.177) | data formatting | bytes 14155776 | tf_op jit(solution)/shard_map/while/body/eval_jaxpr/reshape | solution.py:86
  223.6 21.0 %scatter_fusion.1 = f32[12,64,4,64]{3,1,2,0:T(8,128)S(1)} fusion(f32[12,64,4,64]{3,1,2,0:T(8,128)S(1)} %broadcast_in_dim.71.clone.1, s32[108]{0:T(128)S(1)} %reshape.151, f32[108,64,4,64]{3,1,2,0:T(8,128)} %copy.60), kind=kCustom, calls=%fused_computation.3 | custom fusion | flops 1769472 | bytes 21234096 | tf_op jit(solution)/shard_map/while/body/eval_jaxpr/scatter-add | solution.py:85
  244.6 2.2 copy.61
  246.8 3.0 reshape.146
  249.9 1.2 constant_dynamic-update-slice_fusion
  251.2 1.0 fusion.82
  252.2 2.4 collective-permute-start.3
  254.6 3.3 collective-permute-start.2
  257.9 13.4 %fusion.35 = bf16[4,64,4,64]{1,3,2,0:T(8,128)(2,1)S(1)} fusion(f32[4,4,64,1728]{3,2,1,0:T(8,128)} %fusion.11, bf16[4,1728,4,64]{1,0,3,2:T(4,128)(2,1)} %reshape.139, f32[4,4,64,1728]{3,2,1,0:T(8,128)} %copy-done.4, f32[4,4,64]{2,1,0:T(4,128)S(1)} %copy-done.12, pred[4,1728]{1,0:T(4,128)(4,1)S(1)} %compare_and_fusion), kind=kOutput, calls=%fused_computation.32 | convolution fusion | flops 246024896 | bytes 17836800 | tf_op jit(solution)/shard_map/while/body/eval_jaxpr/ghqk,gkhd->gqhd/dot_general | solution.py:73
  271.3 0.2 copy.53
  271.5 0.2 reshape.142
  271.8 0.3 convolution_bitcast_fusion.4
  272.1 1.3 fusion.42
  273.4 1.3 fusion.41
  274.8 0.3 convolution_bitcast_fusion.2
  275.1 0.3 convolution_bitcast_fusion.3
  275.4 1.9 pad_maximum_fusion
  277.4 0.3 fusion.45
  277.8 0.3 convolution_add_fusion.1
  278.1 1.3 convolution_add_fusion
  279.5 1.6 fusion.66
  281.1 192.2 %all-reduce.3.cloned.1.call-done = (f32[3,1024,256]{1,2,0:T(8,128)}, f32[256,1024]{1,0:T(8,128)}) async-done(((f32[3,1024,256]{1,2,0:T(8,128)}, f32[256,1024]{1,0:T(8,128)}), (f32[3,1024,256]{1,2,0:T(8,128)}, f32[256,1024]{1,0:T(8,128)})) %all-reduce.3.cloned.1.call-update) | async-done | bytes 4194320 | tf_op jit(solution)/shard_map/psum | solution.py:122
  473.4 3.6 copy.62
  477.0 1.6 fusion.67
  478.6 1.0 copy.90
  (56 shorter events, 1.9 us)
Async XLA Ops:
  8.0 16.3 %copy-start = (bf16[256,1024]{1,0:T(8,128)(2,1)S(1)}, bf16[256,1024]{1,0:T(8,128)(2,1)}, u32[]{:S(2)}) copy-start(bf16[256,1024]{1,0:T(8,128)(2,1)} %param.10) | copy-start | bytes 1572868
  8.0 271.5 %reduce-scatter.3.cloned.1.call-start = ((), (), s32[]{:S(2)}) async-start(), calls=%async_computation.2 | async-start | bytes 1310720 | tf_op jit(solution)/shard_map/reduce_scatter | solution.py:100
  11.2 14.8 %collective-permute-start.1 = (bf16[256,512]{0,1:T(8,128)(2,1)S(1)}, bf16[256,512]{0,1:T(8,128)(2,1)S(1)}, u32[]{:S(2)}, u32[]{:S(2)}) collective-permute-start(bf16[256,512]{0,1:T(8,128)(2,1)S(1)} %pad_maximum_fusion.2), channel_id=1, source_target_pairs={{16,0},{32,16},{48,32},{64,48},{80,64},{96,80},{112,96},{128,112},... | collective-permute-start | bytes 786440 | tf_op jit(solution)/shard_map/ppermute | solution.py:19
  16.4 9.7 %collective-permute-start = (bf16[256,512]{0,1:T(8,128)(2,1)S(1)}, bf16[256,512]{0,1:T(8,128)(2,1)S(1)}, u32[]{:S(2)}, u32[]{:S(2)}) collective-permute-start(bf16[256,512]{0,1:T(8,128)(2,1)S(1)} %pad_maximum_fusion.2), channel_id=1, source_target_pairs={{0,16},{16,32},{32,48},{48,64},{64,80},{80,96},{96,112},{112,128},... | collective-permute-start | bytes 786440 | tf_op jit(solution)/shard_map/ppermute | solution.py:18
  84.8 6.3 %copy-start.2 = (bf16[4,1728,4,64]{1,0,3,2:T(4,128)(2,1)S(1)}, bf16[4,1728,4,64]{1,0,3,2:T(4,128)(2,1)}, u32[]{:S(2)}) copy-start(bf16[4,1728,4,64]{1,0,3,2:T(4,128)(2,1)} %reshape.139) | copy-start | bytes 10616836
  91.1 2.3 copy-start.3
  93.3 3.0 copy-start.4
  93.4 8.7 %copy-start.11 = (f32[4,4,64]{2,1,0:T(4,128)}, f32[4,4,64]{2,1,0:T(4,128)S(1)}, u32[]{:S(2)}) copy-start(f32[4,4,64]{2,1,0:T(4,128)S(1)} %get-tuple-element.91) | copy-start | bytes 12292
  102.0 371.4 %all-reduce.3.cloned.1.call-start = ((), (), s32[]{:S(2)}) async-start(), calls=%async_computation.4 | async-start | bytes 8388608 | tf_op jit(solution)/shard_map/psum | solution.py:122
  244.6 13.3 %copy-start.12 = (f32[4,4,64]{2,1,0:T(4,128)S(1)}, f32[4,4,64]{2,1,0:T(4,128)}, u32[]{:S(2)}) copy-start(f32[4,4,64]{2,1,0:T(4,128)} %copy-done.11) | copy-start | bytes 12292
  252.2 21.2 %collective-permute-start.3 = (f32[256,512]{1,0:T(8,128)}, f32[256,512]{1,0:T(8,128)}, u32[]{:S(2)}, u32[]{:S(2)}) collective-permute-start(f32[256,512]{1,0:T(8,128)} %get-tuple-element.88), channel_id=1, source_target_pairs={{16,0},{32,16},{48,32},{64,48},{80,64},{96,80},{112,96},{128,112},... | collective-permute-start | bytes 1572872 | tf_op jit(solution)/shard_map/ppermute | solution.py:19
  254.6 17.2 %copy-start.5 = (bf16[1,256,1024]{2,1,0:T(8,128)(2,1)S(1)}, bf16[1,256,1024]{2,1,0:T(8,128)(2,1)}, u32[]{:S(2)}) copy-start(bf16[1,256,1024]{2,1,0:T(8,128)(2,1)} %param.6) | copy-start | bytes 1572868
  254.6 17.5 %copy-start.6 = (bf16[1,256,1024]{2,1,0:T(8,128)(2,1)S(1)}, bf16[1,256,1024]{2,1,0:T(8,128)(2,1)}, u32[]{:S(2)}) copy-start(bf16[1,256,1024]{2,1,0:T(8,128)(2,1)} %param.11) | copy-start | bytes 1572868
  254.6 18.8 %collective-permute-start.2 = (f32[256,512]{1,0:T(8,128)}, f32[256,512]{1,0:T(8,128)}, u32[]{:S(2)}, u32[]{:S(2)}) collective-permute-start(f32[256,512]{1,0:T(8,128)} %get-tuple-element.87), channel_id=1, source_target_pairs={{0,16},{16,32},{32,48},{48,64},{64,80},{80,96},{96,112},{112,128},... | collective-permute-start | bytes 1572872 | tf_op jit(solution)/shard_map/ppermute | solution.py:18
  271.8 1.7 copy-start.8
  274.8 2.6 copy-start.7
  274.8 2.6 copy-start.9
  277.3 199.7 %reduce-scatter.5.cloned.1.call-start = ((), (), s32[]{:S(2)}) async-start(), calls=%async_computation.3 | async-start | bytes 1310720 | tf_op jit(solution)/shard_map/reduce_scatter | solution.py:113
  277.4 202.2 %copy-start.1 = (bf16[256,1024]{1,0:T(8,128)(2,1)S(1)}, bf16[256,1024]{1,0:T(8,128)(2,1)}, u32[]{:S(2)}) copy-start(bf16[256,1024]{1,0:T(8,128)(2,1)} %param.10) | copy-start | bytes 1572868
  473.4 5.3 %copy-start.10 = (f32[256,1024]{1,0:T(8,128)S(1)}, f32[256,1024]{1,0:T(8,128)}, u32[]{:S(2)}) copy-start(f32[256,1024]{1,0:T(8,128)} %get-tuple-element.96) | copy-start | bytes 3145732
Sparse Core Ops, SparseCore 0:
  102.1 26.5 reduce-scatter.2
  280.9 26.8 reduce-scatter.4
Sparse Core Ops, SparseCore 1:
  277.4 195.9 all-reduce.2
where the time goes:
time: 494 us; the launch traced here: 487 us
  waiting for transfers between devices  192 us (39%)
  local copies, waits for them, and re-layouts  157 us (32%)
  matrix products  56.9 us (12%)
  other arithmetic  51.9 us (11%)
  between operations  16.2 us (3%)
  starting transfers between devices  12.9 us (3%)
    psum x1, waiting for transfers between devices, per_device(): qkv_grad, out_grad = lax.psum((qkv_terms, out_term), ('spatial', 'dp'))  192 us
    reshape x2, local copies, waits for them, and re-layouts, one_group(): value_part.reshape(group_size, NBR, BLOCK, heads_here, HD)  28.3 us
    reshape x2, local copies, waits for them, and re-layouts, one_group(): key_part.reshape(group_size, NBR, BLOCK, heads_here, HD)  28.3 us
    scatter-add x1, other arithmetic, one_group(): key_grad.at[window_idx]  21 us
    scatter-add x1, other arithmetic, one_group(): value_grad.at[window_idx]  21 us
    dot_general x1, matrix products, one_group(): jnp.einsum('ghqk,gqhd->gkhd', dscore, q_blocks, preferred_element_type=jn...  17.3 us
    gather x2, local copies, waits for them, and re-layouts, one_group(): win_values[window_idx].reshape(group_size, NBR * BLOCK, heads_here, HD)  16.7 us
    gather x2, local copies, waits for them, and re-layouts, one_group(): win_keys[window_idx].reshape(group_size, NBR * BLOCK, heads_here, HD)  16.7 us
  transfers between devices with their start and end apart: 7, of which 1 were waited for; matrix products, arithmetic and copies ran while one was open for 38% of the time, Pallas kernels for 0%

commit v1 on v0

v1 whole, which is shorter than its diff:
```python
import functools

import jax
import jax.numpy as jnp
from jax import lax
from jax.experimental import pallas as pl
from jax.experimental.pallas import tpu as pltpu
from jax.sharding import PartitionSpec as P

HD = 64
BLOCK = 64
ROWS = 256
WIDTH = 256
D = 1024
REACH = 4
LOG2E = 1.4426950408889634
BF = jnp.bfloat16
F32 = jnp.float32
VMEM = pl.BlockSpec(memory_space=pltpu.VMEM)
SMEM = pl.BlockSpec(memory_space=pltpu.SMEM)


def call(kernel, outs, operands, flops, in_specs=None, scratch=(), vmem=24):
    moved = sum(a.size * a.dtype.itemsize for a in operands)
    moved += sum(o.size * o.dtype.itemsize for o in outs)
    return pl.pallas_call(
        kernel,
        out_shape=outs,
        in_specs=in_specs or [VMEM] * len(operands),
        out_specs=[VMEM] * len(outs),
        scratch_shapes=list(scratch),
        compiler_params=pltpu.CompilerParams(vmem_limit_bytes=vmem * 2**20),
        cost_estimate=pl.CostEstimate(flops=flops, bytes_accessed=moved, transcendentals=0),
    )(*operands)


def shape(dims, kind):
    return jax.ShapeDtypeStruct(dims, kind)


def nn(a, b):
    return lax.dot_general(a, b, (((1,), (0,)), ((), ())), preferred_element_type=F32)


def nt(a, b):
    return lax.dot_general(a, b, (((1,), (1,)), ((), ())), preferred_element_type=F32)


def tn(a, b):
    return lax.dot_general(a, b, (((0,), (0,)), ((), ())), preferred_element_type=F32)


def kv_kernel(x_ref, w_ref, out_ref):
    out_ref[0] = nn(x_ref[...], w_ref[0]).astype(BF)


def project_kv(x, w_qkv):
    return pl.pallas_call(
        kv_kernel,
        grid=(2,),
        out_shape=shape((2, ROWS, WIDTH), BF),
        in_specs=[
            pl.BlockSpec((ROWS, D), lambda i: (0, 0)),
            pl.BlockSpec((1, D, WIDTH), lambda i: (i + 1, 0, 0)),
        ],
        out_specs=pl.BlockSpec((1, ROWS, WIDTH), lambda i: (i, 0, 0)),
        cost_estimate=pl.CostEstimate(
            flops=4 * ROWS * D * WIDTH, bytes_accessed=2 * 2**20, transcendentals=0
        ),
    )(x, w_qkv)


def attention_kernel(q_ref, u_ref, before_ref, own_ref, after_ref, bias_ref, acts_ref, gb_ref, go_ref, ga_ref):
    factor = HD**-0.5
    window = (before_ref, own_ref, after_ref)
    grads = (gb_ref, go_ref, ga_ref)
    lane = lax.broadcasted_iota(jnp.int32, (1, 128), 1)
    picks = [(lane < HD).astype(F32).astype(BF), (lane >= HD).astype(F32).astype(BF)]
    first = lax.broadcasted_iota(jnp.int32, (ROWS, 128), 1) < HD
    bias = [
        jnp.concatenate(
            [
                jnp.broadcast_to(bias_ref[b : b + 1, c * ROWS : (c + 1) * ROWS], (BLOCK, ROWS))
                for b in range(ROWS // BLOCK)
            ],
            axis=0,
        )
        for c in range(3)
    ]
    for pair in range(WIDTH // 128):
        cols = slice(pair * 128, (pair + 1) * 128)
        q2, u2 = q_ref[:, cols], u_ref[:, cols]
        keys = [w[0, :, cols] for w in window]
        values = [w[1, :, cols] for w in window]
        key_sum, value_sum = [None] * 3, [None] * 3
        att, dq = [], []
        for pick in picks:
            qm, um = q2 * pick, u2 * pick
            weights = [jnp.exp2(nt(qm, keys[c]) * (factor * LOG2E) + bias[c]) for c in range(3)]
            total = sum(jnp.sum(w, axis=1, keepdims=True) for w in weights)
            share = 1.0 / total
            probs = [w * share for w in weights]
            low = [p.astype(BF) for p in probs]
            dprob = [nt(um, values[c]) for c in range(3)]
            spread = sum(jnp.sum(p * d, axis=1, keepdims=True) for p, d in zip(probs, dprob))
            dscore = [(p * (d - spread) * factor).astype(BF) for p, d in zip(probs, dprob)]
            att.append(sum(nn(low[c], values[c]) for c in range(3)))
            dq.append(sum(nn(dscore[c], keys[c]) for c in range(3)))
            for c in range(3):
                dk, dv = tn(dscore[c], qm), tn(low[c], um)
                key_sum[c] = dk if key_sum[c] is None else key_sum[c] + dk
                value_sum[c] = dv if value_sum[c] is None else value_sum[c] + dv
        acts_ref[0, :, cols] = jnp.where(first, att[0], att[1]).astype(BF)
        acts_ref[1, :, cols] = jnp.where(first, dq[0], dq[1]).astype(BF)
        for c in range(3):
            grads[c][0, :, cols] = key_sum[c].astype(grads[c].dtype)
            grads[c][1, :, cols] = value_sum[c].astype(grads[c].dtype)


def out_kernel(idx_ref, acts_ref, w_ref, own_ref, *sent):
    head = idx_ref[3]
    for k in range(4):
        start = pl.multiple_of(lax.rem(head + k, 4) * WIDTH, WIDTH)
        part = nn(acts_ref[0], w_ref[:, pl.ds(start, WIDTH)])
        if k == 0:
            own_ref[...] = part
        else:
            sent[k - 1][...] = part.astype(BF)


def in_kernel(idx_ref, acts_ref, dkv_ref, w_ref, own_ref, *sent):
    head = idx_ref[3]
    for k in range(4):
        rows = pl.ds(pl.multiple_of(lax.rem(head + k, 4) * WIDTH, WIDTH), WIDTH)
        part = nt(acts_ref[1], w_ref[0, rows, :])
        part = part + nt(dkv_ref[0], w_ref[1, rows, :])
        part = part + nt(dkv_ref[1], w_ref[2, rows, :])
        if k == 0:
            own_ref[...] = part
        else:
            sent[k - 1][...] = part.astype(BF)


def weight_kernel(a_ref, a2_ref, b_ref, b2_ref, left_ref, right_ref, *outs, order):
    for k in range(4):
        rows = slice(k * 128, (k + 1) * 128)
        g = nn(a_ref[rows, :], left_ref[order[0]]) + nn(a2_ref[rows, :], right_ref[order[0]])
        outs[k][:, :WIDTH] = g.astype(outs[k].dtype)
        g = nn(b_ref[rows, :], left_ref[order[1]]) + nn(b2_ref[rows, :], right_ref[order[1]])
        outs[k][:, WIDTH:] = g.astype(outs[k].dtype)


def ysum_kernel(*refs):
    ins, outs = refs[:8], refs[8:]
    for part in range(2):
        cols = slice(part * 512, (part + 1) * 512)
        four = ins[part * 4 : part * 4 + 4]
        for o, (begin, end) in zip(outs, ((0, 16), (16, 48), (48, 80), (80, 112), (112, 128))):
            total = four[0][begin:end, :]
            for r in four[1:]:
                total = total + r[begin:end, :].astype(F32)
            o[:, cols] = total.astype(o.dtype)


def zsum_kernel(idx_ref, own_ref, r1_ref, r2_ref, r3_ref, r4_ref, out_ref):
    total = r1_ref[...].astype(F32) + r2_ref[...].astype(F32) + r3_ref[...].astype(F32)
    half = own_ref[...] + r4_ref[...].astype(F32)
    core = idx_ref[1]
    out_ref[0:16, :] = (total[0:16] + half * (1 - core).astype(F32)).astype(BF)
    out_ref[16:32, :] = (total[16:32] + half * core.astype(F32)).astype(BF)


def place_kernel(idx_ref, *refs):
    mine, other, qkv_ref, out_ref, turned = refs[:4], refs[4:8], refs[8], refs[9], refs[10]
    z, core, y = idx_ref[0], idx_ref[1], idx_ref[2]
    for side, blocks in ((core, mine), (1 - core, other)):
        step = 2 * side - 1
        for k in range(4):
            base = lax.rem(y + 4 - k, 4) * 256
            pieces = [(0, 16, z * 32 + side * 16)]
            for j in (1, 2, 3):
                pieces.append((32 * j - 16, 32, lax.rem(z + step * j + 8, 8) * 32))
            pieces.append((112, 16, lax.rem(z + 4, 8) * 32 + side * 16))
            for begin, count, place in pieces:
                rows = pl.ds(pl.multiple_of(base + place, 16), count)
                piece = blocks[k][begin : begin + count, :].astype(F32)
                qkv_ref[0, rows, :] = piece[:, 0:256]
                turned[rows, :] = piece[:, 256:512]
                qkv_ref[1, rows, :] = piece[:, 512:768]
                qkv_ref[2, rows, :] = piece[:, 768:1024]
    out_ref[...] = turned[...].T


def row_of(z, y, side):
    p = jnp.arange(128, dtype=jnp.int32)
    j = (p - 16) // 32 + 1
    middle = (z + (1 - 2 * side) * j) % 8 * 32 + (p - 16) % 32
    row = jnp.where(
        p < 16,
        z * 32 + side * 16 + p,
        jnp.where(p < 112, middle, (z + 4) % 8 * 32 + side * 16 + p - 112),
    )
    k = jnp.arange(4, dtype=jnp.int32)
    return (((y + k) % 4 * 256)[:, None] + row[None, :]).reshape(512)


def per_device(tokens, neighbours, counts, w_qkv, w_out, cotangent):
    x, listed, occupied, cot = tokens[0], neighbours[0], counts[0], cotangent[0]
    spatial, head, y = (lax.axis_index(a) for a in ("spatial", "head", "dp"))
    z, core = spatial // 2, spatial % 2
    idx = jnp.stack([z, core, y, head]).astype(jnp.int32)
    n = 16
    up = [(i, i + 1) for i in range(n - 1)]
    down = [(i + 1, i) for i in range(n - 1)]
    swap = [(i, i ^ 1) for i in range(n)]

    def spread_z(j):
        return [(i, (i // 2 + (j if i % 2 == 0 else -j)) % 8 * 2 + i % 2) for i in range(n)]

    def ring(k):
        return [(i, (i + k) % 4) for i in range(4)]

    def swapped(a):
        return lax.ppermute(a, "spatial", swap)

    kv = project_kv(x, w_qkv)
    before = lax.ppermute(kv, "spatial", up)
    after = lax.ppermute(kv, "spatial", down)

    q = jnp.dot(x, w_qkv[0], preferred_element_type=F32).astype(BF)
    u = lax.dot_general(cot, w_out, (((1,), (1,)), ((), ())), preferred_element_type=F32).astype(BF)

    blocks = ROWS // BLOCK
    near = 3 * blocks
    ids = spatial * blocks - REACH + jnp.arange(near, dtype=jnp.int32)
    hit = jnp.any(listed[:, :, None] == ids[None, None, :], axis=1) & (ids >= 0)[None, :]
    padded = jnp.pad(occupied, (REACH, REACH))
    limit = lax.dynamic_slice_in_dim(padded, spatial * blocks, near, 0)
    limit = jnp.where(hit, limit[None, :], 0)
    slots = jnp.arange(BLOCK, dtype=jnp.int32)
    bias = jnp.where(slots[None, None, :] < limit[:, :, None], 0.0, -1e30).astype(F32)
    bias = bias.reshape(blocks, near * BLOCK)

    features = jnp.arange(D, dtype=jnp.int32)[:, None]
    pick_mine = (features == row_of(z, y, core)[None, :]).astype(BF)
    pick_other = (features == row_of(z, y, 1 - core)[None, :]).astype(BF)

    def picked(pick, a):
        return lax.dot_general(pick, a, (((0,), (1,)), ((), ())), preferred_element_type=F32).astype(BF)

    x_mine, x_other = picked(pick_mine, x), swapped(picked(pick_other, x))
    c_mine, c_other = picked(pick_mine, cot), swapped(picked(pick_other, cot))

    acts, grad_b, grad_o, grad_a = call(
        attention_kernel,
        [
            shape((2, ROWS, WIDTH), BF),
            shape((2, ROWS, WIDTH), BF),
            shape((2, ROWS, WIDTH), F32),
            shape((2, ROWS, WIDTH), BF),
        ],
        [q, u, before, kv, after, bias],
        10 * 256 * 768 * 256,
        vmem=32,
    )
    from_after = lax.ppermute(grad_b, "spatial", down)
    from_before = lax.ppermute(grad_a, "spatial", up)
    acts_other = swapped(acts)

    def sent_shapes():
        return [shape((ROWS, WIDTH), F32)] + [shape((ROWS, WIDTH), BF)] * 3

    def head_sum(parts, base):
        total = parts[0]
        for k in (1, 2, 3):
            total = total + lax.ppermute(parts[k], "head", ring(k)).astype(F32)
        own = lax.dynamic_slice_in_dim(base, head * WIDTH, WIDTH, 1)
        return (own.astype(F32) + total).astype(BF)

    with_idx = [SMEM] + [VMEM] * 2
    out_parts = call(out_kernel, sent_shapes(), [idx, acts, w_out], 2 * ROWS * WIDTH * D, with_idx)
    layer_out = head_sum(out_parts, x)

    part_shapes = [shape((128, 512), F32)] + [shape((128, 512), BF)] * 3

    def to_y(parts):
        return [parts[0]] + [lax.ppermute(parts[k], "dp", ring(k)) for k in (1, 2, 3)]

    g1 = to_y(
        call(
            functools.partial(weight_kernel, order=(1, 0)),
            part_shapes,
            [x_mine, x_other, c_mine, c_other, acts, acts_other],
            4 * 512 * 512 * 256,
        )
    )

    dkv = (grad_o + from_after.astype(F32) + from_before.astype(F32)).astype(BF)
    dkv_other = swapped(dkv)
    in_parts = call(
        in_kernel, sent_shapes(), [idx, acts, dkv, w_qkv], 6 * ROWS * WIDTH * D, [SMEM] + [VMEM] * 3
    )
    g2 = to_y(
        call(
            functools.partial(weight_kernel, order=(0, 1)),
            part_shapes,
            [x_mine, x_other, x_mine, x_other, dkv, dkv_other],
            4 * 512 * 512 * 256,
        )
    )
    grad_tokens = head_sum(in_parts, cot)

    own, *to_z = call(
        ysum_kernel,
        [shape((16, D), F32)] + [shape((32, D), BF)] * 3 + [shape((16, D), BF)],
        g1 + g2,
        2**20,
    )
    arrived = [lax.ppermute(a, "spatial", spread_z(j)) for j, a in zip((1, 2, 3, 4), to_z)]
    chunk = call(
        zsum_kernel, [shape((32, D), BF)], [idx, own] + arrived, 2**18, [SMEM] + [VMEM] * 5
    )[0]
    chunk = (chunk.astype(F32) + swapped(chunk).astype(F32)).astype(BF)
    half = lax.dynamic_slice_in_dim(chunk, core * 16, 16, 0)
    pieces = [half] + [lax.ppermute(chunk, "spatial", spread_z(j)) for j in (1, 2, 3)]
    pieces.append(lax.ppermute(half, "spatial", spread_z(4)))
    column = jnp.concatenate(pieces, axis=0)
    mine = [column] + [lax.ppermute(column, "dp", ring(k)) for k in (1, 2, 3)]
    other = [swapped(a) for a in mine]
    grad_qkv, grad_out = call(
        place_kernel,
        [shape((3, D, WIDTH), F32), shape((WIDTH, D), F32)],
        [idx] + mine + other,
        2**20,
        [SMEM] + [VMEM] * 8,
        scratch=[pltpu.VMEM((D, WIDTH), F32)],
    )
    return layer_out[None], grad_tokens[None], grad_qkv, grad_out


def solution(mesh):
    in_specs = (
        P("dp", "spatial", None),
        P("dp", "spatial", None),
        P("dp", None),
        P(None, None, "head"),
        P("head", None),
        P("dp", "spatial", None),
    )
    out_specs = (
        P("dp", "spatial", "head"),
        P("dp", "spatial", "head"),
        P(None, None, "head"),
        P("head", None),
    )
    return jax.shard_map(
        per_device, mesh=mesh, in_specs=in_specs, out_specs=out_specs, check_vma=False
    )
```

time: 494 us -> 121 us (0.24); the launches traced: 487 us -> 121 us
  waiting for transfers between devices: 192 us -> 31.6 us
  local copies, waits for them, and re-layouts: 157 us -> 3.12 us
  matrix products: 56.9 us -> 5.47 us
  other arithmetic: 51.9 us -> 4.2 us
  starting transfers between devices: 12.9 us -> 59.3 us
  Pallas kernels: 0 us -> 15.9 us
  between operations: 16.2 us -> 0.99 us
    psum x1 -> x0, waiting for transfers between devices: 192 us -> none  [per_device(): qkv_grad, out_grad = lax.psum((qkv_terms, out_term), ('spatial', 'dp'))]
    reshape x18 -> x0, local copies, waits for them, and re-layouts: 88.6 us -> none  [the longest x2 28.3 us: one_group(): value_part.reshape(group_size, NBR, BLOCK, heads_here, HD)]
    dot_general x18 -> x6, matrix products: 56.9 us -> 5.47 us  [the longest x4 2.66 us: picked(): lax.dot_general(pick, a, (((0,), (1,)), ((), ())), preferred_element_type...]
    ppermute x4 -> x36, starting transfers between devices: 12.8 us -> 59.3 us  [the longest x4 13.4 us: per_device(): lax.ppermute(a, 'spatial', spread_z(j))]
    scatter-add x2 -> x0, other arithmetic: 41.9 us -> none  [the longest x1 21 us: one_group(): key_grad.at[window_idx]]
    gather x4 -> x0, local copies, waits for them, and re-layouts: 33.4 us -> none  [the longest x2 16.7 us: one_group(): win_values[window_idx].reshape(group_size, NBR * BLOCK, heads_here, HD)]
    ppermute x4 -> x36, waiting for transfers between devices: 0.01 us -> 31.6 us  [the longest x3 8.21 us: per_device(): lax.ppermute(chunk, 'spatial', spread_z(j))]
    transpose x2 -> x0, local copies, waits for them, and re-layouts: 21.5 us -> none  [the longest x1 10.8 us: one_group(): jnp.einsum('ghqk,gqhd->gkhd', dscore, q_blocks, preferred_element_type=jn...]
  transfers between devices with their start and end apart: 7 -> 36, of which waited for: 1 -> 13; matrix products, arithmetic and copies ran while one was open for 38% -> 8% of each run, Pallas kernels for 0% -> 7%
where the time goes in v1:
time: 121 us
  starting transfers between devices  59.3 us (49%)
  waiting for transfers between devices  31.6 us (26%)
  Pallas kernels  15.9 us (13%)
  matrix products  5.47 us (5%)
  other arithmetic  4.2 us (3%)
  local copies, waits for them, and re-layouts  3.12 us (3%)
    ppermute x4, starting transfers between devices, per_device(): lax.ppermute(a, 'spatial', spread_z(j))  13.4 us
    pallas_call x8, Pallas kernels, call(): pl.pallas_call(kernel, out_shape=outs, in_specs=in_specs or [VMEM] * len(...  13.2 us
    ppermute x9, starting transfers between devices, swapped(): return lax.ppermute(a, 'spatial', swap)  12.3 us
    ppermute x3, waiting for transfers between devices, per_device(): lax.ppermute(chunk, 'spatial', spread_z(j))  8.21 us
    ppermute x6, starting transfers between devices, to_y(): lax.ppermute(parts[k], 'dp', ring(k))  7.36 us
    ppermute x6, waiting for transfers between devices, to_y(): lax.ppermute(parts[k], 'dp', ring(k))  6.57 us
    ppermute x1, waiting for transfers between devices, per_device(): pieces.append(lax.ppermute(half, 'spatial', spread_z(4)))  6.01 us
    ppermute x6, starting transfers between devices, head_sum(): total = total + lax.ppermute(parts[k], 'head', ring(k)).astype(F32)  5.75 us
  transfers between devices with their start and end apart: 36, of which 13 were waited for; matrix products, arithmetic and copies ran while one was open for 8% of the time, Pallas kernels for 7%

profile of v1, /device:TPU:1, one launch (start us, length us, event | category | flops | bytes accessed | tf_op | source)
XLA Modules:
  0.0 120.6 jit_solution(5561581047448306008)
XLA Ops:
  0.7 2.6 %shard_map.93.own_ref = bf16[2,256,256]{2,1,0:T(8,128)(2,1)} custom-call(bf16[256,1024]{1,0:T(8,128)(2,1)} %bitcast.38, bf16[3,1024,256]{2,1,0:T(8,128)(2,1)} %w_ref.5), custom_call_target="tpu_custom_call" | custom-call | flops 268435456 | bytes 2097152 | tf_op jit(solution)/shard_map/pallas_call | solution.py:58
  3.3 5.3 %collective-permute-start.1 = (bf16[2,256,256]{2,1,0:T(8,128)(2,1)}, bf16[2,256,256]{2,1,0:T(8,128)(2,1)S(1)}, u32[]{:S(2)}, u32[]{:S(2)}) collective-permute-start(bf16[2,256,256]{2,1,0:T(8,128)(2,1)} %shard_map.93.own_ref), channel_id=1, source_target_pairs={{16,0},{32,16},{48,32},{64,48},{80,64},{96,80},{112,96},{128,112},... | collective-permute-start | bytes 786440 | tf_op jit(solution)/shard_map/ppermute | solution.py:228
  8.6 1.9 %collective-permute-start = (bf16[2,256,256]{2,1,0:T(8,128)(2,1)}, bf16[2,256,256]{2,1,0:T(8,128)(2,1)S(1)}, u32[]{:S(2)}, u32[]{:S(2)}) collective-permute-start(bf16[2,256,256]{2,1,0:T(8,128)(2,1)} %shard_map.93.own_ref), channel_id=1, source_target_pairs={{0,16},{16,32},{32,48},{48,64},{64,80},{80,96},{96,112},{112,128},... | collective-permute-start | bytes 786440 | tf_op jit(solution)/shard_map/ppermute | solution.py:227
  10.7 1.2 fusion.16
  11.9 0.5 collective-permute-start.10
  12.4 1.3 %convolution_convert_fusion.1.q_ref = bf16[256,256]{1,0:T(8,128)(2,1)S(1)} fusion(bf16[3,1024,256]{2,1,0:T(8,128)(2,1)S(1)} %copy-done, bf16[1,256,1024]{2,1,0:T(8,128)(2,1)} %param.6), kind=kOutput, calls=%fused_computation.13 | convolution fusion | flops 134283264 | bytes 1179648 | tf_op jit(solution)/shard_map/dot_general | solution.py:230
  13.9 0.4 compare_reduce_fusion
  14.3 0.1 copy.10
  14.7 1.5 %convolution_convert_fusion.u_ref = bf16[256,256]{1,0:T(8,128)(2,1)S(1)} fusion(bf16[256,1024]{1,0:T(8,128)(2,1)S(1)} %copy-done.1, bf16[1,256,1024]{2,1,0:T(8,128)(2,1)} %param.11), kind=kOutput, calls=%fused_computation.12 | convolution fusion | flops 134283264 | bytes 1179648 | tf_op jit(solution)/shard_map/dot_general | solution.py:231
  16.2 0.7 copy-done.3
  16.9 0.9 copy-done.4
  17.8 3.3 %shard_map.94 = (bf16[2,256,256]{2,1,0:T(8,128)(2,1)S(1)}, bf16[2,256,256]{2,1,0:T(8,128)(2,1)S(1)}, f32[2,256,256]{2,1,0:T(8,128)S(1)}, bf16[2,256,256]{2,1,0:T(8,128)(2,1)S(1)}) custom-call(bf16[256,256]{1,0:T(8,128)(2,1)S(1)} %convolution_convert_fusion.1.q_ref, bf16[256,256]{1,0:T(8,128)(2,1)S(1)} %convolution_convert_fusion.u_ref, ...), custom_call_target="tpu_custom_call" | custom-call | flops 503316480 | bytes 2371584 | tf_op jit(solution)/shard_map/pallas_call | solution.py:26
  21.2 1.9 %collective-permute-start.5 = (bf16[2,256,256]{2,1,0:T(8,128)(2,1)S(1)}, bf16[2,256,256]{2,1,0:T(8,128)(2,1)S(1)}, u32[]{:S(2)}, u32[]{:S(2)}) collective-permute-start(bf16[2,256,256]{2,1,0:T(8,128)(2,1)S(1)} %get-tuple-element.37), channel_id=1, source_target_pairs={{16,0},{32,16},{48,32},{64,48},{80,64},{96,80},{112,96},{128,112},... | collective-permute-start | bytes 786440 | tf_op jit(solution)/shard_map/ppermute | solution.py:266
  23.1 3.6 %collective-permute-start.6 = (bf16[2,256,256]{2,1,0:T(8,128)(2,1)S(1)}, bf16[2,256,256]{2,1,0:T(8,128)(2,1)S(1)}, u32[]{:S(2)}, u32[]{:S(2)}) collective-permute-start(bf16[2,256,256]{2,1,0:T(8,128)(2,1)S(1)} %get-tuple-element.38), channel_id=1, source_target_pairs={{0,16},{16,32},{32,48},{48,64},{64,80},{80,96},{96,112},{112,128},... | collective-permute-start | bytes 786440 | tf_op jit(solution)/shard_map/ppermute | solution.py:267
  26.8 0.5 fusion.19
  27.3 0.1 collective-permute-start.11
  27.4 0.5 fusion.10.a_ref.b_ref
  27.9 0.6 collective-permute-start.12
  28.4 0.4 collective-permute-done.5
  28.9 1.2 collective-permute-done.6
  30.2 0.5 fusion.13.b_ref
  30.8 1.1 shard_map.97
  31.9 0.9 collective-permute-start.13
  32.7 2.6 %collective-permute-start.14 = (bf16[128,512]{1,0:T(8,128)(2,1)}, bf16[128,512]{1,0:T(8,128)(2,1)}, u32[]{:S(2)}, u32[]{:S(2)}) collective-permute-start(bf16[128,512]{1,0:T(8,128)(2,1)} %get-tuple-element.45), channel_id=1, source_target_pairs={{0,2},{1,3},{2,0},{3,1},{4,6},{5,7},{6,4},{7,5},{8,10},{9,11},{10,... | collective-permute-start | bytes 393224 | tf_op jit(solution)/shard_map/ppermute | solution.py:287
  35.4 1.1 collective-permute-start.15
  36.4 1.1 shard_map.98
  37.5 0.4 collective-permute-start.17
  37.9 0.8 collective-permute-start.18
  38.7 1.6 %collective-permute-start.19 = (bf16[128,512]{1,0:T(8,128)(2,1)}, bf16[128,512]{1,0:T(8,128)(2,1)}, u32[]{:S(2)}, u32[]{:S(2)}) collective-permute-start(bf16[128,512]{1,0:T(8,128)(2,1)} %get-tuple-element.50), channel_id=1, source_target_pairs={{0,3},{1,0},{2,1},{3,2},{4,7},{5,4},{6,5},{7,6},{8,11},{9,8},{10,9... | collective-permute-start | bytes 393224 | tf_op jit(solution)/shard_map/ppermute | solution.py:287
  40.3 1.1 collective-permute-done.14.refs_2_
  41.4 2.7 %collective-permute-done.17.refs_5_ = bf16[128,512]{1,0:T(8,128)(2,1)S(1)} collective-permute-done((bf16[128,512]{1,0:T(8,128)(2,1)}, bf16[128,512]{1,0:T(8,128)(2,1)S(1)}, u32[]{:S(2)}, u32[]{:S(2)}) %collective-permute-start.17) | collective-permute-done | bytes 131104 | tf_op jit(solution)/shard_map/ppermute | solution.py:287
  44.1 2.8 %collective-permute-done.18.refs_6_ = bf16[128,512]{1,0:T(8,128)(2,1)S(1)} collective-permute-done((bf16[128,512]{1,0:T(8,128)(2,1)}, bf16[128,512]{1,0:T(8,128)(2,1)S(1)}, u32[]{:S(2)}, u32[]{:S(2)}) %collective-permute-start.18) | collective-permute-done | bytes 131104 | tf_op jit(solution)/shard_map/ppermute | solution.py:287
  46.9 1.1 shard_map.99
  48.0 10.6 %collective-permute-start.23 = (bf16[16,1024]{1,0:T(8,128)(2,1)S(1)}, bf16[16,1024]{1,0:T(8,128)(2,1)S(1)}, u32[]{:S(2)}, u32[]{:S(2)}) collective-permute-start(bf16[16,1024]{1,0:T(8,128)(2,1)S(1)} %get-tuple-element.55), channel_id=1, source_target_pairs={{0,128},{16,144},{32,160},{48,176},{64,192},{80,208},{96,224},{112... | collective-permute-start | bytes 98312 | tf_op jit(solution)/shard_map/ppermute | solution.py:319
  58.7 2.8 %collective-permute-start.22 = (bf16[32,1024]{1,0:T(8,128)(2,1)S(1)}, bf16[32,1024]{1,0:T(8,128)(2,1)S(1)}, u32[]{:S(2)}, u32[]{:S(2)}) collective-permute-start(bf16[32,1024]{1,0:T(8,128)(2,1)S(1)} %get-tuple-element.54), channel_id=1, source_target_pairs={{0,96},{16,176},{32,128},{48,208},{64,160},{80,240},{96,192},{112,... | collective-permute-start | bytes 196616 | tf_op jit(solution)/shard_map/ppermute | solution.py:319
  61.5 0.3 collective-permute-done.20.r1_ref
  61.8 1.0 collective-permute-done.21.r2_ref
  62.8 2.6 %collective-permute-done.22.r3_ref = bf16[32,1024]{1,0:T(8,128)(2,1)S(1)} collective-permute-done((bf16[32,1024]{1,0:T(8,128)(2,1)S(1)}, bf16[32,1024]{1,0:T(8,128)(2,1)S(1)}, u32[]{:S(2)}, u32[]{:S(2)}) %collective-permute-start.22) | collective-permute-done | bytes 65568 | tf_op jit(solution)/shard_map/ppermute | solution.py:319
  65.4 0.6 shard_map.100
  66.0 3.8 %collective-permute-start.24 = (bf16[32,1024]{1,0:T(8,128)(2,1)S(1)}, bf16[32,1024]{1,0:T(8,128)(2,1)S(1)}, u32[]{:S(2)}, u32[]{:S(2)}) collective-permute-start(bf16[32,1024]{1,0:T(8,128)(2,1)S(1)} %shard_map.100), channel_id=1, source_target_pairs={{0,16},{16,0},{32,48},{48,32},{64,80},{80,64},{96,112},{112,96},{1... | collective-permute-start | bytes 196616 | tf_op jit(solution)/shard_map/ppermute | solution.py:224
  69.8 0.8 shard_map.95
  70.7 1.3 %collective-permute-start.2 = (bf16[256,256]{1,0:T(8,128)(2,1)S(1)}, bf16[256,256]{1,0:T(8,128)(2,1)}, u32[]{:S(2)}, u32[]{:S(2)}) collective-permute-start(bf16[256,256]{1,0:T(8,128)(2,1)S(1)} %get-tuple-element.33), channel_id=1, source_target_pairs={{0,4},{4,8},{8,12},{12,0},{1,5},{5,9},{9,13},{13,1},{2,6},{6,10},{... | collective-permute-start | bytes 393224 | tf_op jit(solution)/shard_map/ppermute | solution.py:276
  72.0 2.5 %collective-permute-start.3 = (bf16[256,256]{1,0:T(8,128)(2,1)S(1)}, bf16[256,256]{1,0:T(8,128)(2,1)S(1)}, u32[]{:S(2)}, u32[]{:S(2)}) collective-permute-start(bf16[256,256]{1,0:T(8,128)(2,1)S(1)} %get-tuple-element.34), channel_id=1, source_target_pairs={{0,8},{4,12},{8,0},{12,4},{1,9},{5,13},{9,1},{13,5},{2,10},{6,14},... | collective-permute-start | bytes 393224 | tf_op jit(solution)/shard_map/ppermute | solution.py:276
  74.4 1.2 collective-permute-start.4
  75.6 3.4 %collective-permute-start.27 = (bf16[32,1024]{1,0:T(8,128)(2,1)S(1)}, bf16[32,1024]{1,0:T(8,128)(2,1)S(1)}, u32[]{:S(2)}, u32[]{:S(2)}) collective-permute-start(bf16[32,1024]{1,0:T(8,128)(2,1)S(1)} %add_convert_fusion.1), channel_id=1, source_target_pairs={{0,96},{16,176},{32,128},{48,208},{64,160},{80,240},{96,192},{112,... | collective-permute-start | bytes 196616 | tf_op jit(solution)/shard_map/ppermute | solution.py:325
  79.0 3.4 %collective-permute-done.25 = bf16[32,1024]{1,0:T(8,128)(2,1)S(1)} collective-permute-done((bf16[32,1024]{1,0:T(8,128)(2,1)S(1)}, bf16[32,1024]{1,0:T(8,128)(2,1)S(1)}, u32[]{:S(2)}, u32[]{:S(2)}) %collective-permute-start.25) | collective-permute-done | bytes 65568 | tf_op jit(solution)/shard_map/ppermute | solution.py:325
  82.4 4.8 %collective-permute-done.26 = bf16[32,1024]{1,0:T(8,128)(2,1)S(1)} collective-permute-done((bf16[32,1024]{1,0:T(8,128)(2,1)S(1)}, bf16[32,1024]{1,0:T(8,128)(2,1)S(1)}, u32[]{:S(2)}, u32[]{:S(2)}) %collective-permute-start.26) | collective-permute-done | bytes 65568 | tf_op jit(solution)/shard_map/ppermute | solution.py:325
  87.2 1.0 collective-permute-start.28
  88.3 6.0 %collective-permute-done.28 = bf16[16,1024]{1,0:T(8,128)(2,1)S(1)} collective-permute-done((bf16[16,1024]{1,0:T(8,128)(2,1)S(1)}, bf16[16,1024]{1,0:T(8,128)(2,1)S(1)}, u32[]{:S(2)}, u32[]{:S(2)}) %collective-permute-start.28) | collective-permute-done | bytes 32800 | tf_op jit(solution)/shard_map/ppermute | solution.py:326
  94.3 1.7 %collective-permute-start.31 = (bf16[128,1024]{1,0:T(8,128)(2,1)S(1)}, bf16[128,1024]{1,0:T(8,128)(2,1)S(1)}, u32[]{:S(2)}, u32[]{:S(2)}) collective-permute-start(bf16[128,1024]{1,0:T(8,128)(2,1)S(1)} %constant_dynamic-update-slice_fusion.refs_0_), channel_id=1, source_target_pairs={{0,3},{1,0},{2,1},{3,2},{4,7},{5,4},{6,5},{7,6},{8,11},{9,8},{10,9... | collective-permute-start | bytes 786440 | tf_op jit(solution)/shard_map/ppermute | solution.py:328
  96.0 1.3 %collective-permute-start.30 = (bf16[128,1024]{1,0:T(8,128)(2,1)S(1)}, bf16[128,1024]{1,0:T(8,128)(2,1)S(1)}, u32[]{:S(2)}, u32[]{:S(2)}) collective-permute-start(bf16[128,1024]{1,0:T(8,128)(2,1)S(1)} %constant_dynamic-update-slice_fusion.refs_0_), channel_id=1, source_target_pairs={{0,2},{1,3},{2,0},{3,1},{4,6},{5,7},{6,4},{7,5},{8,10},{9,11},{10,... | collective-permute-start | bytes 786440 | tf_op jit(solution)/shard_map/ppermute | solution.py:328
  97.3 0.3 collective-permute-start.29
  97.6 1.8 %shard_map.96 = (f32[256,256]{1,0:T(8,128)S(1)}, bf16[256,256]{1,0:T(8,128)(2,1)}, bf16[256,256]{1,0:T(8,128)(2,1)}, bf16[256,256]{1,0:T(8,128)(2,1)S(1)}) custom-call(s32[4]{0:T(128)S(1)} %pad_add_fusion.idx_ref, bf16[2,256,256]{2,1,0:T(8,128)(2,1)S(1)} %get-tuple-element.31.acts_ref.left_ref, bf16[2,256,256]{2,1,0:T(8,128)(2,1)S(1)} %add_convert_fusion.dkv_ref.left_ref, ...), custom_call_target="tpu_custom_call" | custom-call | flops 402653184 | bytes 2752528 | tf_op jit(solution)/shard_map/pallas_call | solution.py:26
  99.4 0.3 collective-permute-start.7
  99.8 0.3 copy-done.8
  100.1 0.7 copy-done.9
  100.8 0.5 collective-permute-start.8
  101.3 3.4 %collective-permute-done.7 = bf16[256,256]{1,0:T(8,128)(2,1)S(1)} collective-permute-done((bf16[256,256]{1,0:T(8,128)(2,1)}, bf16[256,256]{1,0:T(8,128)(2,1)S(1)}, u32[]{:S(2)}, u32[]{:S(2)}) %collective-permute-start.7) | collective-permute-done | bytes 131104 | tf_op jit(solution)/shard_map/ppermute | solution.py:276
  104.7 1.9 %collective-permute-done.8 = bf16[256,256]{1,0:T(8,128)(2,1)S(1)} collective-permute-done((bf16[256,256]{1,0:T(8,128)(2,1)}, bf16[256,256]{1,0:T(8,128)(2,1)S(1)}, u32[]{:S(2)}, u32[]{:S(2)}) %collective-permute-start.8) | collective-permute-done | bytes 131104 | tf_op jit(solution)/shard_map/ppermute | solution.py:276
  106.6 6.6 %collective-permute-start.32 = (bf16[128,1024]{1,0:T(8,128)(2,1)S(1)}, bf16[128,1024]{1,0:T(8,128)(2,1)S(1)}, u32[]{:S(2)}, u32[]{:S(2)}) collective-permute-start(bf16[128,1024]{1,0:T(8,128)(2,1)S(1)} %constant_dynamic-update-slice_fusion.refs_0_), channel_id=1, source_target_pairs={{0,16},{16,0},{32,48},{48,32},{64,80},{80,64},{96,112},{112,96},{1... | collective-permute-start | bytes 786440 | tf_op jit(solution)/shard_map/ppermute | solution.py:224
  113.2 0.5 collective-permute-start.34
  113.8 1.8 %fusion.33 = bf16[1,256,256]{2,1,0:T(8,128)(2,1)} fusion(bf16[256,256]{1,0:T(8,128)(2,1)} %copy-done.9, bf16[256,256]{1,0:T(8,128)(2,1)} %copy-done.8, f32[256,256]{1,0:T(8,128)S(1)} %get-tuple-element.32, bf16[256,256]{1,0:T(8,128)(2,1)} %collective-permute-done.2, bf16[1,256,1024]{2,1,0:T(8,128)(2,1)} %param.6, s32[]{:T(128)S(6)} %select_n.128), kind=kLoop, calls=%fused_computation.28 | loop fusion | flops 589824 | bytes 917508 | tf_op jit(solution)/shard_map/broadcast_in_dim | solution.py:338
  115.6 1.6 %fusion.34 = bf16[1,256,256]{2,1,0:T(8,128)(2,1)} fusion(bf16[256,256]{1,0:T(8,128)(2,1)S(1)} %collective-permute-done.9, bf16[256,256]{1,0:T(8,128)(2,1)S(1)} %collective-permute-done.8, f32[256,256]{1,0:T(8,128)S(1)} %get-tuple-element.39, bf16[256,256]{1,0:T(8,128)(2,1)S(1)} %collective-permute-done.7, bf16[1,256,1024]{2,1,0:T(8,128)(2,1)} %param.11, ...), kind=kLoop, calls=%fused_computation.29 | loop fusion | flops 589824 | bytes 917508 | tf_op jit(solution)/shard_map/broadcast_in_dim | solution.py:338
  117.3 3.3 %shard_map.101 = (f32[3,1024,256]{2,1,0:T(8,128)}, f32[256,1024]{1,0:T(8,128)}) custom-call(s32[4]{0:T(128)S(1)} %pad_add_fusion.idx_ref, bf16[128,1024]{1,0:T(8,128)(2,1)S(1)} %constant_dynamic-update-slice_fusion.refs_0_, bf16[128,1024]{1,0:T(8,128)(2,1)} %collective-permute-done.29.refs_1_, bf16[128,1024]{1,0:T(8,128)(2,1)S(1)} %collective-permute-done.30.refs_2_, ...), custom_call_target="tpu_custom_call" | custom-call | flops 1048576 | bytes 6291472 | tf_op jit(solution)/shard_map/pallas_call | solution.py:26
  (71 shorter events, 1.0 us)
Async XLA Ops:
  0.6 10.1 %copy-start.6 = (bf16[1,256,1024]{2,1,0:T(8,128)(2,1)S(1)}, bf16[1,256,1024]{2,1,0:T(8,128)(2,1)}, u32[]{:S(2)}) copy-start(bf16[1,256,1024]{2,1,0:T(8,128)(2,1)} %param.6) | copy-start | bytes 1572868
  0.6 11.8 %copy-start = (bf16[3,1024,256]{2,1,0:T(8,128)(2,1)S(1)}, bf16[3,1024,256]{2,1,0:T(8,128)(2,1)}, u32[]{:S(2)}) copy-start(bf16[3,1024,256]{2,1,0:T(8,128)(2,1)} %w_ref.5) | copy-start | bytes 4718596
  3.3 10.5 %copy-start.11 = (s32[1,64]{1,0:T(1,128)S(1)}, s32[1,64]{1,0:T(1,128)}, u32[]{:S(2)}) copy-start(s32[1,64]{1,0:T(1,128)} %param.8) | copy-start | bytes 772
  3.3 10.6 %copy-start.10 = (s32[1,4,27]{2,1,0:T(4,128)S(1)}, s32[1,4,27]{2,1,0:T(4,128)}, u32[]{:S(2)}) copy-start(s32[1,4,27]{2,1,0:T(4,128)} %param.7) | copy-start | bytes 1300
  3.3 11.3 %copy-start.1 = (bf16[256,1024]{1,0:T(8,128)(2,1)S(1)}, bf16[256,1024]{1,0:T(8,128)(2,1)}, u32[]{:S(2)}) copy-start(bf16[256,1024]{1,0:T(8,128)(2,1)} %w_ref.4) | copy-start | bytes 1572868
  3.3 12.8 %collective-permute-start.1 = (bf16[2,256,256]{2,1,0:T(8,128)(2,1)}, bf16[2,256,256]{2,1,0:T(8,128)(2,1)S(1)}, u32[]{:S(2)}, u32[]{:S(2)}) collective-permute-start(bf16[2,256,256]{2,1,0:T(8,128)(2,1)} %shard_map.93.own_ref), channel_id=1, source_target_pairs={{16,0},{32,16},{48,32},{64,48},{80,64},{96,80},{112,96},{128,112},... | collective-permute-start | bytes 786440 | tf_op jit(solution)/shard_map/ppermute | solution.py:228
  8.6 7.5 %collective-permute-start = (bf16[2,256,256]{2,1,0:T(8,128)(2,1)}, bf16[2,256,256]{2,1,0:T(8,128)(2,1)S(1)}, u32[]{:S(2)}, u32[]{:S(2)}) collective-permute-start(bf16[2,256,256]{2,1,0:T(8,128)(2,1)} %shard_map.93.own_ref), channel_id=1, source_target_pairs={{0,16},{16,32},{32,48},{48,64},{64,80},{80,96},{96,112},{112,128},... | collective-permute-start | bytes 786440 | tf_op jit(solution)/shard_map/ppermute | solution.py:227
  10.7 6.2 %copy-start.2 = (bf16[2,256,256]{2,1,0:T(8,128)(2,1)S(1)}, bf16[2,256,256]{2,1,0:T(8,128)(2,1)}, u32[]{:S(2)}) copy-start(bf16[2,256,256]{2,1,0:T(8,128)(2,1)} %shard_map.93.own_ref) | copy-start | bytes 786436
  11.9 18.8 %collective-permute-start.10 = (bf16[512,256]{1,0:T(8,128)(2,1)}, bf16[512,256]{1,0:T(8,128)(2,1)S(1)}, u32[]{:S(2)}, u32[]{:S(2)}) collective-permute-start(bf16[512,256]{1,0:T(8,128)(2,1)} %fusion.16), channel_id=1, source_target_pairs={{0,16},{16,0},{32,48},{48,32},{64,80},{80,64},{96,112},{112,96},{1... | collective-permute-start | bytes 786440 | tf_op jit(solution)/shard_map/ppermute | solution.py:224
  14.6 12.1 %copy-start.5 = (bf16[1,256,1024]{2,1,0:T(8,128)(2,1)S(1)}, bf16[1,256,1024]{2,1,0:T(8,128)(2,1)}, u32[]{:S(2)}) copy-start(bf16[1,256,1024]{2,1,0:T(8,128)(2,1)} %param.11) | copy-start | bytes 1572868
  14.6 12.7 %copy-start.7 = (bf16[1,256,1024]{2,1,0:T(8,128)(2,1)S(1)}, bf16[1,256,1024]{2,1,0:T(8,128)(2,1)}, u32[]{:S(2)}) copy-start(bf16[1,256,1024]{2,1,0:T(8,128)(2,1)} %param.6) | copy-start | bytes 1572868
  16.2 0.7 copy-start.3
  16.9 1.0 copy-start.4
  21.2 7.7 %collective-permute-start.5 = (bf16[2,256,256]{2,1,0:T(8,128)(2,1)S(1)}, bf16[2,256,256]{2,1,0:T(8,128)(2,1)S(1)}, u32[]{:S(2)}, u32[]{:S(2)}) collective-permute-start(bf16[2,256,256]{2,1,0:T(8,128)(2,1)S(1)} %get-tuple-element.37), channel_id=1, source_target_pairs={{16,0},{32,16},{48,32},{64,48},{80,64},{96,80},{112,96},{128,112},... | collective-permute-start | bytes 786440 | tf_op jit(solution)/shard_map/ppermute | solution.py:266
  23.1 6.9 %collective-permute-start.6 = (bf16[2,256,256]{2,1,0:T(8,128)(2,1)S(1)}, bf16[2,256,256]{2,1,0:T(8,128)(2,1)S(1)}, u32[]{:S(2)}, u32[]{:S(2)}) collective-permute-start(bf16[2,256,256]{2,1,0:T(8,128)(2,1)S(1)} %get-tuple-element.38), channel_id=1, source_target_pairs={{0,16},{16,32},{32,48},{48,64},{64,80},{80,96},{96,112},{112,128},... | collective-permute-start | bytes 786440 | tf_op jit(solution)/shard_map/ppermute | solution.py:267
  27.3 3.5 %collective-permute-start.11 = (bf16[512,256]{1,0:T(8,128)(2,1)S(1)}, bf16[512,256]{1,0:T(8,128)(2,1)S(1)}, u32[]{:S(2)}, u32[]{:S(2)}) collective-permute-start(bf16[512,256]{1,0:T(8,128)(2,1)S(1)} %fusion.19), channel_id=1, source_target_pairs={{0,16},{16,0},{32,48},{48,32},{64,80},{80,64},{96,112},{112,96},{1... | collective-permute-start | bytes 786440 | tf_op jit(solution)/shard_map/ppermute | solution.py:224
  27.9 2.9 %collective-permute-start.12 = (bf16[2,256,256]{2,1,0:T(8,128)(2,1)S(1)}, bf16[2,256,256]{2,1,0:T(8,128)(2,1)S(1)}, u32[]{:S(2)}, u32[]{:S(2)}) collective-permute-start(bf16[2,256,256]{2,1,0:T(8,128)(2,1)S(1)} %get-tuple-element.31.acts_ref.left_ref), channel_id=1, source_target_pairs={{0,16},{16,0},{32,48},{48,32},{64,80},{80,64},{96,112},{112,96},{1... | collective-permute-start | bytes 786440 | tf_op jit(solution)/shard_map/ppermute | solution.py:224
  30.1 6.3 %collective-permute-start.16 = (bf16[2,256,256]{2,1,0:T(8,128)(2,1)S(1)}, bf16[2,256,256]{2,1,0:T(8,128)(2,1)S(1)}, u32[]{:S(2)}, u32[]{:S(2)}) collective-permute-start(bf16[2,256,256]{2,1,0:T(8,128)(2,1)S(1)} %add_convert_fusion.dkv_ref.left_ref), channel_id=1, source_target_pairs={{0,16},{16,0},{32,48},{48,32},{64,80},{80,64},{96,112},{112,96},{1... | collective-permute-start | bytes 786440 | tf_op jit(solution)/shard_map/ppermute | solution.py:224
  31.9 6.8 %collective-permute-start.13 = (bf16[128,512]{1,0:T(8,128)(2,1)S(1)}, bf16[128,512]{1,0:T(8,128)(2,1)S(1)}, u32[]{:S(2)}, u32[]{:S(2)}) collective-permute-start(bf16[128,512]{1,0:T(8,128)(2,1)S(1)} %get-tuple-element.44), channel_id=1, source_target_pairs={{0,1},{1,2},{2,3},{3,0},{4,5},{5,6},{6,7},{7,4},{8,9},{9,10},{10,1... | collective-permute-start | bytes 393224 | tf_op jit(solution)/shard_map/ppermute | solution.py:287
  32.7 8.6 %collective-permute-start.14 = (bf16[128,512]{1,0:T(8,128)(2,1)}, bf16[128,512]{1,0:T(8,128)(2,1)}, u32[]{:S(2)}, u32[]{:S(2)}) collective-permute-start(bf16[128,512]{1,0:T(8,128)(2,1)} %get-tuple-element.45), channel_id=1, source_target_pairs={{0,2},{1,3},{2,0},{3,1},{4,6},{5,7},{6,4},{7,5},{8,10},{9,11},{10,... | collective-permute-start | bytes 393224 | tf_op jit(solution)/shard_map/ppermute | solution.py:287
  35.4 6.0 %collective-permute-start.15 = (bf16[128,512]{1,0:T(8,128)(2,1)}, bf16[128,512]{1,0:T(8,128)(2,1)}, u32[]{:S(2)}, u32[]{:S(2)}) collective-permute-start(bf16[128,512]{1,0:T(8,128)(2,1)} %get-tuple-element.46), channel_id=1, source_target_pairs={{0,3},{1,0},{2,1},{3,2},{4,7},{5,4},{6,5},{7,6},{8,11},{9,8},{10,9... | collective-permute-start | bytes 393224 | tf_op jit(solution)/shard_map/ppermute | solution.py:287
  37.5 6.6 %collective-permute-start.17 = (bf16[128,512]{1,0:T(8,128)(2,1)}, bf16[128,512]{1,0:T(8,128)(2,1)S(1)}, u32[]{:S(2)}, u32[]{:S(2)}) collective-permute-start(bf16[128,512]{1,0:T(8,128)(2,1)} %get-tuple-element.48), channel_id=1, source_target_pairs={{0,1},{1,2},{2,3},{3,0},{4,5},{5,6},{6,7},{7,4},{8,9},{9,10},{10,1... | collective-permute-start | bytes 393224 | tf_op jit(solution)/shard_map/ppermute | solution.py:287
  37.9 9.0 %collective-permute-start.18 = (bf16[128,512]{1,0:T(8,128)(2,1)}, bf16[128,512]{1,0:T(8,128)(2,1)S(1)}, u32[]{:S(2)}, u32[]{:S(2)}) collective-permute-start(bf16[128,512]{1,0:T(8,128)(2,1)} %get-tuple-element.49), channel_id=1, source_target_pairs={{0,2},{1,3},{2,0},{3,1},{4,6},{5,7},{6,4},{7,5},{8,10},{9,11},{10,... | collective-permute-start | bytes 393224 | tf_op jit(solution)/shard_map/ppermute | solution.py:287
  38.7 8.2 %collective-permute-start.19 = (bf16[128,512]{1,0:T(8,128)(2,1)}, bf16[128,512]{1,0:T(8,128)(2,1)}, u32[]{:S(2)}, u32[]{:S(2)}) collective-permute-start(bf16[128,512]{1,0:T(8,128)(2,1)} %get-tuple-element.50), channel_id=1, source_target_pairs={{0,3},{1,0},{2,1},{3,2},{4,7},{5,4},{6,5},{7,6},{8,11},{9,8},{10,9... | collective-permute-start | bytes 393224 | tf_op jit(solution)/shard_map/ppermute | solution.py:287
  48.0 13.5 %collective-permute-start.23 = (bf16[16,1024]{1,0:T(8,128)(2,1)S(1)}, bf16[16,1024]{1,0:T(8,128)(2,1)S(1)}, u32[]{:S(2)}, u32[]{:S(2)}) collective-permute-start(bf16[16,1024]{1,0:T(8,128)(2,1)S(1)} %get-tuple-element.55), channel_id=1, source_target_pairs={{0,128},{16,144},{32,160},{48,176},{64,192},{80,208},{96,224},{112... | collective-permute-start | bytes 98312 | tf_op jit(solution)/shard_map/ppermute | solution.py:319
  58.7 3.1 %collective-permute-start.20 = (bf16[32,1024]{1,0:T(8,128)(2,1)S(1)}, bf16[32,1024]{1,0:T(8,128)(2,1)S(1)}, u32[]{:S(2)}, u32[]{:S(2)}) collective-permute-start(bf16[32,1024]{1,0:T(8,128)(2,1)S(1)} %get-tuple-element.52), channel_id=1, source_target_pairs={{0,32},{16,240},{32,64},{48,16},{64,96},{80,48},{96,128},{112,80},... | collective-permute-start | bytes 196616 | tf_op jit(solution)/shard_map/ppermute | solution.py:319
  58.7 4.1 %collective-permute-start.21 = (bf16[32,1024]{1,0:T(8,128)(2,1)S(1)}, bf16[32,1024]{1,0:T(8,128)(2,1)S(1)}, u32[]{:S(2)}, u32[]{:S(2)}) collective-permute-start(bf16[32,1024]{1,0:T(8,128)(2,1)S(1)} %get-tuple-element.53), channel_id=1, source_target_pairs={{0,64},{16,208},{32,96},{48,240},{64,128},{80,16},{96,160},{112,48... | collective-permute-start | bytes 196616 | tf_op jit(solution)/shard_map/ppermute | solution.py:319
  58.7 6.7 %collective-permute-start.22 = (bf16[32,1024]{1,0:T(8,128)(2,1)S(1)}, bf16[32,1024]{1,0:T(8,128)(2,1)S(1)}, u32[]{:S(2)}, u32[]{:S(2)}) collective-permute-start(bf16[32,1024]{1,0:T(8,128)(2,1)S(1)} %get-tuple-element.54), channel_id=1, source_target_pairs={{0,96},{16,176},{32,128},{48,208},{64,160},{80,240},{96,192},{112,... | collective-permute-start | bytes 196616 | tf_op jit(solution)/shard_map/ppermute | solution.py:319
  66.0 9.6 %collective-permute-start.24 = (bf16[32,1024]{1,0:T(8,128)(2,1)S(1)}, bf16[32,1024]{1,0:T(8,128)(2,1)S(1)}, u32[]{:S(2)}, u32[]{:S(2)}) collective-permute-start(bf16[32,1024]{1,0:T(8,128)(2,1)S(1)} %shard_map.100), channel_id=1, source_target_pairs={{0,16},{16,0},{32,48},{48,32},{64,80},{80,64},{96,112},{112,96},{1... | collective-permute-start | bytes 196616 | tf_op jit(solution)/shard_map/ppermute | solution.py:224
  70.7 26.7 %collective-permute-start.2 = (bf16[256,256]{1,0:T(8,128)(2,1)S(1)}, bf16[256,256]{1,0:T(8,128)(2,1)}, u32[]{:S(2)}, u32[]{:S(2)}) collective-permute-start(bf16[256,256]{1,0:T(8,128)(2,1)S(1)} %get-tuple-element.33), channel_id=1, source_target_pairs={{0,4},{4,8},{8,12},{12,0},{1,5},{5,9},{9,13},{13,1},{2,6},{6,10},{... | collective-permute-start | bytes 393224 | tf_op jit(solution)/shard_map/ppermute | solution.py:276
  72.0 27.5 %collective-permute-start.3 = (bf16[256,256]{1,0:T(8,128)(2,1)S(1)}, bf16[256,256]{1,0:T(8,128)(2,1)S(1)}, u32[]{:S(2)}, u32[]{:S(2)}) collective-permute-start(bf16[256,256]{1,0:T(8,128)(2,1)S(1)} %get-tuple-element.34), channel_id=1, source_target_pairs={{0,8},{4,12},{8,0},{12,4},{1,9},{5,13},{9,1},{13,5},{2,10},{6,14},... | collective-permute-start | bytes 393224 | tf_op jit(solution)/shard_map/ppermute | solution.py:276
  74.4 25.4 %collective-permute-start.4 = (bf16[256,256]{1,0:T(8,128)(2,1)S(1)}, bf16[256,256]{1,0:T(8,128)(2,1)S(1)}, u32[]{:S(2)}, u32[]{:S(2)}) collective-permute-start(bf16[256,256]{1,0:T(8,128)(2,1)S(1)} %get-tuple-element.35), channel_id=1, source_target_pairs={{0,12},{4,0},{8,4},{12,8},{1,13},{5,1},{9,5},{13,9},{2,14},{6,2},{... | collective-permute-start | bytes 393224 | tf_op jit(solution)/shard_map/ppermute | solution.py:276
  75.6 12.6 %collective-permute-start.27 = (bf16[32,1024]{1,0:T(8,128)(2,1)S(1)}, bf16[32,1024]{1,0:T(8,128)(2,1)S(1)}, u32[]{:S(2)}, u32[]{:S(2)}) collective-permute-start(bf16[32,1024]{1,0:T(8,128)(2,1)S(1)} %add_convert_fusion.1), channel_id=1, source_target_pairs={{0,96},{16,176},{32,128},{48,208},{64,160},{80,240},{96,192},{112,... | collective-permute-start | bytes 196616 | tf_op jit(solution)/shard_map/ppermute | solution.py:325
  79.0 3.4 %collective-permute-start.25 = (bf16[32,1024]{1,0:T(8,128)(2,1)S(1)}, bf16[32,1024]{1,0:T(8,128)(2,1)S(1)}, u32[]{:S(2)}, u32[]{:S(2)}) collective-permute-start(bf16[32,1024]{1,0:T(8,128)(2,1)S(1)} %add_convert_fusion.1), channel_id=1, source_target_pairs={{0,32},{16,240},{32,64},{48,16},{64,96},{80,48},{96,128},{112,80},... | collective-permute-start | bytes 196616 | tf_op jit(solution)/shard_map/ppermute | solution.py:325
  82.4 4.8 %collective-permute-start.26 = (bf16[32,1024]{1,0:T(8,128)(2,1)S(1)}, bf16[32,1024]{1,0:T(8,128)(2,1)S(1)}, u32[]{:S(2)}, u32[]{:S(2)}) collective-permute-start(bf16[32,1024]{1,0:T(8,128)(2,1)S(1)} %add_convert_fusion.1), channel_id=1, source_target_pairs={{0,64},{16,208},{32,96},{48,240},{64,128},{80,16},{96,160},{112,48... | collective-permute-start | bytes 196616 | tf_op jit(solution)/shard_map/ppermute | solution.py:325
  87.2 7.0 %collective-permute-start.28 = (bf16[16,1024]{1,0:T(8,128)(2,1)S(1)}, bf16[16,1024]{1,0:T(8,128)(2,1)S(1)}, u32[]{:S(2)}, u32[]{:S(2)}) collective-permute-start(bf16[16,1024]{1,0:T(8,128)(2,1)S(1)} %get-tuple-element.59), channel_id=1, source_target_pairs={{0,128},{16,144},{32,160},{48,176},{64,192},{80,208},{96,224},{112... | collective-permute-start | bytes 98312 | tf_op jit(solution)/shard_map/ppermute | solution.py:326
  94.3 18.9 %collective-permute-start.31 = (bf16[128,1024]{1,0:T(8,128)(2,1)S(1)}, bf16[128,1024]{1,0:T(8,128)(2,1)S(1)}, u32[]{:S(2)}, u32[]{:S(2)}) collective-permute-start(bf16[128,1024]{1,0:T(8,128)(2,1)S(1)} %constant_dynamic-update-slice_fusion.refs_0_), channel_id=1, source_target_pairs={{0,3},{1,0},{2,1},{3,2},{4,7},{5,4},{6,5},{7,6},{8,11},{9,8},{10,9... | collective-permute-start | bytes 786440 | tf_op jit(solution)/shard_map/ppermute | solution.py:328
  96.0 17.2 %collective-permute-start.30 = (bf16[128,1024]{1,0:T(8,128)(2,1)S(1)}, bf16[128,1024]{1,0:T(8,128)(2,1)S(1)}, u32[]{:S(2)}, u32[]{:S(2)}) collective-permute-start(bf16[128,1024]{1,0:T(8,128)(2,1)S(1)} %constant_dynamic-update-slice_fusion.refs_0_), channel_id=1, source_target_pairs={{0,2},{1,3},{2,0},{3,1},{4,6},{5,7},{6,4},{7,5},{8,10},{9,11},{10,... | collective-permute-start | bytes 786440 | tf_op jit(solution)/shard_map/ppermute | solution.py:328
  97.3 16.4 %collective-permute-start.29 = (bf16[128,1024]{1,0:T(8,128)(2,1)S(1)}, bf16[128,1024]{1,0:T(8,128)(2,1)}, u32[]{:S(2)}, u32[]{:S(2)}) collective-permute-start(bf16[128,1024]{1,0:T(8,128)(2,1)S(1)} %constant_dynamic-update-slice_fusion.refs_0_), channel_id=1, source_target_pairs={{0,1},{1,2},{2,3},{3,0},{4,5},{5,6},{6,7},{7,4},{8,9},{9,10},{10,1... | collective-permute-start | bytes 786440 | tf_op jit(solution)/shard_map/ppermute | solution.py:328
  99.4 0.7 copy-start.8
  99.4 5.2 %collective-permute-start.7 = (bf16[256,256]{1,0:T(8,128)(2,1)}, bf16[256,256]{1,0:T(8,128)(2,1)S(1)}, u32[]{:S(2)}, u32[]{:S(2)}) collective-permute-start(bf16[256,256]{1,0:T(8,128)(2,1)} %get-tuple-element.40), channel_id=1, source_target_pairs={{0,4},{4,8},{8,12},{12,0},{1,5},{5,9},{9,13},{13,1},{2,6},{6,10},{... | collective-permute-start | bytes 393224 | tf_op jit(solution)/shard_map/ppermute | solution.py:276
  100.1 0.7 copy-start.9
  100.8 5.8 %collective-permute-start.8 = (bf16[256,256]{1,0:T(8,128)(2,1)}, bf16[256,256]{1,0:T(8,128)(2,1)S(1)}, u32[]{:S(2)}, u32[]{:S(2)}) collective-permute-start(bf16[256,256]{1,0:T(8,128)(2,1)} %get-tuple-element.41), channel_id=1, source_target_pairs={{0,8},{4,12},{8,0},{12,4},{1,9},{5,13},{9,1},{13,5},{2,10},{6,14},... | collective-permute-start | bytes 393224 | tf_op jit(solution)/shard_map/ppermute | solution.py:276
  104.7 10.9 %collective-permute-start.9 = (bf16[256,256]{1,0:T(8,128)(2,1)S(1)}, bf16[256,256]{1,0:T(8,128)(2,1)S(1)}, u32[]{:S(2)}, u32[]{:S(2)}) collective-permute-start(bf16[256,256]{1,0:T(8,128)(2,1)S(1)} %get-tuple-element.42), channel_id=1, source_target_pairs={{0,12},{4,0},{8,4},{12,8},{1,13},{5,1},{9,5},{13,9},{2,14},{6,2},{... | collective-permute-start | bytes 393224 | tf_op jit(solution)/shard_map/ppermute | solution.py:276
  106.6 10.7 %collective-permute-start.32 = (bf16[128,1024]{1,0:T(8,128)(2,1)S(1)}, bf16[128,1024]{1,0:T(8,128)(2,1)S(1)}, u32[]{:S(2)}, u32[]{:S(2)}) collective-permute-start(bf16[128,1024]{1,0:T(8,128)(2,1)S(1)} %constant_dynamic-update-slice_fusion.refs_0_), channel_id=1, source_target_pairs={{0,16},{16,0},{32,48},{48,32},{64,80},{80,64},{96,112},{112,96},{1... | collective-permute-start | bytes 786440 | tf_op jit(solution)/shard_map/ppermute | solution.py:224
  113.2 4.1 %collective-permute-start.35 = (bf16[128,1024]{1,0:T(8,128)(2,1)S(1)}, bf16[128,1024]{1,0:T(8,128)(2,1)S(1)}, u32[]{:S(2)}, u32[]{:S(2)}) collective-permute-start(bf16[128,1024]{1,0:T(8,128)(2,1)S(1)} %collective-permute-done.31.refs_3_), channel_id=1, source_target_pairs={{0,16},{16,0},{32,48},{48,32},{64,80},{80,64},{96,112},{112,96},{1... | collective-permute-start | bytes 786440 | tf_op jit(solution)/shard_map/ppermute | solution.py:224
  113.2 4.1 %collective-permute-start.34 = (bf16[128,1024]{1,0:T(8,128)(2,1)S(1)}, bf16[128,1024]{1,0:T(8,128)(2,1)S(1)}, u32[]{:S(2)}, u32[]{:S(2)}) collective-permute-start(bf16[128,1024]{1,0:T(8,128)(2,1)S(1)} %collective-permute-done.30.refs_2_), channel_id=1, source_target_pairs={{0,16},{16,0},{32,48},{48,32},{64,80},{80,64},{96,112},{112,96},{1... | collective-permute-start | bytes 786440 | tf_op jit(solution)/shard_map/ppermute | solution.py:224
  113.7 3.6 %collective-permute-start.33 = (bf16[128,1024]{1,0:T(8,128)(2,1)}, bf16[128,1024]{1,0:T(8,128)(2,1)S(1)}, u32[]{:S(2)}, u32[]{:S(2)}) collective-permute-start(bf16[128,1024]{1,0:T(8,128)(2,1)} %collective-permute-done.29.refs_1_), channel_id=1, source_target_pairs={{0,16},{16,0},{32,48},{48,32},{64,80},{80,64},{96,112},{112,96},{1... | collective-permute-start | bytes 786440 | tf_op jit(solution)/shard_map/ppermute | solution.py:224

commit v2 on v1

v2 whole, which is shorter than its diff:
```python
import jax
import jax.numpy as jnp
from jax import lax
from jax.experimental import pallas as pl
from jax.experimental.pallas import tpu as pltpu
from jax.sharding import PartitionSpec as P

HD = 64
BLOCK = 64
ROWS = 256
WIDTH = 256
D = 1024
PLACE_ORDER = (0, 3, 1, 2)
LOG2E = 1.4426950408889634
BF = jnp.bfloat16
F32 = jnp.float32
VMEM = pl.BlockSpec(memory_space=pltpu.VMEM)
ANY = pl.BlockSpec(memory_space=pl.ANY)
HBM = pl.BlockSpec(memory_space=pltpu.HBM)


def call(kernel, outs, operands, flops, in_specs=None, scratch=(), vmem=24, after=(), out_specs=None):
    moved = sum(a.size * a.dtype.itemsize for a in operands)
    moved += sum(o.size * o.dtype.itemsize for o in outs)
    count = len(operands)

    def body(*refs):
        kernel(*refs[:count], *refs[count + len(after) :])

    return pl.pallas_call(
        body,
        out_shape=outs,
        in_specs=(in_specs or [VMEM] * count) + [ANY] * len(after),
        out_specs=out_specs or [VMEM] * len(outs),
        scratch_shapes=list(scratch),
        compiler_params=pltpu.CompilerParams(vmem_limit_bytes=vmem * 2**20),
        cost_estimate=pl.CostEstimate(flops=flops, bytes_accessed=moved, transcendentals=0),
    )(*operands, *after)


def shape(dims, kind):
    return jax.ShapeDtypeStruct(dims, kind)


def nn(a, b):
    return lax.dot_general(a, b, (((1,), (0,)), ((), ())), preferred_element_type=F32)


def nt(a, b):
    return lax.dot_general(a, b, (((1,), (1,)), ((), ())), preferred_element_type=F32)


def tn(a, b):
    return lax.dot_general(a, b, (((0,), (0,)), ((), ())), preferred_element_type=F32)


def place_of():
    spatial = lax.axis_index("spatial")
    return spatial >> 1, spatial & 1, lax.axis_index("dp"), lax.axis_index("head")


def picker(side):
    z, _, y, _ = place_of()
    c = lax.broadcasted_iota(jnp.int32, (512, 1), 0)
    k, m = c >> 7, (c >> 4) & 7
    chunk = z ^ (2 * (m & 3) + (m >> 2))
    row = (y ^ k) * 256 + side * 128 + chunk * 16 + (c & 15)
    feature = lax.broadcasted_iota(jnp.int32, (512, D), 1)
    return (feature == row).astype(F32).astype(BF)


def pick_rows(side, x_ref, cot_ref, out_ref):
    pick = picker(side)
    out_ref[0] = nt(pick, x_ref[...]).astype(BF)
    out_ref[1] = nt(pick, cot_ref[...]).astype(BF)


def first_kernel(*refs):
    inputs, (kv_ref, q_ref, u_ref, xc_ref), held, sems = refs[:4], refs[4:8], refs[8:12], refs[12]
    x_ref, wqkv_ref, wo_ref, cot_ref = held
    loads = [
        (inputs[0], x_ref),
        (inputs[1].at[1], wqkv_ref.at[1]),
        (inputs[1].at[2], wqkv_ref.at[2]),
        (inputs[1].at[0], wqkv_ref.at[0]),
        (inputs[2], wo_ref),
        (inputs[3], cot_ref),
    ]
    loads = [pltpu.make_async_copy(a, b, sems.at[i]) for i, (a, b) in enumerate(loads)]
    for load in loads:
        load.start()
    for load in loads[:3]:
        load.wait()
    kv_ref[0] = nn(x_ref[...], wqkv_ref[1]).astype(BF)
    kv_ref[1] = nn(x_ref[...], wqkv_ref[2]).astype(BF)
    for load in loads[3:]:
        load.wait()
    q_ref[...] = nn(x_ref[...], wqkv_ref[0]).astype(BF)
    u_ref[...] = nt(cot_ref[...], wo_ref[...]).astype(BF)

    pick_rows(1 - place_of()[1], x_ref, cot_ref, xc_ref)


def mine_kernel(x_ref, cot_ref, xc_ref):
    pick_rows(place_of()[1], x_ref, cot_ref, xc_ref)


def attention_kernel(q_ref, u_ref, far_ref, own_ref, mate_ref, bias_ref, acts_ref, gf_ref, go_ref, gm_ref):
    factor = HD**-0.5
    window = (far_ref, own_ref, mate_ref)
    grads = (gf_ref, go_ref, gm_ref)
    lane = lax.broadcasted_iota(jnp.int32, (1, 128), 1)
    picks = [(lane < HD).astype(F32).astype(BF), (lane >= HD).astype(F32).astype(BF)]
    first = lax.broadcasted_iota(jnp.int32, (ROWS, 128), 1) < HD
    bias = [
        jnp.concatenate(
            [
                jnp.broadcast_to(bias_ref[b : b + 1, c * ROWS : (c + 1) * ROWS], (BLOCK, ROWS))
                for b in range(ROWS // BLOCK)
            ],
            axis=0,
        )
        for c in range(3)
    ]
    for pair in range(WIDTH // 128):
        cols = slice(pair * 128, (pair + 1) * 128)
        q2, u2 = q_ref[:, cols], u_ref[:, cols]
        keys = [w[0, :, cols] for w in window]
        values = [w[1, :, cols] for w in window]
        key_sum, value_sum = [None] * 3, [None] * 3
        att, dq = [], []
        for pick in picks:
            qm, um = q2 * pick, u2 * pick
            weights = [jnp.exp2(nt(qm, keys[c]) * (factor * LOG2E) + bias[c]) for c in range(3)]
            total = sum(jnp.sum(w, axis=1, keepdims=True) for w in weights)
            share = 1.0 / total
            probs = [w * share for w in weights]
            low = [p.astype(BF) for p in probs]
            dprob = [nt(um, values[c]) for c in range(3)]
            spread = sum(jnp.sum(p * d, axis=1, keepdims=True) for p, d in zip(probs, dprob))
            dscore = [(p * (d - spread) * factor).astype(BF) for p, d in zip(probs, dprob)]
            att.append(sum(nn(low[c], values[c]) for c in range(3)))
            dq.append(sum(nn(dscore[c], keys[c]) for c in range(3)))
            for c in range(3):
                dk, dv = tn(dscore[c], qm), tn(low[c], um)
                key_sum[c] = dk if key_sum[c] is None else key_sum[c] + dk
                value_sum[c] = dv if value_sum[c] is None else value_sum[c] + dv
        acts_ref[0, :, cols] = jnp.where(first, att[0], att[1]).astype(BF)
        acts_ref[1, :, cols] = jnp.where(first, dq[0], dq[1]).astype(BF)
        for c in range(3):
            grads[c][0, :, cols] = key_sum[c].astype(grads[c].dtype)
            grads[c][1, :, cols] = value_sum[c].astype(grads[c].dtype)


def head_kernel(acts_ref, dkv_ref, wo_ref, w_ref, own_ref, *sent):
    head = place_of()[3]
    for k in range(4):
        span = pl.ds(pl.multiple_of((head ^ k) * WIDTH, WIDTH), WIDTH)
        out = nn(acts_ref[0], wo_ref[:, span])
        grad = nt(acts_ref[1], w_ref[0, span, :])
        grad = grad + nt(dkv_ref[0], w_ref[1, span, :])
        grad = grad + nt(dkv_ref[1], w_ref[2, span, :])
        to = own_ref if k == 0 else sent[k - 1]
        to[0] = out.astype(to.dtype)
        to[1] = grad.astype(to.dtype)


def head_sum_kernel(own_ref, r1_ref, r2_ref, r3_ref, x_ref, cot_ref, out_ref, grad_ref, token_ref):
    token_ref[...] = jnp.zeros_like(token_ref)
    span = pl.ds(pl.multiple_of(place_of()[3] * WIDTH, WIDTH), WIDTH)
    for i, (base, to) in enumerate(((x_ref, out_ref), (cot_ref, grad_ref))):
        total = own_ref[i] + r1_ref[i].astype(F32) + r2_ref[i].astype(F32) + r3_ref[i].astype(F32)
        to[...] = (base[:, span].astype(F32) + total).astype(BF)


def dkv_kernel(own_ref, a_ref, b_ref, out_ref):
    out_ref[...] = (own_ref[...] + a_ref[...].astype(F32) + b_ref[...].astype(F32)).astype(BF)


def early_kernel(mine_ref, other_ref, left_ref, right_ref, own_ref, rest_ref):
    for i, (side, act) in enumerate(((0, 1), (1, 0))):
        cols = slice(i * WIDTH, (i + 1) * WIDTH)
        g = nn(mine_ref[side], left_ref[act]) + nn(other_ref[side], right_ref[act])
        own_ref[:, cols] = g[:128]
        rest_ref[:, cols] = g[128:].astype(BF)


def late_kernel(mine_ref, other_ref, left_ref, right_ref, own1_ref, rest1_ref, own_ref, *sent):
    own_ref[:, : 2 * WIDTH] = own1_ref[...]
    for k in range(3):
        sent[k][:, : 2 * WIDTH] = rest1_ref[k * 128 : (k + 1) * 128, :]
    for i in range(2):
        cols = slice((2 + i) * WIDTH, (3 + i) * WIDTH)
        g = nn(mine_ref[0], left_ref[i]) + nn(other_ref[0], right_ref[i])
        own_ref[:, cols] = g[:128]
        for k in range(3):
            sent[k][:, cols] = g[(k + 1) * 128 : (k + 2) * 128].astype(BF)


def ysum_kernel(own_ref, r1_ref, r2_ref, r3_ref, kept_ref, sent_ref):
    total = own_ref[...] + r1_ref[...].astype(F32) + r2_ref[...].astype(F32) + r3_ref[...].astype(F32)
    kept_ref[...] = total[:64]
    sent_ref[...] = total[64:].astype(BF)


def pair_sum_kernel(kept_ref, r_ref, own_ref, *sent):
    total = kept_ref[...] + r_ref[...].astype(F32)
    own_ref[...] = total[:16]
    for i in range(3):
        sent[i][...] = total[16 * i + 16 : 16 * i + 32].astype(BF)


def chunk_kernel(own_ref, r1_ref, r2_ref, r3_ref, out_ref):
    total = own_ref[...] + r1_ref[...].astype(F32) + r2_ref[...].astype(F32) + r3_ref[...].astype(F32)
    out_ref[...] = total.astype(BF)


def join_kernel(*refs):
    begin = 0
    for r in refs[:-1]:
        refs[-1][begin : begin + r.shape[0], :] = r[...]
        begin += r.shape[0]


def place_kernel(*refs):
    mine, other, (qkv_ref, out_ref, held, turned, sems) = refs[:4], refs[4:8], refs[8:]
    z, core, y, _ = place_of()
    copies = []
    for k in PLACE_ORDER:
        block = pl.ds(pl.multiple_of((y ^ k) * 256, 256), 256)
        for array, column in ((3, 1), (0, 0), (1, 2), (2, 3)):
            cols = slice(column * WIDTH, (column + 1) * WIDTH)
            for side, blocks in ((core, mine), (1 - core, other)):
                for m in range(8):
                    chunk = z ^ (2 * (m & 3) + (m >> 2))
                    rows = pl.ds(pl.multiple_of(side * 128 + chunk * 16, 16), 16)
                    held[k, array, rows, :] = blocks[k][m * 16 : m * 16 + 16, cols].astype(F32)
            if array == 3:
                turned[k] = held[k, 3].T
                copy = pltpu.make_async_copy(turned.at[k], out_ref.at[:, block], sems.at[k, 3])
            else:
                copy = pltpu.make_async_copy(
                    held.at[k, array], qkv_ref.at[array, block], sems.at[k, array]
                )
            copy.start()
            copies.append(copy)
    for copy in copies:
        copy.wait()


def per_device(tokens, neighbours, counts, w_qkv, w_out, cotangent):
    x, listed, occupied, cot = tokens[0], neighbours[0], counts[0], cotangent[0]
    n = 16
    swap = [(i, i ^ 1) for i in range(n)]
    cross = [(i, i if i in (0, n - 1) else i + 1 if i % 2 else i - 1) for i in range(n)]

    def pair_z(k):
        return [(i, i ^ (2 * k)) for i in range(n)]

    def pair(k):
        return [(i, i ^ k) for i in range(4)]

    def swapped(a):
        return lax.ppermute(a, "spatial", swap)

    kv, q, u, xc_sent = call(
        first_kernel,
        [
            shape((2, ROWS, WIDTH), BF),
            shape((ROWS, WIDTH), BF),
            shape((ROWS, WIDTH), BF),
            shape((2, 512, ROWS), BF),
        ],
        [x, w_qkv, w_out, cot],
        12 * ROWS * D * WIDTH,
        [HBM] * 4,
        scratch=[
            pltpu.VMEM((ROWS, D), BF),
            pltpu.VMEM((3, D, WIDTH), BF),
            pltpu.VMEM((WIDTH, D), BF),
            pltpu.VMEM((ROWS, D), BF),
            pltpu.SemaphoreType.DMA((6,)),
        ],
        vmem=53,
    )
    far_kv = lax.ppermute(kv, "spatial", cross)
    mate_kv = swapped(kv)

    xc_other = swapped(xc_sent)

    spatial = lax.axis_index("spatial")
    base, side = spatial * 4, 1 - 2 * (spatial % 2)
    ids = (base + jnp.array([-4, 0, 4]) * side)[:, None] + jnp.arange(4)
    ids = ids.reshape(12).astype(jnp.int32)
    hit = jnp.any(listed[:, :, None] == ids[None, None, :], axis=1)
    table = jnp.arange(occupied.shape[0], dtype=jnp.int32)
    limit = jnp.sum(jnp.where(ids[:, None] == table[None, :], occupied[None, :], 0), axis=1)
    limit = jnp.where(hit, limit[None, :], 0)
    slots = jnp.arange(BLOCK, dtype=jnp.int32)
    bias = jnp.where(slots[None, None, :] < limit[:, :, None], 0.0, -1e30).astype(F32)
    bias = bias.reshape(4, 12 * BLOCK)

    acts, grad_far, grad_own, grad_mate = call(
        attention_kernel,
        [
            shape((2, ROWS, WIDTH), BF),
            shape((2, ROWS, WIDTH), BF),
            shape((2, ROWS, WIDTH), F32),
            shape((2, ROWS, WIDTH), BF),
        ],
        [q, u, far_kv, kv, mate_kv, bias],
        10 * 256 * 768 * 256,
        vmem=32,
    )
    from_far = lax.ppermute(grad_far, "spatial", cross)
    from_mate = swapped(grad_mate)
    acts_other = swapped(acts)
    xc_mine = call(
        mine_kernel,
        [shape((2, 512, ROWS), BF)],
        [x, cot],
        4 * 512 * 256 * D,
        after=[acts],
    )[0]
    early = call(
        early_kernel,
        [shape((128, 512), F32), shape((384, 512), BF)],
        [xc_mine, xc_other, acts, acts_other],
        4 * 512 * 512 * 256,
    )
    dkv = call(
        dkv_kernel,
        [shape((2, ROWS, WIDTH), BF)],
        [grad_own, from_far, from_mate],
        2**18,
        after=[early[0]],
    )[0]
    own, *to_y = call(
        late_kernel,
        [shape((128, D), F32)] + [shape((128, D), BF)] * 3,
        [xc_mine, xc_other, dkv, swapped(dkv), *early],
        4 * 512 * 512 * 256,
    )
    from_y = [lax.ppermute(a, "dp", pair(k)) for k, a in zip((1, 2, 3), to_y)]

    head_own, *to_head = call(
        head_kernel,
        [shape((2, ROWS, WIDTH), F32)] + [shape((2, ROWS, WIDTH), BF)] * 3,
        [acts, dkv, w_out, w_qkv],
        8 * ROWS * WIDTH * D,
        after=[own],
    )
    from_head = [lax.ppermute(a, "head", pair(k)) for k, a in zip((1, 2, 3), to_head)]

    kept, sent = call(
        ysum_kernel,
        [shape((64, D), F32), shape((64, D), BF)],
        [own] + from_y,
        2**20,
        after=[from_head[0], from_head[2]],
    )
    own, *to_z = call(
        pair_sum_kernel,
        [shape((16, D), F32)] + [shape((16, D), BF)] * 3,
        [kept, lax.ppermute(sent, "spatial", pair_z(1))],
        2**18,
    )
    from_z = [lax.ppermute(a, "spatial", pair_z(k)) for k, a in zip((2, 4, 6), to_z)]
    chunk = call(chunk_kernel, [shape((16, D), BF)], [own] + from_z, 2**16)[0]
    pieces = [chunk] + [lax.ppermute(chunk, "spatial", pair_z(k)) for k in (2, 4, 6)]
    layer_out, grad_tokens, token = call(
        head_sum_kernel,
        [shape((ROWS, WIDTH), BF)] * 2 + [shape((8, 128), F32)],
        [head_own, *from_head, x, cot],
        2**20,
        after=[chunk],
    )
    half = call(join_kernel, [shape((64, D), BF)], pieces, 2**16)[0]
    column = call(
        join_kernel,
        [shape((128, D), BF)],
        [half, lax.ppermute(half, "spatial", pair_z(1))],
        2**16,
        after=[token],
    )[0]
    mine = [column] + [lax.ppermute(column, "dp", pair(k)) for k in (1, 2, 3)]
    other = [swapped(a) for a in mine]
    grad_qkv, grad_out = call(
        place_kernel,
        [shape((3, D, WIDTH), F32), shape((WIDTH, D), F32)],
        mine + other,
        2**20,
        scratch=[
            pltpu.VMEM((4, 4, 256, WIDTH), F32),
            pltpu.VMEM((4, WIDTH, 256), F32),
            pltpu.SemaphoreType.DMA((4, 4)),
        ],
        out_specs=[ANY, ANY],
    )
    return layer_out[None], grad_tokens[None], grad_qkv, grad_out


def solution(mesh):
    in_specs = (
        P("dp", "spatial", None),
        P("dp", "spatial", None),
        P("dp", None),
        P(None, None, "head"),
        P("head", None),
        P("dp", "spatial", None),
    )
    out_specs = (
        P("dp", "spatial", "head"),
        P("dp", "spatial", "head"),
        P(None, None, "head"),
        P("head", None),
    )
    return jax.shard_map(
        per_device, mesh=mesh, in_specs=in_specs, out_specs=out_specs, check_vma=False
    )
```

time: 121 us -> 99 us (0.82)
  starting transfers between devices: 59.3 us -> 51.2 us
  matrix products: 5.47 us -> 0 us
  other arithmetic: 4.2 us -> 0.7 us
  Pallas kernels: 15.9 us -> 13 us
  local copies, waits for them, and re-layouts: 3.12 us -> 0.45 us
    ppermute x27 -> x19, starting transfers between devices: 47 us -> 32.8 us  [the longest x3 8.69 us: per_device(): lax.ppermute(a, 'spatial', pair_z(k))]
    ppermute x9, starting transfers between devices: 12.3 us -> 18.4 us  [swapped(): return lax.ppermute(a, 'spatial', swap)]
    dot_general x6 -> x0, matrix products: 5.47 us -> none  [the longest x4 2.66 us: picked(): lax.dot_general(pick, a, (((0,), (1,)), ((), ())), preferred_element_type...]
    broadcast_in_dim x2 -> x0, other arithmetic: 3.46 us -> none  [per_device(): return (layer_out[None], grad_tokens[None], grad_qkv, grad_out)]
    pallas_call x9 -> x14, Pallas kernels: 15.9 us -> 13 us  [call(): pl.pallas_call(body, out_shape=outs, in_specs=(in_specs or [VMEM] * count...]
    ppermute x9, waiting for transfers between devices: 0.02 us -> 2.69 us  [swapped(): return lax.ppermute(a, 'spatial', swap)]
    unnamed x28 -> x14, local copies, waits for them, and re-layouts: 2.7 us -> 0.04 us
    ppermute x27 -> x19, waiting for transfers between devices: 31.6 us -> 29.7 us  [the longest x3 9.9 us: per_device(): from_y = [lax.ppermute(a, 'dp', pair(k)) for k, a in zip((1, 2, 3), to_y)]]
  transfers between devices with their start and end apart: 36 -> 28, of which waited for: 13 -> 14; matrix products, arithmetic and copies ran while one was open for 8% -> 1% of each run, Pallas kernels for 7% -> 6%
where the time goes in v2:
time: 99 us; the launch traced here: 98.8 us
  starting transfers between devices  51.2 us (52%)
  waiting for transfers between devices  32.4 us (33%)
  Pallas kernels  13 us (13%)
  between operations  1.09 us (1%)
    ppermute x9, starting transfers between devices, swapped(): return lax.ppermute(a, 'spatial', swap)  18.4 us
    pallas_call x14, Pallas kernels, call(): pl.pallas_call(body, out_shape=outs, in_specs=(in_specs or [VMEM] * count...  13 us
    ppermute x3, waiting for transfers between devices, per_device(): from_y = [lax.ppermute(a, 'dp', pair(k)) for k, a in zip((1, 2, 3), to_y)]  9.9 us
    ppermute x3, starting transfers between devices, per_device(): lax.ppermute(a, 'spatial', pair_z(k))  8.69 us
    ppermute x3, starting transfers between devices, per_device(): lax.ppermute(chunk, 'spatial', pair_z(k))  5.77 us
    ppermute x3, starting transfers between devices, per_device(): lax.ppermute(a, 'head', pair(k))  4.64 us
    ppermute x3, waiting for transfers between devices, per_device(): lax.ppermute(a, 'spatial', pair_z(k))  4.61 us
    ppermute x1, waiting for transfers between devices, per_device(): far_kv = lax.ppermute(kv, 'spatial', cross)  4.49 us
  transfers between devices with their start and end apart: 28, of which 14 were waited for; matrix products, arithmetic and copies ran while one was open for 1% of the time, Pallas kernels for 6%

profile of v2, /device:TPU:1, one launch (start us, length us, event | category | flops | bytes accessed | tf_op | source)
XLA Modules:
  0.0 98.8 jit_solution(12562572786922981491)
XLA Ops:
  0.6 0.0 copy-start.5
  0.7 3.8 %shard_map.102 = (bf16[2,256,256]{2,1,0:T(8,128)(2,1)S(1)}, bf16[256,256]{1,0:T(8,128)(2,1)S(1)}, bf16[256,256]{1,0:T(8,128)(2,1)S(1)}, bf16[2,512,256]{2,1,0:T(8,128)(2,1)}) custom-call(bf16[256,1024]{1,0:T(8,128)(2,1)} %bitcast.6, bf16[3,1024,256]{2,1,0:T(8,128)(2,1)} %refs_3_.1, bf16[256,1024]{1,0:T(8,128)(2,1)} %refs_2_.3, bf16[256,1024]{1,0:T(8,128)(2,1)} %bitcast.9), custom_call_target="tpu_custom_call" | custom-call | flops 805306368 | bytes 4194304 | tf_op jit(solution)/shard_map/pallas_call | solution.py:30
  4.5 3.3 %collective-permute-start.1 = (bf16[2,256,256]{2,1,0:T(8,128)(2,1)S(1)}, bf16[2,256,256]{2,1,0:T(8,128)(2,1)S(1)}, u32[]{:S(2)}, u32[]{:S(2)}) collective-permute-start(bf16[2,256,256]{2,1,0:T(8,128)(2,1)S(1)} %get-tuple-element.35.refs_3_), channel_id=1, source_target_pairs={{0,16},{16,0},{32,48},{48,32},{64,80},{80,64},{96,112},{112,96},{1... | collective-permute-start | bytes 786440 | tf_op jit(solution)/shard_map/ppermute | solution.py:264
  7.8 1.9 %collective-permute-start = (bf16[2,256,256]{2,1,0:T(8,128)(2,1)S(1)}, bf16[2,256,256]{2,1,0:T(8,128)(2,1)S(1)}, u32[]{:S(2)}, u32[]{:S(2)}) collective-permute-start(bf16[2,256,256]{2,1,0:T(8,128)(2,1)S(1)} %get-tuple-element.35.refs_3_), channel_id=1, source_target_pairs={{0,0},{16,32},{32,16},{48,64},{64,48},{80,96},{96,80},{112,128},{1... | collective-permute-start | bytes 786440 | tf_op jit(solution)/shard_map/ppermute | solution.py:286
  9.8 0.1 collective-permute-start.4
  9.9 0.1 iota_add_fusion
  10.0 0.1 add.40
  10.1 0.2 select_reduce_fusion
  10.2 0.4 compare_reduce_fusion
  10.6 0.1 broadcast_select_fusion
  10.7 0.1 copy.11
  10.8 0.1 lt.27
  10.8 0.1 lt.30
  10.9 0.1 lt.31
  11.0 0.0 collective-permute-done.1.refs_4_
  11.0 4.5 %collective-permute-done.refs_2_ = bf16[2,256,256]{2,1,0:T(8,128)(2,1)S(1)} collective-permute-done((bf16[2,256,256]{2,1,0:T(8,128)(2,1)S(1)}, bf16[2,256,256]{2,1,0:T(8,128)(2,1)S(1)}, u32[]{:S(2)}, u32[]{:S(2)}) %collective-permute-start) | collective-permute-done | bytes 262176 | tf_op jit(solution)/shard_map/ppermute | solution.py:286
  15.5 3.3 %shard_map.103 = (bf16[2,256,256]{2,1,0:T(8,128)(2,1)S(1)}, bf16[2,256,256]{2,1,0:T(8,128)(2,1)S(1)}, f32[2,256,256]{2,1,0:T(8,128)S(1)}, bf16[2,256,256]{2,1,0:T(8,128)(2,1)S(1)}) custom-call(bf16[256,256]{1,0:T(8,128)(2,1)S(1)} %get-tuple-element.33.refs_0_, bf16[256,256]{1,0:T(8,128)(2,1)S(1)} %get-tuple-element.34.refs_1_, ...), custom_call_target="tpu_custom_call" | custom-call | flops 503316480 | bytes 2371584 | tf_op jit(solution)/shard_map/pallas_call | solution.py:30
  18.9 0.1 collective-permute-start.5
  19.0 2.2 %collective-permute-start.2 = (bf16[2,256,256]{2,1,0:T(8,128)(2,1)S(1)}, bf16[2,256,256]{2,1,0:T(8,128)(2,1)S(1)}, u32[]{:S(2)}, u32[]{:S(2)}) collective-permute-start(bf16[2,256,256]{2,1,0:T(8,128)(2,1)S(1)} %get-tuple-element.38), channel_id=1, source_target_pairs={{0,0},{16,32},{32,16},{48,64},{64,48},{80,96},{96,80},{112,128},{1... | collective-permute-start | bytes 786440 | tf_op jit(solution)/shard_map/ppermute | solution.py:315
  21.2 0.1 collective-permute-start.3
  21.3 0.8 shard_map.104.refs_0_
  22.1 0.0 copy-start
  22.1 0.0 copy-start.1
  22.1 0.4 shard_map.105
  22.6 4.1 %collective-permute-done.2.refs_1_ = bf16[2,256,256]{2,1,0:T(8,128)(2,1)S(1)} collective-permute-done((bf16[2,256,256]{2,1,0:T(8,128)(2,1)S(1)}, bf16[2,256,256]{2,1,0:T(8,128)(2,1)S(1)}, u32[]{:S(2)}, u32[]{:S(2)}) %collective-permute-start.2) | collective-permute-done | bytes 262176 | tf_op jit(solution)/shard_map/ppermute | solution.py:315
  26.7 0.1 shard_map.106.refs_2_.refs_1_
  26.8 0.1 collective-permute-start.6
  26.9 1.5 %collective-permute-done.6.refs_3_ = bf16[2,256,256]{2,1,0:T(8,128)(2,1)S(1)} collective-permute-done((bf16[2,256,256]{2,1,0:T(8,128)(2,1)S(1)}, bf16[2,256,256]{2,1,0:T(8,128)(2,1)S(1)}, u32[]{:S(2)}, u32[]{:S(2)}) %collective-permute-start.6) | collective-permute-done | bytes 262176 | tf_op jit(solution)/shard_map/ppermute | solution.py:264
  28.4 0.4 shard_map.107
  28.9 0.1 collective-permute-start.10
  29.0 2.4 %collective-permute-start.11 = (bf16[128,1024]{1,0:T(8,128)(2,1)S(1)}, bf16[128,1024]{1,0:T(8,128)(2,1)S(1)}, u32[]{:S(2)}, u32[]{:S(2)}) collective-permute-start(bf16[128,1024]{1,0:T(8,128)(2,1)S(1)} %get-tuple-element.49), channel_id=1, source_target_pairs={{0,2},{1,3},{2,0},{3,1},{4,6},{5,7},{6,4},{7,5},{8,10},{9,11},{10,... | collective-permute-start | bytes 786440 | tf_op jit(solution)/shard_map/ppermute | solution.py:344
  31.4 1.4 %collective-permute-start.12 = (bf16[128,1024]{1,0:T(8,128)(2,1)S(1)}, bf16[128,1024]{1,0:T(8,128)(2,1)S(1)}, u32[]{:S(2)}, u32[]{:S(2)}) collective-permute-start(bf16[128,1024]{1,0:T(8,128)(2,1)S(1)} %get-tuple-element.50), channel_id=1, source_target_pairs={{0,3},{1,2},{2,1},{3,0},{4,7},{5,6},{6,5},{7,4},{8,11},{9,10},{10,... | collective-permute-start | bytes 786440 | tf_op jit(solution)/shard_map/ppermute | solution.py:344
  32.8 0.7 shard_map.108
  33.5 0.3 collective-permute-start.7
  33.8 1.6 %collective-permute-start.9 = (bf16[2,256,256]{2,1,0:T(8,128)(2,1)S(1)}, bf16[2,256,256]{2,1,0:T(8,128)(2,1)S(1)}, u32[]{:S(2)}, u32[]{:S(2)}) collective-permute-start(bf16[2,256,256]{2,1,0:T(8,128)(2,1)S(1)} %get-tuple-element.47), channel_id=1, source_target_pairs={{0,12},{4,8},{8,4},{12,0},{1,13},{5,9},{9,5},{13,1},{2,14},{6,10},... | collective-permute-start | bytes 786440 | tf_op jit(solution)/shard_map/ppermute | solution.py:353
  35.5 1.3 %collective-permute-done.10.refs_1_ = bf16[128,1024]{1,0:T(8,128)(2,1)S(1)} collective-permute-done((bf16[128,1024]{1,0:T(8,128)(2,1)S(1)}, bf16[128,1024]{1,0:T(8,128)(2,1)S(1)}, u32[]{:S(2)}, u32[]{:S(2)}) %collective-permute-start.10) | collective-permute-done | bytes 262176 | tf_op jit(solution)/shard_map/ppermute | solution.py:344
  36.7 6.7 %collective-permute-done.11.refs_2_ = bf16[128,1024]{1,0:T(8,128)(2,1)S(1)} collective-permute-done((bf16[128,1024]{1,0:T(8,128)(2,1)S(1)}, bf16[128,1024]{1,0:T(8,128)(2,1)S(1)}, u32[]{:S(2)}, u32[]{:S(2)}) %collective-permute-start.11) | collective-permute-done | bytes 262176 | tf_op jit(solution)/shard_map/ppermute | solution.py:344
  43.4 2.0 %collective-permute-done.12.refs_3_ = bf16[128,1024]{1,0:T(8,128)(2,1)S(1)} collective-permute-done((bf16[128,1024]{1,0:T(8,128)(2,1)S(1)}, bf16[128,1024]{1,0:T(8,128)(2,1)S(1)}, u32[]{:S(2)}, u32[]{:S(2)}) %collective-permute-start.12) | collective-permute-done | bytes 262176 | tf_op jit(solution)/shard_map/ppermute | solution.py:344
  45.4 0.1 shard_map.109
  45.5 1.6 %collective-permute-start.13 = (bf16[64,1024]{1,0:T(8,128)(2,1)S(1)}, bf16[64,1024]{1,0:T(8,128)(2,1)S(1)}, u32[]{:S(2)}, u32[]{:S(2)}) collective-permute-start(bf16[64,1024]{1,0:T(8,128)(2,1)S(1)} %get-tuple-element.52), channel_id=1, source_target_pairs={{0,32},{16,48},{32,0},{48,16},{64,96},{80,112},{96,64},{112,80},{1... | collective-permute-start | bytes 393224 | tf_op jit(solution)/shard_map/ppermute | solution.py:365
  47.1 2.7 %collective-permute-start.8 = (bf16[2,256,256]{2,1,0:T(8,128)(2,1)S(1)}, bf16[2,256,256]{2,1,0:T(8,128)(2,1)S(1)}, u32[]{:S(2)}, u32[]{:S(2)}) collective-permute-start(bf16[2,256,256]{2,1,0:T(8,128)(2,1)S(1)} %get-tuple-element.46), channel_id=1, source_target_pairs={{0,8},{4,12},{8,0},{12,4},{1,9},{5,13},{9,1},{13,5},{2,10},{6,14},... | collective-permute-start | bytes 786440 | tf_op jit(solution)/shard_map/ppermute | solution.py:353
  49.9 5.3 %collective-permute-start.14 = (bf16[16,1024]{1,0:T(8,128)(2,1)S(1)}, bf16[16,1024]{1,0:T(8,128)(2,1)S(1)}, u32[]{:S(2)}, u32[]{:S(2)}) collective-permute-start(bf16[16,1024]{1,0:T(8,128)(2,1)S(1)} %get-tuple-element.54), channel_id=1, source_target_pairs={{0,64},{16,80},{32,96},{48,112},{64,0},{80,16},{96,32},{112,48},{1... | collective-permute-start | bytes 98312 | tf_op jit(solution)/shard_map/ppermute | solution.py:368
  55.2 2.9 %collective-permute-start.15 = (bf16[16,1024]{1,0:T(8,128)(2,1)S(1)}, bf16[16,1024]{1,0:T(8,128)(2,1)S(1)}, u32[]{:S(2)}, u32[]{:S(2)}) collective-permute-start(bf16[16,1024]{1,0:T(8,128)(2,1)S(1)} %get-tuple-element.55), channel_id=1, source_target_pairs={{0,128},{16,144},{32,160},{48,176},{64,192},{80,208},{96,224},{112... | collective-permute-start | bytes 98312 | tf_op jit(solution)/shard_map/ppermute | solution.py:368
  58.1 0.5 collective-permute-start.16
  58.6 3.3 %collective-permute-done.15.refs_2_ = bf16[16,1024]{1,0:T(8,128)(2,1)S(1)} collective-permute-done((bf16[16,1024]{1,0:T(8,128)(2,1)S(1)}, bf16[16,1024]{1,0:T(8,128)(2,1)S(1)}, u32[]{:S(2)}, u32[]{:S(2)}) %collective-permute-start.15) | collective-permute-done | bytes 32800 | tf_op jit(solution)/shard_map/ppermute | solution.py:368
  61.9 1.3 %collective-permute-done.16.refs_3_ = bf16[16,1024]{1,0:T(8,128)(2,1)S(1)} collective-permute-done((bf16[16,1024]{1,0:T(8,128)(2,1)S(1)}, bf16[16,1024]{1,0:T(8,128)(2,1)S(1)}, u32[]{:S(2)}, u32[]{:S(2)}) %collective-permute-start.16) | collective-permute-done | bytes 32800 | tf_op jit(solution)/shard_map/ppermute | solution.py:368
  63.2 2.1 %collective-permute-start.19 = (bf16[16,1024]{1,0:T(8,128)(2,1)S(1)}, bf16[16,1024]{1,0:T(8,128)(2,1)S(1)}, u32[]{:S(2)}, u32[]{:S(2)}) collective-permute-start(bf16[16,1024]{1,0:T(8,128)(2,1)S(1)} %shard_map.111.refs_6_.refs_0_), channel_id=1, source_target_pairs={{0,192},{16,208},{32,224},{48,240},{64,128},{80,144},{96,160},{112... | collective-permute-start | bytes 98312 | tf_op jit(solution)/shard_map/ppermute | solution.py:370
  65.3 3.7 %collective-permute-start.18 = (bf16[16,1024]{1,0:T(8,128)(2,1)S(1)}, bf16[16,1024]{1,0:T(8,128)(2,1)S(1)}, u32[]{:S(2)}, u32[]{:S(2)}) collective-permute-start(bf16[16,1024]{1,0:T(8,128)(2,1)S(1)} %shard_map.111.refs_6_.refs_0_), channel_id=1, source_target_pairs={{0,128},{16,144},{32,160},{48,176},{64,192},{80,208},{96,224},{112... | collective-permute-start | bytes 98312 | tf_op jit(solution)/shard_map/ppermute | solution.py:370
  69.0 3.0 %collective-permute-done.18.refs_2_ = bf16[16,1024]{1,0:T(8,128)(2,1)S(1)} collective-permute-done((bf16[16,1024]{1,0:T(8,128)(2,1)S(1)}, bf16[16,1024]{1,0:T(8,128)(2,1)S(1)}, u32[]{:S(2)}, u32[]{:S(2)}) %collective-permute-start.18) | collective-permute-done | bytes 32800 | tf_op jit(solution)/shard_map/ppermute | solution.py:370
  72.0 1.0 collective-permute-done.17.refs_1_
  73.0 0.7 collective-permute-start.20
  73.7 0.8 shard_map.112
  74.5 2.6 %collective-permute-done.20.refs_1_ = bf16[64,1024]{1,0:T(8,128)(2,1)S(1)} collective-permute-done((bf16[64,1024]{1,0:T(8,128)(2,1)S(1)}, bf16[64,1024]{1,0:T(8,128)(2,1)S(1)}, u32[]{:S(2)}, u32[]{:S(2)}) %collective-permute-start.20) | collective-permute-done | bytes 131104 | tf_op jit(solution)/shard_map/ppermute | solution.py:382
  77.2 0.1 collective-permute-start.23
  77.3 0.1 collective-permute-start.22
  77.4 3.1 %collective-permute-start.21 = (bf16[128,1024]{1,0:T(8,128)(2,1)S(1)}, bf16[128,1024]{1,0:T(8,128)(2,1)S(1)}, u32[]{:S(2)}, u32[]{:S(2)}) collective-permute-start(bf16[128,1024]{1,0:T(8,128)(2,1)S(1)} %shard_map.114.refs_0_), channel_id=1, source_target_pairs={{0,1},{1,0},{2,3},{3,2},{4,5},{5,4},{6,7},{7,6},{8,9},{9,8},{10,11... | collective-permute-start | bytes 786440 | tf_op jit(solution)/shard_map/ppermute | solution.py:386
  80.5 7.5 %collective-permute-start.24 = (bf16[128,1024]{1,0:T(8,128)(2,1)S(1)}, bf16[128,1024]{1,0:T(8,128)(2,1)S(1)}, u32[]{:S(2)}, u32[]{:S(2)}) collective-permute-start(bf16[128,1024]{1,0:T(8,128)(2,1)S(1)} %shard_map.114.refs_0_), channel_id=1, source_target_pairs={{0,16},{16,0},{32,48},{48,32},{64,80},{80,64},{96,112},{112,96},{1... | collective-permute-start | bytes 786440 | tf_op jit(solution)/shard_map/ppermute | solution.py:264
  88.1 6.3 %collective-permute-start.27 = (bf16[128,1024]{1,0:T(8,128)(2,1)S(1)}, bf16[128,1024]{1,0:T(8,128)(2,1)S(1)}, u32[]{:S(2)}, u32[]{:S(2)}) collective-permute-start(bf16[128,1024]{1,0:T(8,128)(2,1)S(1)} %collective-permute-done.23.refs_3_), channel_id=1, source_target_pairs={{0,16},{16,0},{32,48},{48,32},{64,80},{80,64},{96,112},{112,96},{1... | collective-permute-start | bytes 786440 | tf_op jit(solution)/shard_map/ppermute | solution.py:264
  94.4 0.0 collective-permute-start.26
  94.4 0.8 collective-permute-start.25
  95.2 0.3 collective-permute-done.27.refs_7_
  95.5 0.4 collective-permute-done.26.refs_6_
  95.9 0.5 collective-permute-done.25.refs_5_
  96.4 2.3 %shard_map.115 = (f32[3,1024,256]{2,1,0:T(8,128)}, f32[256,1024]{1,0:T(8,128)}) custom-call(bf16[128,1024]{1,0:T(8,128)(2,1)S(1)} %shard_map.114.refs_0_, bf16[128,1024]{1,0:T(8,128)(2,1)S(1)} %collective-permute-done.21.refs_1_, bf16[128,1024]{1,0:T(8,128)(2,1)S(1)} %collective-permute-done.22.refs_2_, ...), custom_call_target="tpu_custom_call" | custom-call | flops 1048576 | bytes 6291456 | tf_op jit(solution)/shard_map/pallas_call | solution.py:30
  (32 shorter events, 0.1 us)
Async XLA Ops:
  0.6 9.2 %copy-start.5 = (s32[3]{0:T(128)S(1)}, s32[3]{0:T(128)}, u32[]{:S(2)}) copy-start(s32[3]{0:T(128)} %constant.30.clone) | copy-start | bytes 40
  0.6 20.6 %copy-start.3 = (bf16[1,256,1024]{2,1,0:T(8,128)(2,1)S(1)}, bf16[1,256,1024]{2,1,0:T(8,128)(2,1)}, u32[]{:S(2)}) copy-start(bf16[1,256,1024]{2,1,0:T(8,128)(2,1)} %param.12) | copy-start | bytes 1572868
  0.7 20.6 %copy-start.2 = (bf16[1,256,1024]{2,1,0:T(8,128)(2,1)S(1)}, bf16[1,256,1024]{2,1,0:T(8,128)(2,1)}, u32[]{:S(2)}) copy-start(bf16[1,256,1024]{2,1,0:T(8,128)(2,1)} %param.7) | copy-start | bytes 1572868
  0.7 9.4 %copy-start.6 = (s32[1,64]{1,0:T(1,128)S(1)}, s32[1,64]{1,0:T(1,128)}, u32[]{:S(2)}) copy-start(s32[1,64]{1,0:T(1,128)} %param.9) | copy-start | bytes 772
  0.7 9.6 %copy-start.4 = (s32[1,4,27]{2,1,0:T(4,128)S(1)}, s32[1,4,27]{2,1,0:T(4,128)}, u32[]{:S(2)}) copy-start(s32[1,4,27]{2,1,0:T(4,128)} %param.8) | copy-start | bytes 1300
  4.5 6.5 %collective-permute-start.1 = (bf16[2,256,256]{2,1,0:T(8,128)(2,1)S(1)}, bf16[2,256,256]{2,1,0:T(8,128)(2,1)S(1)}, u32[]{:S(2)}, u32[]{:S(2)}) collective-permute-start(bf16[2,256,256]{2,1,0:T(8,128)(2,1)S(1)} %get-tuple-element.35.refs_3_), channel_id=1, source_target_pairs={{0,16},{16,0},{32,48},{48,32},{64,80},{80,64},{96,112},{112,96},{1... | collective-permute-start | bytes 786440 | tf_op jit(solution)/shard_map/ppermute | solution.py:264
  7.8 7.7 %collective-permute-start = (bf16[2,256,256]{2,1,0:T(8,128)(2,1)S(1)}, bf16[2,256,256]{2,1,0:T(8,128)(2,1)S(1)}, u32[]{:S(2)}, u32[]{:S(2)}) collective-permute-start(bf16[2,256,256]{2,1,0:T(8,128)(2,1)S(1)} %get-tuple-element.35.refs_3_), channel_id=1, source_target_pairs={{0,0},{16,32},{32,16},{48,64},{64,48},{80,96},{96,80},{112,128},{1... | collective-permute-start | bytes 786440 | tf_op jit(solution)/shard_map/ppermute | solution.py:286
  9.8 12.3 %collective-permute-start.4 = (bf16[2,512,256]{2,1,0:T(8,128)(2,1)}, bf16[2,512,256]{2,1,0:T(8,128)(2,1)S(1)}, u32[]{:S(2)}, u32[]{:S(2)}) collective-permute-start(bf16[2,512,256]{2,1,0:T(8,128)(2,1)} %get-tuple-element.40), channel_id=1, source_target_pairs={{0,16},{16,0},{32,48},{48,32},{64,80},{80,64},{96,112},{112,96},{1... | collective-permute-start | bytes 1572872 | tf_op jit(solution)/shard_map/ppermute | solution.py:264
  18.9 3.2 %collective-permute-start.5 = (bf16[2,256,256]{2,1,0:T(8,128)(2,1)S(1)}, bf16[2,256,256]{2,1,0:T(8,128)(2,1)S(1)}, u32[]{:S(2)}, u32[]{:S(2)}) collective-permute-start(bf16[2,256,256]{2,1,0:T(8,128)(2,1)S(1)} %get-tuple-element.36.refs_2_.refs_0_), channel_id=1, source_target_pairs={{0,16},{16,0},{32,48},{48,32},{64,80},{80,64},{96,112},{112,96},{1... | collective-permute-start | bytes 786440 | tf_op jit(solution)/shard_map/ppermute | solution.py:264
  19.0 7.7 %collective-permute-start.2 = (bf16[2,256,256]{2,1,0:T(8,128)(2,1)S(1)}, bf16[2,256,256]{2,1,0:T(8,128)(2,1)S(1)}, u32[]{:S(2)}, u32[]{:S(2)}) collective-permute-start(bf16[2,256,256]{2,1,0:T(8,128)(2,1)S(1)} %get-tuple-element.38), channel_id=1, source_target_pairs={{0,0},{16,32},{32,16},{48,64},{64,48},{80,96},{96,80},{112,128},{1... | collective-permute-start | bytes 786440 | tf_op jit(solution)/shard_map/ppermute | solution.py:315
  21.2 5.5 %collective-permute-start.3 = (bf16[2,256,256]{2,1,0:T(8,128)(2,1)S(1)}, bf16[2,256,256]{2,1,0:T(8,128)(2,1)S(1)}, u32[]{:S(2)}, u32[]{:S(2)}) collective-permute-start(bf16[2,256,256]{2,1,0:T(8,128)(2,1)S(1)} %get-tuple-element.39), channel_id=1, source_target_pairs={{0,16},{16,0},{32,48},{48,32},{64,80},{80,64},{96,112},{112,96},{1... | collective-permute-start | bytes 786440 | tf_op jit(solution)/shard_map/ppermute | solution.py:264
  22.1 10.7 %copy-start = (bf16[3,1024,256]{2,1,0:T(8,128)(2,1)S(1)}, bf16[3,1024,256]{2,1,0:T(8,128)(2,1)}, u32[]{:S(2)}) copy-start(bf16[3,1024,256]{2,1,0:T(8,128)(2,1)} %refs_3_.1) | copy-start | bytes 4718596
  22.1 10.7 %copy-start.1 = (bf16[256,1024]{1,0:T(8,128)(2,1)S(1)}, bf16[256,1024]{1,0:T(8,128)(2,1)}, u32[]{:S(2)}) copy-start(bf16[256,1024]{1,0:T(8,128)(2,1)} %refs_2_.3) | copy-start | bytes 1572868
  26.8 1.6 %collective-permute-start.6 = (bf16[2,256,256]{2,1,0:T(8,128)(2,1)S(1)}, bf16[2,256,256]{2,1,0:T(8,128)(2,1)S(1)}, u32[]{:S(2)}, u32[]{:S(2)}) collective-permute-start(bf16[2,256,256]{2,1,0:T(8,128)(2,1)S(1)} %shard_map.106.refs_2_.refs_1_), channel_id=1, source_target_pairs={{0,16},{16,0},{32,48},{48,32},{64,80},{80,64},{96,112},{112,96},{1... | collective-permute-start | bytes 786440 | tf_op jit(solution)/shard_map/ppermute | solution.py:264
  28.9 7.9 %collective-permute-start.10 = (bf16[128,1024]{1,0:T(8,128)(2,1)S(1)}, bf16[128,1024]{1,0:T(8,128)(2,1)S(1)}, u32[]{:S(2)}, u32[]{:S(2)}) collective-permute-start(bf16[128,1024]{1,0:T(8,128)(2,1)S(1)} %get-tuple-element.48), channel_id=1, source_target_pairs={{0,1},{1,0},{2,3},{3,2},{4,5},{5,4},{6,7},{7,6},{8,9},{9,8},{10,11... | collective-permute-start | bytes 786440 | tf_op jit(solution)/shard_map/ppermute | solution.py:344
  29.0 14.4 %collective-permute-start.11 = (bf16[128,1024]{1,0:T(8,128)(2,1)S(1)}, bf16[128,1024]{1,0:T(8,128)(2,1)S(1)}, u32[]{:S(2)}, u32[]{:S(2)}) collective-permute-start(bf16[128,1024]{1,0:T(8,128)(2,1)S(1)} %get-tuple-element.49), channel_id=1, source_target_pairs={{0,2},{1,3},{2,0},{3,1},{4,6},{5,7},{6,4},{7,5},{8,10},{9,11},{10,... | collective-permute-start | bytes 786440 | tf_op jit(solution)/shard_map/ppermute | solution.py:344
  31.4 14.0 %collective-permute-start.12 = (bf16[128,1024]{1,0:T(8,128)(2,1)S(1)}, bf16[128,1024]{1,0:T(8,128)(2,1)S(1)}, u32[]{:S(2)}, u32[]{:S(2)}) collective-permute-start(bf16[128,1024]{1,0:T(8,128)(2,1)S(1)} %get-tuple-element.50), channel_id=1, source_target_pairs={{0,3},{1,2},{2,1},{3,0},{4,7},{5,6},{6,5},{7,4},{8,11},{9,10},{10,... | collective-permute-start | bytes 786440 | tf_op jit(solution)/shard_map/ppermute | solution.py:344
  33.5 11.8 %collective-permute-start.7 = (bf16[2,256,256]{2,1,0:T(8,128)(2,1)S(1)}, bf16[2,256,256]{2,1,0:T(8,128)(2,1)S(1)}, u32[]{:S(2)}, u32[]{:S(2)}) collective-permute-start(bf16[2,256,256]{2,1,0:T(8,128)(2,1)S(1)} %get-tuple-element.45), channel_id=1, source_target_pairs={{0,4},{4,0},{8,12},{12,8},{1,5},{5,1},{9,13},{13,9},{2,6},{6,2},{1... | collective-permute-start | bytes 786440 | tf_op jit(solution)/shard_map/ppermute | solution.py:353
  33.8 11.5 %collective-permute-start.9 = (bf16[2,256,256]{2,1,0:T(8,128)(2,1)S(1)}, bf16[2,256,256]{2,1,0:T(8,128)(2,1)S(1)}, u32[]{:S(2)}, u32[]{:S(2)}) collective-permute-start(bf16[2,256,256]{2,1,0:T(8,128)(2,1)S(1)} %get-tuple-element.47), channel_id=1, source_target_pairs={{0,12},{4,8},{8,4},{12,0},{1,13},{5,9},{9,5},{13,1},{2,14},{6,10},... | collective-permute-start | bytes 786440 | tf_op jit(solution)/shard_map/ppermute | solution.py:353
  45.5 4.4 %collective-permute-start.13 = (bf16[64,1024]{1,0:T(8,128)(2,1)S(1)}, bf16[64,1024]{1,0:T(8,128)(2,1)S(1)}, u32[]{:S(2)}, u32[]{:S(2)}) collective-permute-start(bf16[64,1024]{1,0:T(8,128)(2,1)S(1)} %get-tuple-element.52), channel_id=1, source_target_pairs={{0,32},{16,48},{32,0},{48,16},{64,96},{80,112},{96,64},{112,80},{1... | collective-permute-start | bytes 393224 | tf_op jit(solution)/shard_map/ppermute | solution.py:365
  47.1 26.6 %collective-permute-start.8 = (bf16[2,256,256]{2,1,0:T(8,128)(2,1)S(1)}, bf16[2,256,256]{2,1,0:T(8,128)(2,1)S(1)}, u32[]{:S(2)}, u32[]{:S(2)}) collective-permute-start(bf16[2,256,256]{2,1,0:T(8,128)(2,1)S(1)} %get-tuple-element.46), channel_id=1, source_target_pairs={{0,8},{4,12},{8,0},{12,4},{1,9},{5,13},{9,1},{13,5},{2,10},{6,14},... | collective-permute-start | bytes 786440 | tf_op jit(solution)/shard_map/ppermute | solution.py:353
  49.9 8.7 %collective-permute-start.14 = (bf16[16,1024]{1,0:T(8,128)(2,1)S(1)}, bf16[16,1024]{1,0:T(8,128)(2,1)S(1)}, u32[]{:S(2)}, u32[]{:S(2)}) collective-permute-start(bf16[16,1024]{1,0:T(8,128)(2,1)S(1)} %get-tuple-element.54), channel_id=1, source_target_pairs={{0,64},{16,80},{32,96},{48,112},{64,0},{80,16},{96,32},{112,48},{1... | collective-permute-start | bytes 98312 | tf_op jit(solution)/shard_map/ppermute | solution.py:368
  55.2 6.7 %collective-permute-start.15 = (bf16[16,1024]{1,0:T(8,128)(2,1)S(1)}, bf16[16,1024]{1,0:T(8,128)(2,1)S(1)}, u32[]{:S(2)}, u32[]{:S(2)}) collective-permute-start(bf16[16,1024]{1,0:T(8,128)(2,1)S(1)} %get-tuple-element.55), channel_id=1, source_target_pairs={{0,128},{16,144},{32,160},{48,176},{64,192},{80,208},{96,224},{112... | collective-permute-start | bytes 98312 | tf_op jit(solution)/shard_map/ppermute | solution.py:368
  58.1 5.2 %collective-permute-start.16 = (bf16[16,1024]{1,0:T(8,128)(2,1)S(1)}, bf16[16,1024]{1,0:T(8,128)(2,1)S(1)}, u32[]{:S(2)}, u32[]{:S(2)}) collective-permute-start(bf16[16,1024]{1,0:T(8,128)(2,1)S(1)} %get-tuple-element.56), channel_id=1, source_target_pairs={{0,192},{16,208},{32,224},{48,240},{64,128},{80,144},{96,160},{112... | collective-permute-start | bytes 98312 | tf_op jit(solution)/shard_map/ppermute | solution.py:368
  63.2 5.8 %collective-permute-start.19 = (bf16[16,1024]{1,0:T(8,128)(2,1)S(1)}, bf16[16,1024]{1,0:T(8,128)(2,1)S(1)}, u32[]{:S(2)}, u32[]{:S(2)}) collective-permute-start(bf16[16,1024]{1,0:T(8,128)(2,1)S(1)} %shard_map.111.refs_6_.refs_0_), channel_id=1, source_target_pairs={{0,192},{16,208},{32,224},{48,240},{64,128},{80,144},{96,160},{112... | collective-permute-start | bytes 98312 | tf_op jit(solution)/shard_map/ppermute | solution.py:370
  65.3 6.7 %collective-permute-start.18 = (bf16[16,1024]{1,0:T(8,128)(2,1)S(1)}, bf16[16,1024]{1,0:T(8,128)(2,1)S(1)}, u32[]{:S(2)}, u32[]{:S(2)}) collective-permute-start(bf16[16,1024]{1,0:T(8,128)(2,1)S(1)} %shard_map.111.refs_6_.refs_0_), channel_id=1, source_target_pairs={{0,128},{16,144},{32,160},{48,176},{64,192},{80,208},{96,224},{112... | collective-permute-start | bytes 98312 | tf_op jit(solution)/shard_map/ppermute | solution.py:370
  69.0 4.0 %collective-permute-start.17 = (bf16[16,1024]{1,0:T(8,128)(2,1)S(1)}, bf16[16,1024]{1,0:T(8,128)(2,1)S(1)}, u32[]{:S(2)}, u32[]{:S(2)}) collective-permute-start(bf16[16,1024]{1,0:T(8,128)(2,1)S(1)} %shard_map.111.refs_6_.refs_0_), channel_id=1, source_target_pairs={{0,64},{16,80},{32,96},{48,112},{64,0},{80,16},{96,32},{112,48},{1... | collective-permute-start | bytes 98312 | tf_op jit(solution)/shard_map/ppermute | solution.py:370
  73.0 4.2 %collective-permute-start.20 = (bf16[64,1024]{1,0:T(8,128)(2,1)S(1)}, bf16[64,1024]{1,0:T(8,128)(2,1)S(1)}, u32[]{:S(2)}, u32[]{:S(2)}) collective-permute-start(bf16[64,1024]{1,0:T(8,128)(2,1)S(1)} %shard_map.113.refs_0_), channel_id=1, source_target_pairs={{0,32},{16,48},{32,0},{48,16},{64,96},{80,112},{96,64},{112,80},{1... | collective-permute-start | bytes 393224 | tf_op jit(solution)/shard_map/ppermute | solution.py:382
  77.2 10.9 %collective-permute-start.23 = (bf16[128,1024]{1,0:T(8,128)(2,1)S(1)}, bf16[128,1024]{1,0:T(8,128)(2,1)S(1)}, u32[]{:S(2)}, u32[]{:S(2)}) collective-permute-start(bf16[128,1024]{1,0:T(8,128)(2,1)S(1)} %shard_map.114.refs_0_), channel_id=1, source_target_pairs={{0,3},{1,2},{2,1},{3,0},{4,7},{5,6},{6,5},{7,4},{8,11},{9,10},{10,... | collective-permute-start | bytes 786440 | tf_op jit(solution)/shard_map/ppermute | solution.py:386
  77.3 17.1 %collective-permute-start.22 = (bf16[128,1024]{1,0:T(8,128)(2,1)S(1)}, bf16[128,1024]{1,0:T(8,128)(2,1)S(1)}, u32[]{:S(2)}, u32[]{:S(2)}) collective-permute-start(bf16[128,1024]{1,0:T(8,128)(2,1)S(1)} %shard_map.114.refs_0_), channel_id=1, source_target_pairs={{0,2},{1,3},{2,0},{3,1},{4,6},{5,7},{6,4},{7,5},{8,10},{9,11},{10,... | collective-permute-start | bytes 786440 | tf_op jit(solution)/shard_map/ppermute | solution.py:386
  77.4 16.9 %collective-permute-start.21 = (bf16[128,1024]{1,0:T(8,128)(2,1)S(1)}, bf16[128,1024]{1,0:T(8,128)(2,1)S(1)}, u32[]{:S(2)}, u32[]{:S(2)}) collective-permute-start(bf16[128,1024]{1,0:T(8,128)(2,1)S(1)} %shard_map.114.refs_0_), channel_id=1, source_target_pairs={{0,1},{1,0},{2,3},{3,2},{4,5},{5,4},{6,7},{7,6},{8,9},{9,8},{10,11... | collective-permute-start | bytes 786440 | tf_op jit(solution)/shard_map/ppermute | solution.py:386
  80.5 14.7 %collective-permute-start.24 = (bf16[128,1024]{1,0:T(8,128)(2,1)S(1)}, bf16[128,1024]{1,0:T(8,128)(2,1)S(1)}, u32[]{:S(2)}, u32[]{:S(2)}) collective-permute-start(bf16[128,1024]{1,0:T(8,128)(2,1)S(1)} %shard_map.114.refs_0_), channel_id=1, source_target_pairs={{0,16},{16,0},{32,48},{48,32},{64,80},{80,64},{96,112},{112,96},{1... | collective-permute-start | bytes 786440 | tf_op jit(solution)/shard_map/ppermute | solution.py:264
  88.1 7.5 %collective-permute-start.27 = (bf16[128,1024]{1,0:T(8,128)(2,1)S(1)}, bf16[128,1024]{1,0:T(8,128)(2,1)S(1)}, u32[]{:S(2)}, u32[]{:S(2)}) collective-permute-start(bf16[128,1024]{1,0:T(8,128)(2,1)S(1)} %collective-permute-done.23.refs_3_), channel_id=1, source_target_pairs={{0,16},{16,0},{32,48},{48,32},{64,80},{80,64},{96,112},{112,96},{1... | collective-permute-start | bytes 786440 | tf_op jit(solution)/shard_map/ppermute | solution.py:264
  94.4 1.5 %collective-permute-start.26 = (bf16[128,1024]{1,0:T(8,128)(2,1)S(1)}, bf16[128,1024]{1,0:T(8,128)(2,1)S(1)}, u32[]{:S(2)}, u32[]{:S(2)}) collective-permute-start(bf16[128,1024]{1,0:T(8,128)(2,1)S(1)} %collective-permute-done.22.refs_2_), channel_id=1, source_target_pairs={{0,16},{16,0},{32,48},{48,32},{64,80},{80,64},{96,112},{112,96},{1... | collective-permute-start | bytes 786440 | tf_op jit(solution)/shard_map/ppermute | solution.py:264
  94.4 2.0 %collective-permute-start.25 = (bf16[128,1024]{1,0:T(8,128)(2,1)S(1)}, bf16[128,1024]{1,0:T(8,128)(2,1)S(1)}, u32[]{:S(2)}, u32[]{:S(2)}) collective-permute-start(bf16[128,1024]{1,0:T(8,128)(2,1)S(1)} %collective-permute-done.21.refs_1_), channel_id=1, source_target_pairs={{0,16},{16,0},{32,48},{48,32},{64,80},{80,64},{96,112},{112,96},{1... | collective-permute-start | bytes 786440 | tf_op jit(solution)/shard_map/ppermute | solution.py:264

commit v3 on v2

--- a/solution.py
+++ b/solution.py
@@ -1,3 +1,5 @@
+import functools
+
 import jax
 import jax.numpy as jnp
 from jax import lax
@@ -10,7 +12,7 @@
 ROWS = 256
 WIDTH = 256
 D = 1024
-PLACE_ORDER = (0, 3, 1, 2)
+PLACE_ORDER = (0, 2, 3, 1)
 LOG2E = 1.4426950408889634
 BF = jnp.bfloat16
 F32 = jnp.float32
@@ -33,7 +35,7 @@
         in_specs=(in_specs or [VMEM] * count) + [ANY] * len(after),
         out_specs=out_specs or [VMEM] * len(outs),
         scratch_shapes=list(scratch),
-        compiler_params=pltpu.CompilerParams(vmem_limit_bytes=vmem * 2**20),
+        compiler_params=pltpu.CompilerParams(vmem_limit_bytes=int(vmem * 2**20)),
         cost_estimate=pl.CostEstimate(flops=flops, bytes_accessed=moved, transcendentals=0),
     )(*operands, *after)
 
@@ -62,9 +64,8 @@
 def picker(side):
     z, _, y, _ = place_of()
     c = lax.broadcasted_iota(jnp.int32, (512, 1), 0)
-    k, m = c >> 7, (c >> 4) & 7
-    chunk = z ^ (2 * (m & 3) + (m >> 2))
-    row = (y ^ k) * 256 + side * 128 + chunk * 16 + (c & 15)
+    k, m = c >> 7, (c >> 5) & 3
+    row = (y ^ k) * 256 + side * 128 + ((z & 3) ^ m) * 32 + (c & 31)
     feature = lax.broadcasted_iota(jnp.int32, (512, D), 1)
     return (feature == row).astype(F32).astype(BF)
 
@@ -75,37 +76,60 @@
     out_ref[1] = nt(pick, cot_ref[...]).astype(BF)
 
 
-def first_kernel(*refs):
-    inputs, (kv_ref, q_ref, u_ref, xc_ref), held, sems = refs[:4], refs[4:8], refs[8:12], refs[12]
-    x_ref, wqkv_ref, wo_ref, cot_ref = held
-    loads = [
-        (inputs[0], x_ref),
-        (inputs[1].at[1], wqkv_ref.at[1]),
-        (inputs[1].at[2], wqkv_ref.at[2]),
-        (inputs[1].at[0], wqkv_ref.at[0]),
-        (inputs[2], wo_ref),
-        (inputs[3], cot_ref),
-    ]
-    loads = [pltpu.make_async_copy(a, b, sems.at[i]) for i, (a, b) in enumerate(loads)]
+def fetch(pairs, sems):
+    loads = [pltpu.make_async_copy(a, b, sems.at[i]) for i, (a, b) in enumerate(pairs)]
     for load in loads:
         load.start()
-    for load in loads[:3]:
-        load.wait()
-    kv_ref[0] = nn(x_ref[...], wqkv_ref[1]).astype(BF)
-    kv_ref[1] = nn(x_ref[...], wqkv_ref[2]).astype(BF)
-    for load in loads[3:]:
-        load.wait()
-    q_ref[...] = nn(x_ref[...], wqkv_ref[0]).astype(BF)
+    return loads
+
+
+def kv_kernel(x_hbm, w_hbm, out_ref, x_ref, w_ref, sems):
+    pairs = [(x_hbm, x_ref), (w_hbm.at[1], w_ref.at[0]), (w_hbm.at[2], w_ref.at[1])]
+    x_load, *loads = fetch(pairs, sems)
+    x_load.wait()
+    for i in range(2):
+        loads[i].wait()
+        out_ref[i] = nn(x_ref[...], w_ref[i]).astype(BF)
+
+
+def prep_kernel(
+    x_hbm, w_hbm, wo_hbm, cot_hbm, blocks_ref,
+    q_ref, u_ref, xc_ref, bias_ref, x_ref, w_ref, wo_ref, cot_ref, sems
+):
+    pairs = [(x_hbm, x_ref), (w_hbm.at[0], w_ref), (cot_hbm, cot_ref), (wo_hbm, wo_ref)]
+    x_load, w_load, cot_load, wo_load = fetch(pairs, sems)
+
+    z, core, _, _ = place_of()
+    base = (z * 2 + core) * 4
+    starts = (base - 4 + 8 * core, base, base + 4 - 8 * core)
+    lane = lax.broadcasted_iota(jnp.int32, (4, 128), 1)
+    slot = (lane & (BLOCK - 1)).astype(F32)
+    table = lax.broadcasted_iota(jnp.int32, (1, 128), 1)
+    listed, occupied = blocks_ref[0:4, :], blocks_ref[4:5, :].astype(F32)
+
+    def limit(block):
+        hit = jnp.max(jnp.where(listed == block, 1.0, 0.0), axis=1, keepdims=True)
+        return hit * jnp.sum(jnp.where(table == block, occupied, 0.0), axis=1, keepdims=True)
+
+    for w in range(0, 12, 2):
+        block = starts[w // 4] + w % 4
+        edge = jnp.where(lane < BLOCK, limit(block), limit(block + 1))
+        bias_ref[:, w * BLOCK : (w + 2) * BLOCK] = jnp.where(slot < edge, 0.0, -1e30)
+
+    x_load.wait()
+    w_load.wait()
+    q_ref[...] = nn(x_ref[...], w_ref[...]).astype(BF)
+    cot_load.wait()
+    wo_load.wait()
     u_ref[...] = nt(cot_ref[...], wo_ref[...]).astype(BF)
-
-    pick_rows(1 - place_of()[1], x_ref, cot_ref, xc_ref)
+    pick_rows(1 - core, x_ref, cot_ref, xc_ref)
 
 
 def mine_kernel(x_ref, cot_ref, xc_ref):
     pick_rows(place_of()[1], x_ref, cot_ref, xc_ref)
 
 
-def attention_kernel(q_ref, u_ref, far_ref, own_ref, mate_ref, bias_ref, acts_ref, gf_ref, go_ref, gm_ref):
+def attention_kernel(q_ref, u_ref, mate_ref, own_ref, far_ref, bias_ref, acts_ref, gf_ref, go_ref, gm_ref):
     factor = HD**-0.5
     window = (far_ref, own_ref, mate_ref)
     grads = (gf_ref, go_ref, gm_ref)
@@ -152,15 +176,14 @@
             grads[c][1, :, cols] = value_sum[c].astype(grads[c].dtype)
 
 
-def head_kernel(acts_ref, dkv_ref, wo_ref, w_ref, own_ref, *sent):
+def head_kernel(acts_ref, dkv_ref, wo_ref, w_ref, *outs, parts):
     head = place_of()[3]
-    for k in range(4):
+    for to, k in zip(outs, parts):
         span = pl.ds(pl.multiple_of((head ^ k) * WIDTH, WIDTH), WIDTH)
         out = nn(acts_ref[0], wo_ref[:, span])
         grad = nt(acts_ref[1], w_ref[0, span, :])
         grad = grad + nt(dkv_ref[0], w_ref[1, span, :])
         grad = grad + nt(dkv_ref[1], w_ref[2, span, :])
-        to = own_ref if k == 0 else sent[k - 1]
         to[0] = out.astype(to.dtype)
         to[1] = grad.astype(to.dtype)
 
@@ -171,6 +194,23 @@
     for i, (base, to) in enumerate(((x_ref, out_ref), (cot_ref, grad_ref))):
         total = own_ref[i] + r1_ref[i].astype(F32) + r2_ref[i].astype(F32) + r3_ref[i].astype(F32)
         to[...] = (base[:, span].astype(F32) + total).astype(BF)
+
+
+def dkv_kernel(own_ref, a_ref, b_ref, out_ref):
+    out_ref[...] = (own_ref[...] + a_ref[...].astype(F32) + b_ref[...].astype(F32)).astype(BF)
+
+
+def dkv_kernel(own_ref, a_ref, b_ref, out_ref):
+    out_ref[...] = (own_ref[...] + a_ref[...].astype(F32) + b_ref[...].astype(F32)).astype(BF)
+
+
+def weight_kernel(mine_ref, other_ref, left_ref, right_ref, own_ref, *sent, terms):
+    for i, (side, act) in enumerate(terms):
+        cols = slice(i * WIDTH, (i + 1) * WIDTH)
+        g = nn(mine_ref[side], left_ref[act]) + nn(other_ref[side], right_ref[act])
+        own_ref[:, cols] = g[:128]
+        for k in range(3):
+            sent[k][:, cols] = g[(k + 1) * 128 : (k + 2) * 128].astype(BF)
 
 
 def dkv_kernel(own_ref, a_ref, b_ref, out_ref):
@@ -197,44 +237,42 @@
             sent[k][:, cols] = g[(k + 1) * 128 : (k + 2) * 128].astype(BF)
 
 
-def ysum_kernel(own_ref, r1_ref, r2_ref, r3_ref, kept_ref, sent_ref):
-    total = own_ref[...] + r1_ref[...].astype(F32) + r2_ref[...].astype(F32) + r3_ref[...].astype(F32)
-    kept_ref[...] = total[:64]
-    sent_ref[...] = total[64:].astype(BF)
-
-
-def pair_sum_kernel(kept_ref, r_ref, own_ref, *sent):
-    total = kept_ref[...] + r_ref[...].astype(F32)
-    own_ref[...] = total[:16]
-    for i in range(3):
-        sent[i][...] = total[16 * i + 16 : 16 * i + 32].astype(BF)
-
-
-def chunk_kernel(own_ref, r1_ref, r2_ref, r3_ref, out_ref):
-    total = own_ref[...] + r1_ref[...].astype(F32) + r2_ref[...].astype(F32) + r3_ref[...].astype(F32)
+def ysum_kernel(own_ref, r1_ref, r2_ref, r3_ref, kept_ref, *sent):
+    total = own_ref[...]
+    for r in (r1_ref, r2_ref, r3_ref):
+        total = total + r[...].astype(F32)
+    kept_ref[...] = total[:32]
+    for m in range(3):
+        sent[m][...] = total[32 * m + 32 : 32 * m + 64].astype(BF)
+
+
+def sum_kernel(*refs):
+    *parts, out_ref = refs
+    total = parts[0][...].astype(F32)
+    for r in parts[1:]:
+        total = total + r[...].astype(F32)
     out_ref[...] = total.astype(BF)
 
 
-def join_kernel(*refs):
-    begin = 0
-    for r in refs[:-1]:
-        refs[-1][begin : begin + r.shape[0], :] = r[...]
-        begin += r.shape[0]
+def join_kernel(*refs, order):
+    *parts, out_ref = refs
+    rows = parts[0].shape[0]
+    for i, r in zip(order, parts):
+        out_ref[i * rows : (i + 1) * rows, :] = r[...]
 
 
 def place_kernel(*refs):
     mine, other, (qkv_ref, out_ref, held, turned, sems) = refs[:4], refs[4:8], refs[8:]
     z, core, y, _ = place_of()
     copies = []
-    for k in PLACE_ORDER:
+    for n, k in enumerate(PLACE_ORDER):
         block = pl.ds(pl.multiple_of((y ^ k) * 256, 256), 256)
         for array, column in ((3, 1), (0, 0), (1, 2), (2, 3)):
             cols = slice(column * WIDTH, (column + 1) * WIDTH)
             for side, blocks in ((core, mine), (1 - core, other)):
-                for m in range(8):
-                    chunk = z ^ (2 * (m & 3) + (m >> 2))
-                    rows = pl.ds(pl.multiple_of(side * 128 + chunk * 16, 16), 16)
-                    held[k, array, rows, :] = blocks[k][m * 16 : m * 16 + 16, cols].astype(F32)
+                for m in range(4):
+                    rows = pl.ds(pl.multiple_of(side * 128 + ((z & 3) ^ m) * 32, 32), 32)
+                    held[k, array, rows, :] = blocks[n][m * 32 : m * 32 + 32, cols].astype(F32)
             if array == 3:
                 turned[k] = held[k, 3].T
                 copy = pltpu.make_async_copy(turned.at[k], out_ref.at[:, block], sems.at[k, 3])
@@ -263,42 +301,46 @@
     def swapped(a):
         return lax.ppermute(a, "spatial", swap)
 
-    kv, q, u, xc_sent = call(
-        first_kernel,
-        [
-            shape((2, ROWS, WIDTH), BF),
-            shape((ROWS, WIDTH), BF),
-            shape((ROWS, WIDTH), BF),
-            shape((2, 512, ROWS), BF),
-        ],
-        [x, w_qkv, w_out, cot],
-        12 * ROWS * D * WIDTH,
-        [HBM] * 4,
+    kv = call(
+        kv_kernel,
+        [shape((2, ROWS, WIDTH), BF)],
+        [x, w_qkv],
+        4 * ROWS * D * WIDTH,
+        [HBM] * 2,
         scratch=[
             pltpu.VMEM((ROWS, D), BF),
-            pltpu.VMEM((3, D, WIDTH), BF),
+            pltpu.VMEM((2, D, WIDTH), BF),
+            pltpu.SemaphoreType.DMA((3,)),
+        ],
+        vmem=53.5,
+    )[0]
+    blocks = jnp.concatenate(
+        [
+            jnp.pad(listed, ((0, 0), (0, 128 - listed.shape[1])), constant_values=-1),
+            jnp.pad(occupied[None], ((0, 0), (0, 128 - occupied.shape[0]))),
+        ],
+        axis=0,
+    )
+    q, u, xc_sent, bias = call(
+        prep_kernel,
+        [shape((ROWS, WIDTH), BF)] * 2 + [shape((2, 512, ROWS), BF), shape((4, 12 * BLOCK), F32)],
+        [x, w_qkv, w_out, cot, blocks],
+        8 * ROWS * D * WIDTH,
+        [HBM] * 4 + [VMEM],
+        scratch=[
+            pltpu.VMEM((ROWS, D), BF),
+            pltpu.VMEM((D, WIDTH), BF),
             pltpu.VMEM((WIDTH, D), BF),
             pltpu.VMEM((ROWS, D), BF),
-            pltpu.SemaphoreType.DMA((6,)),
+            pltpu.SemaphoreType.DMA((4,)),
         ],
         vmem=53,
-    )
+        after=[kv],
+    )
+    mate_kv = swapped(kv)
     far_kv = lax.ppermute(kv, "spatial", cross)
-    mate_kv = swapped(kv)
 
     xc_other = swapped(xc_sent)
-
-    spatial = lax.axis_index("spatial")
-    base, side = spatial * 4, 1 - 2 * (spatial % 2)
-    ids = (base + jnp.array([-4, 0, 4]) * side)[:, None] + jnp.arange(4)
-    ids = ids.reshape(12).astype(jnp.int32)
-    hit = jnp.any(listed[:, :, None] == ids[None, None, :], axis=1)
-    table = jnp.arange(occupied.shape[0], dtype=jnp.int32)
-    limit = jnp.sum(jnp.where(ids[:, None] == table[None, :], occupied[None, :], 0), axis=1)
-    limit = jnp.where(hit, limit[None, :], 0)
-    slots = jnp.arange(BLOCK, dtype=jnp.int32)
-    bias = jnp.where(slots[None, None, :] < limit[:, :, None], 0.0, -1e30).astype(F32)
-    bias = bias.reshape(4, 12 * BLOCK)
 
     acts, grad_far, grad_own, grad_mate = call(
         attention_kernel,
@@ -308,7 +350,7 @@
             shape((2, ROWS, WIDTH), F32),
             shape((2, ROWS, WIDTH), BF),
         ],
-        [q, u, far_kv, kv, mate_kv, bias],
+        [q, u, mate_kv, kv, far_kv, bias],
         10 * 256 * 768 * 256,
         vmem=32,
     )
@@ -341,49 +383,50 @@
         [xc_mine, xc_other, dkv, swapped(dkv), *early],
         4 * 512 * 512 * 256,
     )
-    from_y = [lax.ppermute(a, "dp", pair(k)) for k, a in zip((1, 2, 3), to_y)]
+    from_y = [lax.ppermute(to_y[k - 1], "dp", pair(k)) for k in (1, 3, 2)]
 
     head_own, *to_head = call(
-        head_kernel,
-        [shape((2, ROWS, WIDTH), F32)] + [shape((2, ROWS, WIDTH), BF)] * 3,
+        functools.partial(head_kernel, parts=(0, 1, 3)),
+        [shape((2, ROWS, WIDTH), F32)] + [shape((2, ROWS, WIDTH), BF)] * 2,
         [acts, dkv, w_out, w_qkv],
-        8 * ROWS * WIDTH * D,
+        6 * ROWS * WIDTH * D,
         after=[own],
     )
-    from_head = [lax.ppermute(a, "head", pair(k)) for k, a in zip((1, 2, 3), to_head)]
-
-    kept, sent = call(
+    from_head = [lax.ppermute(a, "head", pair(k)) for k, a in zip((1, 3), to_head)]
+
+    own, *to_z = call(
         ysum_kernel,
-        [shape((64, D), F32), shape((64, D), BF)],
+        [shape((32, D), F32)] + [shape((32, D), BF)] * 3,
         [own] + from_y,
         2**20,
-        after=[from_head[0], from_head[2]],
-    )
-    own, *to_z = call(
-        pair_sum_kernel,
-        [shape((16, D), F32)] + [shape((16, D), BF)] * 3,
-        [kept, lax.ppermute(sent, "spatial", pair_z(1))],
-        2**18,
-    )
-    from_z = [lax.ppermute(a, "spatial", pair_z(k)) for k, a in zip((2, 4, 6), to_z)]
-    chunk = call(chunk_kernel, [shape((16, D), BF)], [own] + from_z, 2**16)[0]
-    pieces = [chunk] + [lax.ppermute(chunk, "spatial", pair_z(k)) for k in (2, 4, 6)]
+    )
+    from_z = [lax.ppermute(to_z[m - 1], "spatial", pair_z(m)) for m in (2, 3, 1)]
+    part = call(sum_kernel, [shape((32, D), BF)], [own] + from_z, 2**18)[0]
+    far_part = lax.ppermute(part, "spatial", pair_z(4))
+    chunk = call(sum_kernel, [shape((32, D), BF)], [part, far_part], 2**16)[0]
+    pieces = [chunk] + [lax.ppermute(chunk, "spatial", pair_z(m)) for m in (1, 3, 2)]
+    column = call(
+        functools.partial(join_kernel, order=(0, 1, 3, 2)),
+        [shape((128, D), BF)],
+        pieces,
+        2**16,
+        after=from_head,
+    )[0]
+    mine = [column] + [lax.ppermute(column, "dp", pair(k)) for k in PLACE_ORDER[1:]]
+    last = call(
+        functools.partial(head_kernel, parts=(2,)),
+        [shape((2, ROWS, WIDTH), BF)],
+        [acts, dkv, w_out, w_qkv],
+        2 * ROWS * WIDTH * D,
+        after=[column],
+    )[0]
+    from_head.append(lax.ppermute(last, "head", pair(2)))
     layer_out, grad_tokens, token = call(
         head_sum_kernel,
         [shape((ROWS, WIDTH), BF)] * 2 + [shape((8, 128), F32)],
         [head_own, *from_head, x, cot],
         2**20,
-        after=[chunk],
-    )
-    half = call(join_kernel, [shape((64, D), BF)], pieces, 2**16)[0]
-    column = call(
-        join_kernel,
-        [shape((128, D), BF)],
-        [half, lax.ppermute(half, "spatial", pair_z(1))],
-        2**16,
-        after=[token],
-    )[0]
-    mine = [column] + [lax.ppermute(column, "dp", pair(k)) for k in (1, 2, 3)]
+    )
     other = [swapped(a) for a in mine]
     grad_qkv, grad_out = call(
         place_kernel,
@@ -396,6 +439,7 @@
             pltpu.SemaphoreType.DMA((4, 4)),
         ],
         out_specs=[ANY, ANY],
+        after=[token],
     )
     return layer_out[None], grad_tokens[None], grad_qkv, grad_out
 

time: 99 us -> 89.3 us (0.902)
  waiting for transfers between devices: 32.4 us -> 24.7 us
  starting transfers between devices: 51.2 us -> 47.8 us
  Pallas kernels: 13 us -> 14.9 us
    ppermute x9, starting transfers between devices: 18.4 us -> 10.2 us  [swapped(): return lax.ppermute(a, 'spatial', swap)]
    ppermute x1, waiting for transfers between devices: 4.49 us -> 0.01 us  [per_device(): far_kv = lax.ppermute(kv, 'spatial', cross)]
    ppermute x1, starting transfers between devices: 1.91 us -> 5.07 us  [per_device(): far_kv = lax.ppermute(kv, 'spatial', cross)]
    pallas_call x14 -> x15, Pallas kernels: 13 us -> 14.9 us  [call(): pl.pallas_call(body, out_shape=outs, in_specs=(in_specs or [VMEM] * count...]
    ppermute x1, starting transfers between devices: 2.18 us -> 3.9 us  [per_device(): from_far = lax.ppermute(grad_far, 'spatial', cross)]
    ppermute x1, waiting for transfers between devices: 4.11 us -> 2.67 us  [per_device(): from_far = lax.ppermute(grad_far, 'spatial', cross)]
    ppermute x3 -> x2, starting transfers between devices: 4.64 us -> 3.3 us  [per_device(): lax.ppermute(a, 'head', pair(k))]
    ppermute x14, waiting for transfers between devices: 21.1 us -> 19.8 us  [the longest x3 8 us: per_device(): from_y = [lax.ppermute(to_y[k - 1], 'dp', pair(k)) for k in (1, 3, 2)]]
  transfers between devices with their start and end apart: 28 -> 27, of which waited for: 14 -> 11; matrix products, arithmetic and copies ran while one was open for 1% -> 1% of each run, Pallas kernels for 6% -> 11%
where the time goes in v3:
time: 89.3 us; the launch traced here: 89.1 us
  starting transfers between devices  47.8 us (54%)
  waiting for transfers between devices  24.7 us (28%)
  Pallas kernels  14.9 us (17%)
  between operations  1 us (1%)
    pallas_call x15, Pallas kernels, call(): pl.pallas_call(body, out_shape=outs, in_specs=(in_specs or [VMEM] * count...  14.9 us
    ppermute x9, starting transfers between devices, swapped(): return lax.ppermute(a, 'spatial', swap)  10.2 us
    ppermute x3, waiting for transfers between devices, per_device(): from_y = [lax.ppermute(to_y[k - 1], 'dp', pair(k)) for k in (1, 3, 2)]  8 us
    ppermute x3, starting transfers between devices, per_device(): lax.ppermute(to_z[m - 1], 'spatial', pair_z(m))  6.87 us
    ppermute x3, waiting for transfers between devices, per_device(): lax.ppermute(chunk, 'spatial', pair_z(m))  5.27 us
    ppermute x1, starting transfers between devices, per_device(): far_kv = lax.ppermute(kv, 'spatial', cross)  5.07 us
    ppermute x3, starting transfers between devices, per_device(): lax.ppermute(chunk, 'spatial', pair_z(m))  4.43 us
    ppermute x3, starting transfers between devices, per_device(): from_y = [lax.ppermute(to_y[k - 1], 'dp', pair(k)) for k in (1, 3, 2)]  4 us
  transfers between devices with their start and end apart: 27, of which 11 were waited for; matrix products, arithmetic and copies ran while one was open for 1% of the time, Pallas kernels for 11%

profile of v3, /device:TPU:1, one launch (start us, length us, event | category | flops | bytes accessed | tf_op | source)
XLA Modules:
  0.0 89.1 jit_solution(5099457779786659897)
XLA Ops:
  0.6 2.1 %shard_map.93.refs_5_.refs_3_ = bf16[2,256,256]{2,1,0:T(8,128)(2,1)S(1)} custom-call(bf16[256,1024]{1,0:T(8,128)(2,1)} %bitcast.5, bf16[3,1024,256]{2,1,0:T(8,128)(2,1)} %refs_3_.3), custom_call_target="tpu_custom_call" | custom-call | flops 268435456 | bytes 2359296 | tf_op jit(solution)/shard_map/pallas_call | solution.py:32
  2.7 0.0 copy-start.2
  2.7 0.0 copy-start.3
  2.7 5.1 %collective-permute-start.1 = (bf16[2,256,256]{2,1,0:T(8,128)(2,1)S(1)}, bf16[2,256,256]{2,1,0:T(8,128)(2,1)S(1)}, u32[]{:S(2)}, u32[]{:S(2)}) collective-permute-start(bf16[2,256,256]{2,1,0:T(8,128)(2,1)S(1)} %shard_map.93.refs_5_.refs_3_), channel_id=1, source_target_pairs={{0,0},{16,32},{32,16},{48,64},{64,48},{80,96},{96,80},{112,128},{1... | collective-permute-start | bytes 786440 | tf_op jit(solution)/shard_map/ppermute | solution.py:341
  7.8 0.1 collective-permute-start
  7.9 0.7 pad_add_fusion.refs_4_
  8.6 3.5 %shard_map.94 = (bf16[256,256]{1,0:T(8,128)(2,1)S(1)}, bf16[256,256]{1,0:T(8,128)(2,1)S(1)}, bf16[2,512,256]{2,1,0:T(8,128)(2,1)}, f32[4,768]{1,0:T(4,128)S(1)}) custom-call(bf16[256,1024]{1,0:T(8,128)(2,1)} %bitcast.6, bf16[3,1024,256]{2,1,0:T(8,128)(2,1)} %refs_3_.3, bf16[256,1024]{1,0:T(8,128)(2,1)} %refs_2_.5, bf16[256,1024]{1,0:T(8,128)(2,1)} %bitcast.9, ...), custom_call_target="tpu_custom_call" | custom-call | flops 536870912 | bytes 3947008 | tf_op jit(solution)/shard_map/pallas_call | solution.py:32
  12.1 0.6 collective-permute-start.4
  12.7 0.0 collective-permute-done.1.refs_4_
  12.7 3.4 %shard_map.95 = (bf16[2,256,256]{2,1,0:T(8,128)(2,1)S(1)}, bf16[2,256,256]{2,1,0:T(8,128)(2,1)S(1)}, f32[2,256,256]{2,1,0:T(8,128)S(1)}, bf16[2,256,256]{2,1,0:T(8,128)(2,1)S(1)}) custom-call(bf16[256,256]{1,0:T(8,128)(2,1)S(1)} %get-tuple-element.30.refs_0_, bf16[256,256]{1,0:T(8,128)(2,1)S(1)} %get-tuple-element.31.refs_1_, ...), custom_call_target="tpu_custom_call" | custom-call | flops 503316480 | bytes 2371584 | tf_op jit(solution)/shard_map/pallas_call | solution.py:32
  16.1 0.1 collective-permute-start.5
  16.2 3.9 %collective-permute-start.2 = (bf16[2,256,256]{2,1,0:T(8,128)(2,1)S(1)}, bf16[2,256,256]{2,1,0:T(8,128)(2,1)S(1)}, u32[]{:S(2)}, u32[]{:S(2)}) collective-permute-start(bf16[2,256,256]{2,1,0:T(8,128)(2,1)S(1)} %get-tuple-element.35), channel_id=1, source_target_pairs={{0,0},{16,32},{32,16},{48,64},{64,48},{80,96},{96,80},{112,128},{1... | collective-permute-start | bytes 786440 | tf_op jit(solution)/shard_map/ppermute | solution.py:357
  20.1 0.1 collective-permute-start.3
  20.2 0.7 shard_map.96.refs_0_
  21.0 0.0 copy-start
  21.0 0.0 copy-start.1
  21.0 0.0 collective-permute-done.5.refs_3_
  21.0 0.4 shard_map.97
  21.5 2.7 %collective-permute-done.2.refs_1_ = bf16[2,256,256]{2,1,0:T(8,128)(2,1)S(1)} collective-permute-done((bf16[2,256,256]{2,1,0:T(8,128)(2,1)S(1)}, bf16[2,256,256]{2,1,0:T(8,128)(2,1)S(1)}, u32[]{:S(2)}, u32[]{:S(2)}) %collective-permute-start.2) | collective-permute-done | bytes 262176 | tf_op jit(solution)/shard_map/ppermute | solution.py:357
  24.2 0.1 shard_map.98.refs_2_.refs_1_
  24.3 0.1 collective-permute-start.6
  24.4 1.5 %collective-permute-done.6.refs_3_ = bf16[2,256,256]{2,1,0:T(8,128)(2,1)S(1)} collective-permute-done((bf16[2,256,256]{2,1,0:T(8,128)(2,1)S(1)}, bf16[2,256,256]{2,1,0:T(8,128)(2,1)S(1)}, u32[]{:S(2)}, u32[]{:S(2)}) %collective-permute-start.6) | collective-permute-done | bytes 262176 | tf_op jit(solution)/shard_map/ppermute | solution.py:302
  25.9 0.4 shard_map.99
  26.3 1.4 %collective-permute-start.9 = (bf16[128,1024]{1,0:T(8,128)(2,1)S(1)}, bf16[128,1024]{1,0:T(8,128)(2,1)S(1)}, u32[]{:S(2)}, u32[]{:S(2)}) collective-permute-start(bf16[128,1024]{1,0:T(8,128)(2,1)S(1)} %get-tuple-element.44), channel_id=1, source_target_pairs={{0,1},{1,0},{2,3},{3,2},{4,5},{5,4},{6,7},{7,6},{8,9},{9,8},{10,11... | collective-permute-start | bytes 786440 | tf_op jit(solution)/shard_map/ppermute | solution.py:386
  27.7 1.9 %collective-permute-start.10 = (bf16[128,1024]{1,0:T(8,128)(2,1)S(1)}, bf16[128,1024]{1,0:T(8,128)(2,1)S(1)}, u32[]{:S(2)}, u32[]{:S(2)}) collective-permute-start(bf16[128,1024]{1,0:T(8,128)(2,1)S(1)} %get-tuple-element.45), channel_id=1, source_target_pairs={{0,3},{1,2},{2,1},{3,0},{4,7},{5,6},{6,5},{7,4},{8,11},{9,10},{10,... | collective-permute-start | bytes 786440 | tf_op jit(solution)/shard_map/ppermute | solution.py:386
  29.6 0.7 collective-permute-start.11
  30.3 0.6 shard_map.100
  31.0 1.5 %collective-permute-start.7 = (bf16[2,256,256]{2,1,0:T(8,128)(2,1)S(1)}, bf16[2,256,256]{2,1,0:T(8,128)(2,1)S(1)}, u32[]{:S(2)}, u32[]{:S(2)}) collective-permute-start(bf16[2,256,256]{2,1,0:T(8,128)(2,1)S(1)} %get-tuple-element.42), channel_id=1, source_target_pairs={{0,4},{4,0},{8,12},{12,8},{1,5},{5,1},{9,13},{13,9},{2,6},{6,2},{1... | collective-permute-start | bytes 786440 | tf_op jit(solution)/shard_map/ppermute | solution.py:395
  32.4 1.8 %collective-permute-start.8 = (bf16[2,256,256]{2,1,0:T(8,128)(2,1)S(1)}, bf16[2,256,256]{2,1,0:T(8,128)(2,1)S(1)}, u32[]{:S(2)}, u32[]{:S(2)}) collective-permute-start(bf16[2,256,256]{2,1,0:T(8,128)(2,1)S(1)} %get-tuple-element.43), channel_id=1, source_target_pairs={{0,12},{4,8},{8,4},{12,0},{1,13},{5,9},{9,5},{13,1},{2,14},{6,10},... | collective-permute-start | bytes 786440 | tf_op jit(solution)/shard_map/ppermute | solution.py:395
  34.3 6.1 %collective-permute-done.10.refs_2_ = bf16[128,1024]{1,0:T(8,128)(2,1)S(1)} collective-permute-done((bf16[128,1024]{1,0:T(8,128)(2,1)S(1)}, bf16[128,1024]{1,0:T(8,128)(2,1)S(1)}, u32[]{:S(2)}, u32[]{:S(2)}) %collective-permute-start.10) | collective-permute-done | bytes 262176 | tf_op jit(solution)/shard_map/ppermute | solution.py:386
  40.3 1.9 %collective-permute-done.11.refs_3_ = bf16[128,1024]{1,0:T(8,128)(2,1)S(1)} collective-permute-done((bf16[128,1024]{1,0:T(8,128)(2,1)S(1)}, bf16[128,1024]{1,0:T(8,128)(2,1)S(1)}, u32[]{:S(2)}, u32[]{:S(2)}) %collective-permute-start.11) | collective-permute-done | bytes 262176 | tf_op jit(solution)/shard_map/ppermute | solution.py:386
  42.3 0.1 shard_map.101
  42.4 4.3 %collective-permute-start.12 = (bf16[32,1024]{1,0:T(8,128)(2,1)S(1)}, bf16[32,1024]{1,0:T(8,128)(2,1)S(1)}, u32[]{:S(2)}, u32[]{:S(2)}) collective-permute-start(bf16[32,1024]{1,0:T(8,128)(2,1)S(1)} %get-tuple-element.48), channel_id=1, source_target_pairs={{0,64},{16,80},{32,96},{48,112},{64,0},{80,16},{96,32},{112,48},{1... | collective-permute-start | bytes 196616 | tf_op jit(solution)/shard_map/ppermute | solution.py:403
  46.7 2.4 %collective-permute-start.13 = (bf16[32,1024]{1,0:T(8,128)(2,1)S(1)}, bf16[32,1024]{1,0:T(8,128)(2,1)S(1)}, u32[]{:S(2)}, u32[]{:S(2)}) collective-permute-start(bf16[32,1024]{1,0:T(8,128)(2,1)S(1)} %get-tuple-element.49), channel_id=1, source_target_pairs={{0,96},{16,112},{32,64},{48,80},{64,32},{80,48},{96,0},{112,16},{1... | collective-permute-start | bytes 196616 | tf_op jit(solution)/shard_map/ppermute | solution.py:403
  49.1 0.2 collective-permute-start.14
  49.2 0.0 collective-permute-done.12.refs_1_
  49.2 2.9 %collective-permute-done.13.refs_2_ = bf16[32,1024]{1,0:T(8,128)(2,1)S(1)} collective-permute-done((bf16[32,1024]{1,0:T(8,128)(2,1)S(1)}, bf16[32,1024]{1,0:T(8,128)(2,1)S(1)}, u32[]{:S(2)}, u32[]{:S(2)}) %collective-permute-start.13) | collective-permute-done | bytes 65568 | tf_op jit(solution)/shard_map/ppermute | solution.py:403
  52.1 0.3 collective-permute-done.14.refs_3_
  52.5 3.8 %collective-permute-start.15 = (bf16[32,1024]{1,0:T(8,128)(2,1)S(1)}, bf16[32,1024]{1,0:T(8,128)(2,1)S(1)}, u32[]{:S(2)}, u32[]{:S(2)}) collective-permute-start(bf16[32,1024]{1,0:T(8,128)(2,1)S(1)} %shard_map.102.refs_0_), channel_id=1, source_target_pairs={{0,128},{16,144},{32,160},{48,176},{64,192},{80,208},{96,224},{112... | collective-permute-start | bytes 196616 | tf_op jit(solution)/shard_map/ppermute | solution.py:405
  56.3 3.3 %collective-permute-done.15.refs_1_ = bf16[32,1024]{1,0:T(8,128)(2,1)S(1)} collective-permute-done((bf16[32,1024]{1,0:T(8,128)(2,1)S(1)}, bf16[32,1024]{1,0:T(8,128)(2,1)S(1)}, u32[]{:S(2)}, u32[]{:S(2)}) %collective-permute-start.15) | collective-permute-done | bytes 65568 | tf_op jit(solution)/shard_map/ppermute | solution.py:405
  59.6 4.0 %collective-permute-start.18 = (bf16[32,1024]{1,0:T(8,128)(2,1)S(1)}, bf16[32,1024]{1,0:T(8,128)(2,1)S(1)}, u32[]{:S(2)}, u32[]{:S(2)}) collective-permute-start(bf16[32,1024]{1,0:T(8,128)(2,1)S(1)} %shard_map.103.refs_0_), channel_id=1, source_target_pairs={{0,64},{16,80},{32,96},{48,112},{64,0},{80,16},{96,32},{112,48},{1... | collective-permute-start | bytes 196616 | tf_op jit(solution)/shard_map/ppermute | solution.py:407
  63.7 0.1 collective-permute-start.17
  63.8 0.3 collective-permute-start.16
  64.1 0.0 collective-permute-done.7.refs_4_.refs_1_
  64.1 0.0 collective-permute-done.8.refs_5_.refs_2_
  64.1 2.0 %collective-permute-done.18.refs_3_ = bf16[32,1024]{1,0:T(8,128)(2,1)S(1)} collective-permute-done((bf16[32,1024]{1,0:T(8,128)(2,1)S(1)}, bf16[32,1024]{1,0:T(8,128)(2,1)S(1)}, u32[]{:S(2)}, u32[]{:S(2)}) %collective-permute-start.18) | collective-permute-done | bytes 65568 | tf_op jit(solution)/shard_map/ppermute | solution.py:407
  66.0 3.3 %collective-permute-done.17.refs_2_ = bf16[32,1024]{1,0:T(8,128)(2,1)S(1)} collective-permute-done((bf16[32,1024]{1,0:T(8,128)(2,1)S(1)}, bf16[32,1024]{1,0:T(8,128)(2,1)S(1)}, u32[]{:S(2)}, u32[]{:S(2)}) %collective-permute-start.17) | collective-permute-done | bytes 65568 | tf_op jit(solution)/shard_map/ppermute | solution.py:407
  69.3 0.0 collective-permute-done.16.refs_1_
  69.4 0.1 collective-permute-start.22
  69.5 1.3 %collective-permute-start.21 = (bf16[128,1024]{1,0:T(8,128)(2,1)S(1)}, bf16[128,1024]{1,0:T(8,128)(2,1)S(1)}, u32[]{:S(2)}, u32[]{:S(2)}) collective-permute-start(bf16[128,1024]{1,0:T(8,128)(2,1)S(1)} %shard_map.104.refs_4_.refs_0_), channel_id=1, source_target_pairs={{0,3},{1,2},{2,1},{3,0},{4,7},{5,6},{6,5},{7,4},{8,11},{9,10},{10,... | collective-permute-start | bytes 786440 | tf_op jit(solution)/shard_map/ppermute | solution.py:415
  70.8 1.9 %collective-permute-start.20 = (bf16[128,1024]{1,0:T(8,128)(2,1)S(1)}, bf16[128,1024]{1,0:T(8,128)(2,1)S(1)}, u32[]{:S(2)}, u32[]{:S(2)}) collective-permute-start(bf16[128,1024]{1,0:T(8,128)(2,1)S(1)} %shard_map.104.refs_4_.refs_0_), channel_id=1, source_target_pairs={{0,2},{1,3},{2,0},{3,1},{4,6},{5,7},{6,4},{7,5},{8,10},{9,11},{10,... | collective-permute-start | bytes 786440 | tf_op jit(solution)/shard_map/ppermute | solution.py:415
  72.7 0.3 shard_map.105
  73.0 2.8 %collective-permute-start.19 = (bf16[2,256,256]{2,1,0:T(8,128)(2,1)S(1)}, bf16[2,256,256]{2,1,0:T(8,128)(2,1)S(1)}, u32[]{:S(2)}, u32[]{:S(2)}) collective-permute-start(bf16[2,256,256]{2,1,0:T(8,128)(2,1)S(1)} %shard_map.105), channel_id=1, source_target_pairs={{0,8},{4,12},{8,0},{12,4},{1,9},{5,13},{9,1},{13,5},{2,10},{6,14},... | collective-permute-start | bytes 786440 | tf_op jit(solution)/shard_map/ppermute | solution.py:423
  75.9 4.3 %collective-permute-start.23 = (bf16[128,1024]{1,0:T(8,128)(2,1)S(1)}, bf16[128,1024]{1,0:T(8,128)(2,1)S(1)}, u32[]{:S(2)}, u32[]{:S(2)}) collective-permute-start(bf16[128,1024]{1,0:T(8,128)(2,1)S(1)} %shard_map.104.refs_4_.refs_0_), channel_id=1, source_target_pairs={{0,16},{16,0},{32,48},{48,32},{64,80},{80,64},{96,112},{112,96},{1... | collective-permute-start | bytes 786440 | tf_op jit(solution)/shard_map/ppermute | solution.py:302
  80.1 0.9 collective-permute-start.26
  81.0 0.0 collective-permute-done.21.refs_2_
  81.0 4.1 %collective-permute-start.25 = (bf16[128,1024]{1,0:T(8,128)(2,1)S(1)}, bf16[128,1024]{1,0:T(8,128)(2,1)S(1)}, u32[]{:S(2)}, u32[]{:S(2)}) collective-permute-start(bf16[128,1024]{1,0:T(8,128)(2,1)S(1)} %collective-permute-done.21.refs_2_), channel_id=1, source_target_pairs={{0,16},{16,0},{32,48},{48,32},{64,80},{80,64},{96,112},{112,96},{1... | collective-permute-start | bytes 786440 | tf_op jit(solution)/shard_map/ppermute | solution.py:302
  85.1 0.0 collective-permute-done.20.refs_1_
  85.1 0.0 collective-permute-start.24
  85.1 0.0 collective-permute-done.19.refs_3_
  85.1 0.8 shard_map.106
  85.9 0.3 collective-permute-done.25.refs_6_
  86.3 0.4 collective-permute-done.24.refs_5_
  86.6 2.3 %shard_map.107 = (f32[3,1024,256]{2,1,0:T(8,128)}, f32[256,1024]{1,0:T(8,128)}) custom-call(bf16[128,1024]{1,0:T(8,128)(2,1)S(1)} %shard_map.104.refs_4_.refs_0_, bf16[128,1024]{1,0:T(8,128)(2,1)S(1)} %collective-permute-done.20.refs_1_, bf16[128,1024]{1,0:T(8,128)(2,1)S(1)} %collective-permute-done.21.refs_2_, ...), custom_call_target="tpu_custom_call" | custom-call | flops 1048576 | bytes 6291456 | tf_op jit(solution)/shard_map/pallas_call | solution.py:32
  (14 shorter events, 0.1 us)
Async XLA Ops:
  2.7 17.5 %copy-start.2 = (bf16[1,256,1024]{2,1,0:T(8,128)(2,1)S(1)}, bf16[1,256,1024]{2,1,0:T(8,128)(2,1)}, u32[]{:S(2)}) copy-start(bf16[1,256,1024]{2,1,0:T(8,128)(2,1)} %param.6) | copy-start | bytes 1572868
  2.7 17.5 %copy-start.3 = (bf16[1,256,1024]{2,1,0:T(8,128)(2,1)S(1)}, bf16[1,256,1024]{2,1,0:T(8,128)(2,1)}, u32[]{:S(2)}) copy-start(bf16[1,256,1024]{2,1,0:T(8,128)(2,1)} %param.11) | copy-start | bytes 1572868
  2.7 10.0 %collective-permute-start.1 = (bf16[2,256,256]{2,1,0:T(8,128)(2,1)S(1)}, bf16[2,256,256]{2,1,0:T(8,128)(2,1)S(1)}, u32[]{:S(2)}, u32[]{:S(2)}) collective-permute-start(bf16[2,256,256]{2,1,0:T(8,128)(2,1)S(1)} %shard_map.93.refs_5_.refs_3_), channel_id=1, source_target_pairs={{0,0},{16,32},{32,16},{48,64},{64,48},{80,96},{96,80},{112,128},{1... | collective-permute-start | bytes 786440 | tf_op jit(solution)/shard_map/ppermute | solution.py:341
  7.8 4.9 %collective-permute-start = (bf16[2,256,256]{2,1,0:T(8,128)(2,1)S(1)}, bf16[2,256,256]{2,1,0:T(8,128)(2,1)S(1)}, u32[]{:S(2)}, u32[]{:S(2)}) collective-permute-start(bf16[2,256,256]{2,1,0:T(8,128)(2,1)S(1)} %shard_map.93.refs_5_.refs_3_), channel_id=1, source_target_pairs={{0,16},{16,0},{32,48},{48,32},{64,80},{80,64},{96,112},{112,96},{1... | collective-permute-start | bytes 786440 | tf_op jit(solution)/shard_map/ppermute | solution.py:302
  12.1 8.9 %collective-permute-start.4 = (bf16[2,512,256]{2,1,0:T(8,128)(2,1)}, bf16[2,512,256]{2,1,0:T(8,128)(2,1)S(1)}, u32[]{:S(2)}, u32[]{:S(2)}) collective-permute-start(bf16[2,512,256]{2,1,0:T(8,128)(2,1)} %get-tuple-element.37), channel_id=1, source_target_pairs={{0,16},{16,0},{32,48},{48,32},{64,80},{80,64},{96,112},{112,96},{1... | collective-permute-start | bytes 1572872 | tf_op jit(solution)/shard_map/ppermute | solution.py:302
  16.1 4.9 %collective-permute-start.5 = (bf16[2,256,256]{2,1,0:T(8,128)(2,1)S(1)}, bf16[2,256,256]{2,1,0:T(8,128)(2,1)S(1)}, u32[]{:S(2)}, u32[]{:S(2)}) collective-permute-start(bf16[2,256,256]{2,1,0:T(8,128)(2,1)S(1)} %get-tuple-element.33.refs_2_.refs_0_), channel_id=1, source_target_pairs={{0,16},{16,0},{32,48},{48,32},{64,80},{80,64},{96,112},{112,96},{1... | collective-permute-start | bytes 786440 | tf_op jit(solution)/shard_map/ppermute | solution.py:302
  16.2 7.9 %collective-permute-start.2 = (bf16[2,256,256]{2,1,0:T(8,128)(2,1)S(1)}, bf16[2,256,256]{2,1,0:T(8,128)(2,1)S(1)}, u32[]{:S(2)}, u32[]{:S(2)}) collective-permute-start(bf16[2,256,256]{2,1,0:T(8,128)(2,1)S(1)} %get-tuple-element.35), channel_id=1, source_target_pairs={{0,0},{16,32},{32,16},{48,64},{64,48},{80,96},{96,80},{112,128},{1... | collective-permute-start | bytes 786440 | tf_op jit(solution)/shard_map/ppermute | solution.py:357
  20.1 4.0 %collective-permute-start.3 = (bf16[2,256,256]{2,1,0:T(8,128)(2,1)S(1)}, bf16[2,256,256]{2,1,0:T(8,128)(2,1)S(1)}, u32[]{:S(2)}, u32[]{:S(2)}) collective-permute-start(bf16[2,256,256]{2,1,0:T(8,128)(2,1)S(1)} %get-tuple-element.36), channel_id=1, source_target_pairs={{0,16},{16,0},{32,48},{48,32},{64,80},{80,64},{96,112},{112,96},{1... | collective-permute-start | bytes 786440 | tf_op jit(solution)/shard_map/ppermute | solution.py:302
  21.0 9.4 %copy-start = (bf16[3,1024,256]{2,1,0:T(8,128)(2,1)S(1)}, bf16[3,1024,256]{2,1,0:T(8,128)(2,1)}, u32[]{:S(2)}) copy-start(bf16[3,1024,256]{2,1,0:T(8,128)(2,1)} %refs_3_.3) | copy-start | bytes 4718596
  21.0 9.3 %copy-start.1 = (bf16[256,1024]{1,0:T(8,128)(2,1)S(1)}, bf16[256,1024]{1,0:T(8,128)(2,1)}, u32[]{:S(2)}) copy-start(bf16[256,1024]{1,0:T(8,128)(2,1)} %refs_2_.5) | copy-start | bytes 1572868
  24.3 1.6 %collective-permute-start.6 = (bf16[2,256,256]{2,1,0:T(8,128)(2,1)S(1)}, bf16[2,256,256]{2,1,0:T(8,128)(2,1)S(1)}, u32[]{:S(2)}, u32[]{:S(2)}) collective-permute-start(bf16[2,256,256]{2,1,0:T(8,128)(2,1)S(1)} %shard_map.98.refs_2_.refs_1_), channel_id=1, source_target_pairs={{0,16},{16,0},{32,48},{48,32},{64,80},{80,64},{96,112},{112,96},{1... | collective-permute-start | bytes 786440 | tf_op jit(solution)/shard_map/ppermute | solution.py:302
  26.3 7.9 %collective-permute-start.9 = (bf16[128,1024]{1,0:T(8,128)(2,1)S(1)}, bf16[128,1024]{1,0:T(8,128)(2,1)S(1)}, u32[]{:S(2)}, u32[]{:S(2)}) collective-permute-start(bf16[128,1024]{1,0:T(8,128)(2,1)S(1)} %get-tuple-element.44), channel_id=1, source_target_pairs={{0,1},{1,0},{2,3},{3,2},{4,5},{5,4},{6,7},{7,6},{8,9},{9,8},{10,11... | collective-permute-start | bytes 786440 | tf_op jit(solution)/shard_map/ppermute | solution.py:386
  27.7 12.6 %collective-permute-start.10 = (bf16[128,1024]{1,0:T(8,128)(2,1)S(1)}, bf16[128,1024]{1,0:T(8,128)(2,1)S(1)}, u32[]{:S(2)}, u32[]{:S(2)}) collective-permute-start(bf16[128,1024]{1,0:T(8,128)(2,1)S(1)} %get-tuple-element.45), channel_id=1, source_target_pairs={{0,3},{1,2},{2,1},{3,0},{4,7},{5,6},{6,5},{7,4},{8,11},{9,10},{10,... | collective-permute-start | bytes 786440 | tf_op jit(solution)/shard_map/ppermute | solution.py:386
  29.6 12.6 %collective-permute-start.11 = (bf16[128,1024]{1,0:T(8,128)(2,1)S(1)}, bf16[128,1024]{1,0:T(8,128)(2,1)S(1)}, u32[]{:S(2)}, u32[]{:S(2)}) collective-permute-start(bf16[128,1024]{1,0:T(8,128)(2,1)S(1)} %get-tuple-element.46), channel_id=1, source_target_pairs={{0,2},{1,3},{2,0},{3,1},{4,6},{5,7},{6,4},{7,5},{8,10},{9,11},{10,... | collective-permute-start | bytes 786440 | tf_op jit(solution)/shard_map/ppermute | solution.py:386
  31.0 33.1 %collective-permute-start.7 = (bf16[2,256,256]{2,1,0:T(8,128)(2,1)S(1)}, bf16[2,256,256]{2,1,0:T(8,128)(2,1)S(1)}, u32[]{:S(2)}, u32[]{:S(2)}) collective-permute-start(bf16[2,256,256]{2,1,0:T(8,128)(2,1)S(1)} %get-tuple-element.42), channel_id=1, source_target_pairs={{0,4},{4,0},{8,12},{12,8},{1,5},{5,1},{9,13},{13,9},{2,6},{6,2},{1... | collective-permute-start | bytes 786440 | tf_op jit(solution)/shard_map/ppermute | solution.py:395
  32.4 31.6 %collective-permute-start.8 = (bf16[2,256,256]{2,1,0:T(8,128)(2,1)S(1)}, bf16[2,256,256]{2,1,0:T(8,128)(2,1)S(1)}, u32[]{:S(2)}, u32[]{:S(2)}) collective-permute-start(bf16[2,256,256]{2,1,0:T(8,128)(2,1)S(1)} %get-tuple-element.43), channel_id=1, source_target_pairs={{0,12},{4,8},{8,4},{12,0},{1,13},{5,9},{9,5},{13,1},{2,14},{6,10},... | collective-permute-start | bytes 786440 | tf_op jit(solution)/shard_map/ppermute | solution.py:395
  42.4 6.9 %collective-permute-start.12 = (bf16[32,1024]{1,0:T(8,128)(2,1)S(1)}, bf16[32,1024]{1,0:T(8,128)(2,1)S(1)}, u32[]{:S(2)}, u32[]{:S(2)}) collective-permute-start(bf16[32,1024]{1,0:T(8,128)(2,1)S(1)} %get-tuple-element.48), channel_id=1, source_target_pairs={{0,64},{16,80},{32,96},{48,112},{64,0},{80,16},{96,32},{112,48},{1... | collective-permute-start | bytes 196616 | tf_op jit(solution)/shard_map/ppermute | solution.py:403
  46.7 5.5 %collective-permute-start.13 = (bf16[32,1024]{1,0:T(8,128)(2,1)S(1)}, bf16[32,1024]{1,0:T(8,128)(2,1)S(1)}, u32[]{:S(2)}, u32[]{:S(2)}) collective-permute-start(bf16[32,1024]{1,0:T(8,128)(2,1)S(1)} %get-tuple-element.49), channel_id=1, source_target_pairs={{0,96},{16,112},{32,64},{48,80},{64,32},{80,48},{96,0},{112,16},{1... | collective-permute-start | bytes 196616 | tf_op jit(solution)/shard_map/ppermute | solution.py:403
  49.1 3.4 %collective-permute-start.14 = (bf16[32,1024]{1,0:T(8,128)(2,1)S(1)}, bf16[32,1024]{1,0:T(8,128)(2,1)S(1)}, u32[]{:S(2)}, u32[]{:S(2)}) collective-permute-start(bf16[32,1024]{1,0:T(8,128)(2,1)S(1)} %get-tuple-element.50), channel_id=1, source_target_pairs={{0,32},{16,48},{32,0},{48,16},{64,96},{80,112},{96,64},{112,80},{1... | collective-permute-start | bytes 196616 | tf_op jit(solution)/shard_map/ppermute | solution.py:403
  52.5 7.1 %collective-permute-start.15 = (bf16[32,1024]{1,0:T(8,128)(2,1)S(1)}, bf16[32,1024]{1,0:T(8,128)(2,1)S(1)}, u32[]{:S(2)}, u32[]{:S(2)}) collective-permute-start(bf16[32,1024]{1,0:T(8,128)(2,1)S(1)} %shard_map.102.refs_0_), channel_id=1, source_target_pairs={{0,128},{16,144},{32,160},{48,176},{64,192},{80,208},{96,224},{112... | collective-permute-start | bytes 196616 | tf_op jit(solution)/shard_map/ppermute | solution.py:405
  59.6 6.4 %collective-permute-start.18 = (bf16[32,1024]{1,0:T(8,128)(2,1)S(1)}, bf16[32,1024]{1,0:T(8,128)(2,1)S(1)}, u32[]{:S(2)}, u32[]{:S(2)}) collective-permute-start(bf16[32,1024]{1,0:T(8,128)(2,1)S(1)} %shard_map.103.refs_0_), channel_id=1, source_target_pairs={{0,64},{16,80},{32,96},{48,112},{64,0},{80,16},{96,32},{112,48},{1... | collective-permute-start | bytes 196616 | tf_op jit(solution)/shard_map/ppermute | solution.py:407
  63.7 5.7 %collective-permute-start.17 = (bf16[32,1024]{1,0:T(8,128)(2,1)S(1)}, bf16[32,1024]{1,0:T(8,128)(2,1)S(1)}, u32[]{:S(2)}, u32[]{:S(2)}) collective-permute-start(bf16[32,1024]{1,0:T(8,128)(2,1)S(1)} %shard_map.103.refs_0_), channel_id=1, source_target_pairs={{0,96},{16,112},{32,64},{48,80},{64,32},{80,48},{96,0},{112,16},{1... | collective-permute-start | bytes 196616 | tf_op jit(solution)/shard_map/ppermute | solution.py:407
  63.8 5.6 %collective-permute-start.16 = (bf16[32,1024]{1,0:T(8,128)(2,1)S(1)}, bf16[32,1024]{1,0:T(8,128)(2,1)S(1)}, u32[]{:S(2)}, u32[]{:S(2)}) collective-permute-start(bf16[32,1024]{1,0:T(8,128)(2,1)S(1)} %shard_map.103.refs_0_), channel_id=1, source_target_pairs={{0,32},{16,48},{32,0},{48,16},{64,96},{80,112},{96,64},{112,80},{1... | collective-permute-start | bytes 196616 | tf_op jit(solution)/shard_map/ppermute | solution.py:407
  69.4 10.7 %collective-permute-start.22 = (bf16[128,1024]{1,0:T(8,128)(2,1)S(1)}, bf16[128,1024]{1,0:T(8,128)(2,1)S(1)}, u32[]{:S(2)}, u32[]{:S(2)}) collective-permute-start(bf16[128,1024]{1,0:T(8,128)(2,1)S(1)} %shard_map.104.refs_4_.refs_0_), channel_id=1, source_target_pairs={{0,1},{1,0},{2,3},{3,2},{4,5},{5,4},{6,7},{7,6},{8,9},{9,8},{10,11... | collective-permute-start | bytes 786440 | tf_op jit(solution)/shard_map/ppermute | solution.py:415
  69.5 11.5 %collective-permute-start.21 = (bf16[128,1024]{1,0:T(8,128)(2,1)S(1)}, bf16[128,1024]{1,0:T(8,128)(2,1)S(1)}, u32[]{:S(2)}, u32[]{:S(2)}) collective-permute-start(bf16[128,1024]{1,0:T(8,128)(2,1)S(1)} %shard_map.104.refs_4_.refs_0_), channel_id=1, source_target_pairs={{0,3},{1,2},{2,1},{3,0},{4,7},{5,6},{6,5},{7,4},{8,11},{9,10},{10,... | collective-permute-start | bytes 786440 | tf_op jit(solution)/shard_map/ppermute | solution.py:415
  70.8 14.3 %collective-permute-start.20 = (bf16[128,1024]{1,0:T(8,128)(2,1)S(1)}, bf16[128,1024]{1,0:T(8,128)(2,1)S(1)}, u32[]{:S(2)}, u32[]{:S(2)}) collective-permute-start(bf16[128,1024]{1,0:T(8,128)(2,1)S(1)} %shard_map.104.refs_4_.refs_0_), channel_id=1, source_target_pairs={{0,2},{1,3},{2,0},{3,1},{4,6},{5,7},{6,4},{7,5},{8,10},{9,11},{10,... | collective-permute-start | bytes 786440 | tf_op jit(solution)/shard_map/ppermute | solution.py:415
  73.0 12.1 %collective-permute-start.19 = (bf16[2,256,256]{2,1,0:T(8,128)(2,1)S(1)}, bf16[2,256,256]{2,1,0:T(8,128)(2,1)S(1)}, u32[]{:S(2)}, u32[]{:S(2)}) collective-permute-start(bf16[2,256,256]{2,1,0:T(8,128)(2,1)S(1)} %shard_map.105), channel_id=1, source_target_pairs={{0,8},{4,12},{8,0},{12,4},{1,9},{5,13},{9,1},{13,5},{2,10},{6,14},... | collective-permute-start | bytes 786440 | tf_op jit(solution)/shard_map/ppermute | solution.py:423
  75.9 10.1 %collective-permute-start.23 = (bf16[128,1024]{1,0:T(8,128)(2,1)S(1)}, bf16[128,1024]{1,0:T(8,128)(2,1)S(1)}, u32[]{:S(2)}, u32[]{:S(2)}) collective-permute-start(bf16[128,1024]{1,0:T(8,128)(2,1)S(1)} %shard_map.104.refs_4_.refs_0_), channel_id=1, source_target_pairs={{0,16},{16,0},{32,48},{48,32},{64,80},{80,64},{96,112},{112,96},{1... | collective-permute-start | bytes 786440 | tf_op jit(solution)/shard_map/ppermute | solution.py:302
  80.1 5.8 %collective-permute-start.26 = (bf16[128,1024]{1,0:T(8,128)(2,1)S(1)}, bf16[128,1024]{1,0:T(8,128)(2,1)S(1)}, u32[]{:S(2)}, u32[]{:S(2)}) collective-permute-start(bf16[128,1024]{1,0:T(8,128)(2,1)S(1)} %collective-permute-done.22.refs_3_), channel_id=1, source_target_pairs={{0,16},{16,0},{32,48},{48,32},{64,80},{80,64},{96,112},{112,96},{1... | collective-permute-start | bytes 786440 | tf_op jit(solution)/shard_map/ppermute | solution.py:302
  81.0 5.3 %collective-permute-start.25 = (bf16[128,1024]{1,0:T(8,128)(2,1)S(1)}, bf16[128,1024]{1,0:T(8,128)(2,1)S(1)}, u32[]{:S(2)}, u32[]{:S(2)}) collective-permute-start(bf16[128,1024]{1,0:T(8,128)(2,1)S(1)} %collective-permute-done.21.refs_2_), channel_id=1, source_target_pairs={{0,16},{16,0},{32,48},{48,32},{64,80},{80,64},{96,112},{112,96},{1... | collective-permute-start | bytes 786440 | tf_op jit(solution)/shard_map/ppermute | solution.py:302
  85.1 1.5 %collective-permute-start.24 = (bf16[128,1024]{1,0:T(8,128)(2,1)S(1)}, bf16[128,1024]{1,0:T(8,128)(2,1)S(1)}, u32[]{:S(2)}, u32[]{:S(2)}) collective-permute-start(bf16[128,1024]{1,0:T(8,128)(2,1)S(1)} %collective-permute-done.20.refs_1_), channel_id=1, source_target_pairs={{0,16},{16,0},{32,48},{48,32},{64,80},{80,64},{96,112},{112,96},{1... | collective-permute-start | bytes 786440 | tf_op jit(solution)/shard_map/ppermute | solution.py:302

commit v4 on v3

--- a/solution.py
+++ b/solution.py
@@ -200,23 +200,6 @@
     out_ref[...] = (own_ref[...] + a_ref[...].astype(F32) + b_ref[...].astype(F32)).astype(BF)
 
 
-def dkv_kernel(own_ref, a_ref, b_ref, out_ref):
-    out_ref[...] = (own_ref[...] + a_ref[...].astype(F32) + b_ref[...].astype(F32)).astype(BF)
-
-
-def weight_kernel(mine_ref, other_ref, left_ref, right_ref, own_ref, *sent, terms):
-    for i, (side, act) in enumerate(terms):
-        cols = slice(i * WIDTH, (i + 1) * WIDTH)
-        g = nn(mine_ref[side], left_ref[act]) + nn(other_ref[side], right_ref[act])
-        own_ref[:, cols] = g[:128]
-        for k in range(3):
-            sent[k][:, cols] = g[(k + 1) * 128 : (k + 2) * 128].astype(BF)
-
-
-def dkv_kernel(own_ref, a_ref, b_ref, out_ref):
-    out_ref[...] = (own_ref[...] + a_ref[...].astype(F32) + b_ref[...].astype(F32)).astype(BF)
-
-
 def early_kernel(mine_ref, other_ref, left_ref, right_ref, own_ref, rest_ref):
     for i, (side, act) in enumerate(((0, 1), (1, 0))):
         cols = slice(i * WIDTH, (i + 1) * WIDTH)
@@ -290,7 +273,7 @@
     x, listed, occupied, cot = tokens[0], neighbours[0], counts[0], cotangent[0]
     n = 16
     swap = [(i, i ^ 1) for i in range(n)]
-    cross = [(i, i if i in (0, n - 1) else i + 1 if i % 2 else i - 1) for i in range(n)]
+    cross = [(i, (i + 1) % n if i % 2 else (i - 1) % n) for i in range(n)]
 
     def pair_z(k):
         return [(i, i ^ (2 * k)) for i in range(n)]

time: 89.3 us -> 86.2 us (0.965)
  starting transfers between devices: 47.8 us -> 42.4 us
  waiting for transfers between devices: 24.7 us -> 27.1 us
    ppermute x9, starting transfers between devices: 10.2 us -> 17.1 us  [swapped(): return lax.ppermute(a, 'spatial', swap)]
    ppermute x3, starting transfers between devices: 6.87 us -> 2.77 us  [per_device(): lax.ppermute(to_z[m - 1], 'spatial', pair_z(m))]
    ppermute x1, starting transfers between devices: 3.9 us -> 0.01 us  [per_device(): from_far = lax.ppermute(grad_far, 'spatial', cross)]
    ppermute x3, waiting for transfers between devices: 3.22 us -> 5.18 us  [per_device(): lax.ppermute(to_z[m - 1], 'spatial', pair_z(m))]
    ppermute x1, starting transfers between devices: 5.07 us -> 3.11 us  [per_device(): far_kv = lax.ppermute(kv, 'spatial', cross)]
    ppermute x1, waiting for transfers between devices: 3.3 us -> 4.58 us  [per_device(): far_part = lax.ppermute(part, 'spatial', pair_z(4))]
    ppermute x1, starting transfers between devices: 3.81 us -> 2.63 us  [per_device(): far_part = lax.ppermute(part, 'spatial', pair_z(4))]
    ppermute x3, starting transfers between devices: 4.43 us -> 3.52 us  [per_device(): lax.ppermute(chunk, 'spatial', pair_z(m))]
  transfers between devices with their start and end apart: 27 -> 27, of which waited for: 11 -> 11; matrix products, arithmetic and copies ran while one was open for 1% -> 1% of each run, Pallas kernels for 11% -> 12%
where the time goes in v4:
time: 86.2 us; the launch traced here: 86.1 us
  starting transfers between devices  42.4 us (49%)
  waiting for transfers between devices  27.1 us (31%)
  Pallas kernels  14.9 us (17%)
  between operations  0.97 us (1%)
    ppermute x9, starting transfers between devices, swapped(): return lax.ppermute(a, 'spatial', swap)  17.1 us
    pallas_call x15, Pallas kernels, call(): pl.pallas_call(body, out_shape=outs, in_specs=(in_specs or [VMEM] * count...  14.9 us
    ppermute x3, waiting for transfers between devices, per_device(): from_y = [lax.ppermute(to_y[k - 1], 'dp', pair(k)) for k in (1, 3, 2)]  7.94 us
    ppermute x3, waiting for transfers between devices, per_device(): lax.ppermute(to_z[m - 1], 'spatial', pair_z(m))  5.18 us
    ppermute x3, waiting for transfers between devices, per_device(): lax.ppermute(chunk, 'spatial', pair_z(m))  4.94 us
    ppermute x1, waiting for transfers between devices, per_device(): far_part = lax.ppermute(part, 'spatial', pair_z(4))  4.58 us
    ppermute x3, starting transfers between devices, per_device(): from_y = [lax.ppermute(to_y[k - 1], 'dp', pair(k)) for k in (1, 3, 2)]  4.01 us
    ppermute x3, starting transfers between devices, per_device(): lax.ppermute(chunk, 'spatial', pair_z(m))  3.52 us
  transfers between devices with their start and end apart: 27, of which 11 were waited for; matrix products, arithmetic and copies ran while one was open for 1% of the time, Pallas kernels for 12%

profile of v4, /device:TPU:1, one launch (start us, length us, event | category | flops | bytes accessed | tf_op | source)
XLA Modules:
  0.0 86.1 jit_solution(17882963164620526585)
XLA Ops:
  0.6 2.1 %shard_map.93.refs_5_.refs_3_ = bf16[2,256,256]{2,1,0:T(8,128)(2,1)S(1)} custom-call(bf16[256,1024]{1,0:T(8,128)(2,1)} %bitcast.5, bf16[3,1024,256]{2,1,0:T(8,128)(2,1)} %refs_3_.3), custom_call_target="tpu_custom_call" | custom-call | flops 268435456 | bytes 2359296 | tf_op jit(solution)/shard_map/pallas_call | solution.py:32
  2.7 0.0 copy-start.2
  2.7 0.0 copy-start.3
  2.7 3.1 %collective-permute-start.1 = (bf16[2,256,256]{2,1,0:T(8,128)(2,1)S(1)}, bf16[2,256,256]{2,1,0:T(8,128)(2,1)S(1)}, u32[]{:S(2)}, u32[]{:S(2)}) collective-permute-start(bf16[2,256,256]{2,1,0:T(8,128)(2,1)S(1)} %shard_map.93.refs_5_.refs_3_), channel_id=1, source_target_pairs={{0,240},{16,32},{32,16},{48,64},{64,48},{80,96},{96,80},{112,128},... | collective-permute-start | bytes 786440 | tf_op jit(solution)/shard_map/ppermute | solution.py:324
  5.8 3.8 %collective-permute-start = (bf16[2,256,256]{2,1,0:T(8,128)(2,1)S(1)}, bf16[2,256,256]{2,1,0:T(8,128)(2,1)S(1)}, u32[]{:S(2)}, u32[]{:S(2)}) collective-permute-start(bf16[2,256,256]{2,1,0:T(8,128)(2,1)S(1)} %shard_map.93.refs_5_.refs_3_), channel_id=1, source_target_pairs={{0,16},{16,0},{32,48},{48,32},{64,80},{80,64},{96,112},{112,96},{1... | collective-permute-start | bytes 786440 | tf_op jit(solution)/shard_map/ppermute | solution.py:285
  9.6 0.7 pad_add_fusion.refs_4_
  10.3 3.5 %shard_map.94 = (bf16[256,256]{1,0:T(8,128)(2,1)S(1)}, bf16[256,256]{1,0:T(8,128)(2,1)S(1)}, bf16[2,512,256]{2,1,0:T(8,128)(2,1)}, f32[4,768]{1,0:T(4,128)S(1)}) custom-call(bf16[256,1024]{1,0:T(8,128)(2,1)} %bitcast.6, bf16[3,1024,256]{2,1,0:T(8,128)(2,1)} %refs_3_.3, bf16[256,1024]{1,0:T(8,128)(2,1)} %refs_2_.5, bf16[256,1024]{1,0:T(8,128)(2,1)} %bitcast.9, ...), custom_call_target="tpu_custom_call" | custom-call | flops 536870912 | bytes 3947008 | tf_op jit(solution)/shard_map/pallas_call | solution.py:32
  13.8 0.1 collective-permute-start.4
  13.9 0.0 collective-permute-done.1.refs_4_
  13.9 0.0 collective-permute-done.refs_2_
  13.9 3.4 %shard_map.95 = (bf16[2,256,256]{2,1,0:T(8,128)(2,1)S(1)}, bf16[2,256,256]{2,1,0:T(8,128)(2,1)S(1)}, f32[2,256,256]{2,1,0:T(8,128)S(1)}, bf16[2,256,256]{2,1,0:T(8,128)(2,1)S(1)}) custom-call(bf16[256,256]{1,0:T(8,128)(2,1)S(1)} %get-tuple-element.30.refs_0_, bf16[256,256]{1,0:T(8,128)(2,1)S(1)} %get-tuple-element.31.refs_1_, ...), custom_call_target="tpu_custom_call" | custom-call | flops 503316480 | bytes 2371584 | tf_op jit(solution)/shard_map/pallas_call | solution.py:32
  17.3 0.6 collective-permute-start.5
  17.9 0.0 collective-permute-start.2
  17.9 2.3 %collective-permute-start.3 = (bf16[2,256,256]{2,1,0:T(8,128)(2,1)S(1)}, bf16[2,256,256]{2,1,0:T(8,128)(2,1)S(1)}, u32[]{:S(2)}, u32[]{:S(2)}) collective-permute-start(bf16[2,256,256]{2,1,0:T(8,128)(2,1)S(1)} %get-tuple-element.36), channel_id=1, source_target_pairs={{0,16},{16,0},{32,48},{48,32},{64,80},{80,64},{96,112},{112,96},{1... | collective-permute-start | bytes 786440 | tf_op jit(solution)/shard_map/ppermute | solution.py:285
  20.2 0.7 shard_map.96.refs_0_
  21.0 0.0 copy-start
  21.0 0.0 copy-start.1
  21.0 0.0 collective-permute-done.5.refs_3_
  21.0 0.0 collective-permute-done.4.refs_1_
  21.0 0.4 shard_map.97
  21.4 2.5 %collective-permute-done.2.refs_1_ = bf16[2,256,256]{2,1,0:T(8,128)(2,1)S(1)} collective-permute-done((bf16[2,256,256]{2,1,0:T(8,128)(2,1)S(1)}, bf16[2,256,256]{2,1,0:T(8,128)(2,1)S(1)}, u32[]{:S(2)}, u32[]{:S(2)}) %collective-permute-start.2) | collective-permute-done | bytes 262176 | tf_op jit(solution)/shard_map/ppermute | solution.py:340
  24.0 0.0 collective-permute-done.3.refs_2_
  24.0 0.1 shard_map.98.refs_2_.refs_1_
  24.1 1.1 %collective-permute-start.6 = (bf16[2,256,256]{2,1,0:T(8,128)(2,1)S(1)}, bf16[2,256,256]{2,1,0:T(8,128)(2,1)S(1)}, u32[]{:S(2)}, u32[]{:S(2)}) collective-permute-start(bf16[2,256,256]{2,1,0:T(8,128)(2,1)S(1)} %shard_map.98.refs_2_.refs_1_), channel_id=1, source_target_pairs={{0,16},{16,0},{32,48},{48,32},{64,80},{80,64},{96,112},{112,96},{1... | collective-permute-start | bytes 786440 | tf_op jit(solution)/shard_map/ppermute | solution.py:285
  25.2 1.2 %collective-permute-done.6.refs_3_ = bf16[2,256,256]{2,1,0:T(8,128)(2,1)S(1)} collective-permute-done((bf16[2,256,256]{2,1,0:T(8,128)(2,1)S(1)}, bf16[2,256,256]{2,1,0:T(8,128)(2,1)S(1)}, u32[]{:S(2)}, u32[]{:S(2)}) %collective-permute-start.6) | collective-permute-done | bytes 262176 | tf_op jit(solution)/shard_map/ppermute | solution.py:285
  26.4 0.4 shard_map.99
  26.8 1.4 %collective-permute-start.9 = (bf16[128,1024]{1,0:T(8,128)(2,1)S(1)}, bf16[128,1024]{1,0:T(8,128)(2,1)S(1)}, u32[]{:S(2)}, u32[]{:S(2)}) collective-permute-start(bf16[128,1024]{1,0:T(8,128)(2,1)S(1)} %get-tuple-element.44), channel_id=1, source_target_pairs={{0,1},{1,0},{2,3},{3,2},{4,5},{5,4},{6,7},{7,6},{8,9},{9,8},{10,11... | collective-permute-start | bytes 786440 | tf_op jit(solution)/shard_map/ppermute | solution.py:369
  28.2 1.9 %collective-permute-start.10 = (bf16[128,1024]{1,0:T(8,128)(2,1)S(1)}, bf16[128,1024]{1,0:T(8,128)(2,1)S(1)}, u32[]{:S(2)}, u32[]{:S(2)}) collective-permute-start(bf16[128,1024]{1,0:T(8,128)(2,1)S(1)} %get-tuple-element.45), channel_id=1, source_target_pairs={{0,3},{1,2},{2,1},{3,0},{4,7},{5,6},{6,5},{7,4},{8,11},{9,10},{10,... | collective-permute-start | bytes 786440 | tf_op jit(solution)/shard_map/ppermute | solution.py:369
  30.1 0.7 collective-permute-start.11
  30.8 0.6 shard_map.100
  31.4 1.3 %collective-permute-start.7 = (bf16[2,256,256]{2,1,0:T(8,128)(2,1)S(1)}, bf16[2,256,256]{2,1,0:T(8,128)(2,1)S(1)}, u32[]{:S(2)}, u32[]{:S(2)}) collective-permute-start(bf16[2,256,256]{2,1,0:T(8,128)(2,1)S(1)} %get-tuple-element.42), channel_id=1, source_target_pairs={{0,4},{4,0},{8,12},{12,8},{1,5},{5,1},{9,13},{13,9},{2,6},{6,2},{1... | collective-permute-start | bytes 786440 | tf_op jit(solution)/shard_map/ppermute | solution.py:378
  32.7 1.8 %collective-permute-start.8 = (bf16[2,256,256]{2,1,0:T(8,128)(2,1)S(1)}, bf16[2,256,256]{2,1,0:T(8,128)(2,1)S(1)}, u32[]{:S(2)}, u32[]{:S(2)}) collective-permute-start(bf16[2,256,256]{2,1,0:T(8,128)(2,1)S(1)} %get-tuple-element.43), channel_id=1, source_target_pairs={{0,12},{4,8},{8,4},{12,0},{1,13},{5,9},{9,5},{13,1},{2,14},{6,10},... | collective-permute-start | bytes 786440 | tf_op jit(solution)/shard_map/ppermute | solution.py:378
  34.6 0.0 collective-permute-done.9.refs_1_
  34.6 6.0 %collective-permute-done.10.refs_2_ = bf16[128,1024]{1,0:T(8,128)(2,1)S(1)} collective-permute-done((bf16[128,1024]{1,0:T(8,128)(2,1)S(1)}, bf16[128,1024]{1,0:T(8,128)(2,1)S(1)}, u32[]{:S(2)}, u32[]{:S(2)}) %collective-permute-start.10) | collective-permute-done | bytes 262176 | tf_op jit(solution)/shard_map/ppermute | solution.py:369
  40.6 1.9 %collective-permute-done.11.refs_3_ = bf16[128,1024]{1,0:T(8,128)(2,1)S(1)} collective-permute-done((bf16[128,1024]{1,0:T(8,128)(2,1)S(1)}, bf16[128,1024]{1,0:T(8,128)(2,1)S(1)}, u32[]{:S(2)}, u32[]{:S(2)}) %collective-permute-start.11) | collective-permute-done | bytes 262176 | tf_op jit(solution)/shard_map/ppermute | solution.py:369
  42.5 0.1 shard_map.101
  42.6 0.1 collective-permute-start.12
  42.7 2.5 %collective-permute-start.13 = (bf16[32,1024]{1,0:T(8,128)(2,1)S(1)}, bf16[32,1024]{1,0:T(8,128)(2,1)S(1)}, u32[]{:S(2)}, u32[]{:S(2)}) collective-permute-start(bf16[32,1024]{1,0:T(8,128)(2,1)S(1)} %get-tuple-element.49), channel_id=1, source_target_pairs={{0,96},{16,112},{32,64},{48,80},{64,32},{80,48},{96,0},{112,16},{1... | collective-permute-start | bytes 196616 | tf_op jit(solution)/shard_map/ppermute | solution.py:386
  45.2 0.2 collective-permute-start.14
  45.4 4.7 %collective-permute-done.12.refs_1_ = bf16[32,1024]{1,0:T(8,128)(2,1)S(1)} collective-permute-done((bf16[32,1024]{1,0:T(8,128)(2,1)S(1)}, bf16[32,1024]{1,0:T(8,128)(2,1)S(1)}, u32[]{:S(2)}, u32[]{:S(2)}) %collective-permute-start.12) | collective-permute-done | bytes 65568 | tf_op jit(solution)/shard_map/ppermute | solution.py:386
  50.1 0.0 collective-permute-done.13.refs_2_
  50.1 0.5 collective-permute-done.14.refs_3_
  50.6 2.6 %collective-permute-start.15 = (bf16[32,1024]{1,0:T(8,128)(2,1)S(1)}, bf16[32,1024]{1,0:T(8,128)(2,1)S(1)}, u32[]{:S(2)}, u32[]{:S(2)}) collective-permute-start(bf16[32,1024]{1,0:T(8,128)(2,1)S(1)} %shard_map.102.refs_0_), channel_id=1, source_target_pairs={{0,128},{16,144},{32,160},{48,176},{64,192},{80,208},{96,224},{112... | collective-permute-start | bytes 196616 | tf_op jit(solution)/shard_map/ppermute | solution.py:388
  53.2 4.6 %collective-permute-done.15.refs_1_ = bf16[32,1024]{1,0:T(8,128)(2,1)S(1)} collective-permute-done((bf16[32,1024]{1,0:T(8,128)(2,1)S(1)}, bf16[32,1024]{1,0:T(8,128)(2,1)S(1)}, u32[]{:S(2)}, u32[]{:S(2)}) %collective-permute-start.15) | collective-permute-done | bytes 65568 | tf_op jit(solution)/shard_map/ppermute | solution.py:388
  57.8 3.1 %collective-permute-start.18 = (bf16[32,1024]{1,0:T(8,128)(2,1)S(1)}, bf16[32,1024]{1,0:T(8,128)(2,1)S(1)}, u32[]{:S(2)}, u32[]{:S(2)}) collective-permute-start(bf16[32,1024]{1,0:T(8,128)(2,1)S(1)} %shard_map.103.refs_0_), channel_id=1, source_target_pairs={{0,64},{16,80},{32,96},{48,112},{64,0},{80,16},{96,32},{112,48},{1... | collective-permute-start | bytes 196616 | tf_op jit(solution)/shard_map/ppermute | solution.py:390
  60.9 0.4 collective-permute-start.17
  61.4 0.0 collective-permute-start.16
  61.4 0.0 collective-permute-done.8.refs_5_.refs_2_
  61.4 1.9 %collective-permute-done.18.refs_3_ = bf16[32,1024]{1,0:T(8,128)(2,1)S(1)} collective-permute-done((bf16[32,1024]{1,0:T(8,128)(2,1)S(1)}, bf16[32,1024]{1,0:T(8,128)(2,1)S(1)}, u32[]{:S(2)}, u32[]{:S(2)}) %collective-permute-start.18) | collective-permute-done | bytes 65568 | tf_op jit(solution)/shard_map/ppermute | solution.py:390
  63.3 3.0 %collective-permute-done.17.refs_2_ = bf16[32,1024]{1,0:T(8,128)(2,1)S(1)} collective-permute-done((bf16[32,1024]{1,0:T(8,128)(2,1)S(1)}, bf16[32,1024]{1,0:T(8,128)(2,1)S(1)}, u32[]{:S(2)}, u32[]{:S(2)}) %collective-permute-start.17) | collective-permute-done | bytes 65568 | tf_op jit(solution)/shard_map/ppermute | solution.py:390
  66.3 0.1 collective-permute-start.22
  66.4 0.9 %collective-permute-start.21 = (bf16[128,1024]{1,0:T(8,128)(2,1)S(1)}, bf16[128,1024]{1,0:T(8,128)(2,1)S(1)}, u32[]{:S(2)}, u32[]{:S(2)}) collective-permute-start(bf16[128,1024]{1,0:T(8,128)(2,1)S(1)} %shard_map.104.refs_4_.refs_0_), channel_id=1, source_target_pairs={{0,3},{1,2},{2,1},{3,0},{4,7},{5,6},{6,5},{7,4},{8,11},{9,10},{10,... | collective-permute-start | bytes 786440 | tf_op jit(solution)/shard_map/ppermute | solution.py:398
  67.3 2.3 %collective-permute-start.20 = (bf16[128,1024]{1,0:T(8,128)(2,1)S(1)}, bf16[128,1024]{1,0:T(8,128)(2,1)S(1)}, u32[]{:S(2)}, u32[]{:S(2)}) collective-permute-start(bf16[128,1024]{1,0:T(8,128)(2,1)S(1)} %shard_map.104.refs_4_.refs_0_), channel_id=1, source_target_pairs={{0,2},{1,3},{2,0},{3,1},{4,6},{5,7},{6,4},{7,5},{8,10},{9,11},{10,... | collective-permute-start | bytes 786440 | tf_op jit(solution)/shard_map/ppermute | solution.py:398
  69.7 0.3 shard_map.105
  70.0 2.8 %collective-permute-start.19 = (bf16[2,256,256]{2,1,0:T(8,128)(2,1)S(1)}, bf16[2,256,256]{2,1,0:T(8,128)(2,1)S(1)}, u32[]{:S(2)}, u32[]{:S(2)}) collective-permute-start(bf16[2,256,256]{2,1,0:T(8,128)(2,1)S(1)} %shard_map.105), channel_id=1, source_target_pairs={{0,8},{4,12},{8,0},{12,4},{1,9},{5,13},{9,1},{13,5},{2,10},{6,14},... | collective-permute-start | bytes 786440 | tf_op jit(solution)/shard_map/ppermute | solution.py:406
  72.8 3.7 %collective-permute-start.23 = (bf16[128,1024]{1,0:T(8,128)(2,1)S(1)}, bf16[128,1024]{1,0:T(8,128)(2,1)S(1)}, u32[]{:S(2)}, u32[]{:S(2)}) collective-permute-start(bf16[128,1024]{1,0:T(8,128)(2,1)S(1)} %shard_map.104.refs_4_.refs_0_), channel_id=1, source_target_pairs={{0,16},{16,0},{32,48},{48,32},{64,80},{80,64},{96,112},{112,96},{1... | collective-permute-start | bytes 786440 | tf_op jit(solution)/shard_map/ppermute | solution.py:285
  76.6 1.4 %collective-permute-start.26 = (bf16[128,1024]{1,0:T(8,128)(2,1)S(1)}, bf16[128,1024]{1,0:T(8,128)(2,1)S(1)}, u32[]{:S(2)}, u32[]{:S(2)}) collective-permute-start(bf16[128,1024]{1,0:T(8,128)(2,1)S(1)} %collective-permute-done.22.refs_3_), channel_id=1, source_target_pairs={{0,16},{16,0},{32,48},{48,32},{64,80},{80,64},{96,112},{112,96},{1... | collective-permute-start | bytes 786440 | tf_op jit(solution)/shard_map/ppermute | solution.py:285
  78.0 4.1 %collective-permute-start.25 = (bf16[128,1024]{1,0:T(8,128)(2,1)S(1)}, bf16[128,1024]{1,0:T(8,128)(2,1)S(1)}, u32[]{:S(2)}, u32[]{:S(2)}) collective-permute-start(bf16[128,1024]{1,0:T(8,128)(2,1)S(1)} %collective-permute-done.21.refs_2_), channel_id=1, source_target_pairs={{0,16},{16,0},{32,48},{48,32},{64,80},{80,64},{96,112},{112,96},{1... | collective-permute-start | bytes 786440 | tf_op jit(solution)/shard_map/ppermute | solution.py:285
  82.1 0.0 collective-permute-start.24
  82.1 0.8 shard_map.106
  82.9 0.0 collective-permute-done.23.refs_4_
  82.9 0.3 collective-permute-done.25.refs_6_
  83.2 0.4 collective-permute-done.24.refs_5_
  83.6 2.3 %shard_map.107 = (f32[3,1024,256]{2,1,0:T(8,128)}, f32[256,1024]{1,0:T(8,128)}) custom-call(bf16[128,1024]{1,0:T(8,128)(2,1)S(1)} %shard_map.104.refs_4_.refs_0_, bf16[128,1024]{1,0:T(8,128)(2,1)S(1)} %collective-permute-done.20.refs_1_, bf16[128,1024]{1,0:T(8,128)(2,1)S(1)} %collective-permute-done.21.refs_2_, ...), custom_call_target="tpu_custom_call" | custom-call | flops 1048576 | bytes 6291456 | tf_op jit(solution)/shard_map/pallas_call | solution.py:32
  (14 shorter events, 0.1 us)
Async XLA Ops:
  2.7 17.5 %copy-start.2 = (bf16[1,256,1024]{2,1,0:T(8,128)(2,1)S(1)}, bf16[1,256,1024]{2,1,0:T(8,128)(2,1)}, u32[]{:S(2)}) copy-start(bf16[1,256,1024]{2,1,0:T(8,128)(2,1)} %param.6) | copy-start | bytes 1572868
  2.7 17.5 %copy-start.3 = (bf16[1,256,1024]{2,1,0:T(8,128)(2,1)S(1)}, bf16[1,256,1024]{2,1,0:T(8,128)(2,1)}, u32[]{:S(2)}) copy-start(bf16[1,256,1024]{2,1,0:T(8,128)(2,1)} %param.11) | copy-start | bytes 1572868
  2.7 11.2 %collective-permute-start.1 = (bf16[2,256,256]{2,1,0:T(8,128)(2,1)S(1)}, bf16[2,256,256]{2,1,0:T(8,128)(2,1)S(1)}, u32[]{:S(2)}, u32[]{:S(2)}) collective-permute-start(bf16[2,256,256]{2,1,0:T(8,128)(2,1)S(1)} %shard_map.93.refs_5_.refs_3_), channel_id=1, source_target_pairs={{0,240},{16,32},{32,16},{48,64},{64,48},{80,96},{96,80},{112,128},... | collective-permute-start | bytes 786440 | tf_op jit(solution)/shard_map/ppermute | solution.py:324
  5.8 8.1 %collective-permute-start = (bf16[2,256,256]{2,1,0:T(8,128)(2,1)S(1)}, bf16[2,256,256]{2,1,0:T(8,128)(2,1)S(1)}, u32[]{:S(2)}, u32[]{:S(2)}) collective-permute-start(bf16[2,256,256]{2,1,0:T(8,128)(2,1)S(1)} %shard_map.93.refs_5_.refs_3_), channel_id=1, source_target_pairs={{0,16},{16,0},{32,48},{48,32},{64,80},{80,64},{96,112},{112,96},{1... | collective-permute-start | bytes 786440 | tf_op jit(solution)/shard_map/ppermute | solution.py:285
  13.8 7.2 %collective-permute-start.4 = (bf16[2,512,256]{2,1,0:T(8,128)(2,1)}, bf16[2,512,256]{2,1,0:T(8,128)(2,1)S(1)}, u32[]{:S(2)}, u32[]{:S(2)}) collective-permute-start(bf16[2,512,256]{2,1,0:T(8,128)(2,1)} %get-tuple-element.37), channel_id=1, source_target_pairs={{0,16},{16,0},{32,48},{48,32},{64,80},{80,64},{96,112},{112,96},{1... | collective-permute-start | bytes 1572872 | tf_op jit(solution)/shard_map/ppermute | solution.py:285
  17.3 3.7 %collective-permute-start.5 = (bf16[2,256,256]{2,1,0:T(8,128)(2,1)S(1)}, bf16[2,256,256]{2,1,0:T(8,128)(2,1)S(1)}, u32[]{:S(2)}, u32[]{:S(2)}) collective-permute-start(bf16[2,256,256]{2,1,0:T(8,128)(2,1)S(1)} %get-tuple-element.33.refs_2_.refs_0_), channel_id=1, source_target_pairs={{0,16},{16,0},{32,48},{48,32},{64,80},{80,64},{96,112},{112,96},{1... | collective-permute-start | bytes 786440 | tf_op jit(solution)/shard_map/ppermute | solution.py:285
  17.9 6.1 %collective-permute-start.2 = (bf16[2,256,256]{2,1,0:T(8,128)(2,1)S(1)}, bf16[2,256,256]{2,1,0:T(8,128)(2,1)S(1)}, u32[]{:S(2)}, u32[]{:S(2)}) collective-permute-start(bf16[2,256,256]{2,1,0:T(8,128)(2,1)S(1)} %get-tuple-element.35), channel_id=1, source_target_pairs={{0,240},{16,32},{32,16},{48,64},{64,48},{80,96},{96,80},{112,128},... | collective-permute-start | bytes 786440 | tf_op jit(solution)/shard_map/ppermute | solution.py:340
  17.9 6.1 %collective-permute-start.3 = (bf16[2,256,256]{2,1,0:T(8,128)(2,1)S(1)}, bf16[2,256,256]{2,1,0:T(8,128)(2,1)S(1)}, u32[]{:S(2)}, u32[]{:S(2)}) collective-permute-start(bf16[2,256,256]{2,1,0:T(8,128)(2,1)S(1)} %get-tuple-element.36), channel_id=1, source_target_pairs={{0,16},{16,0},{32,48},{48,32},{64,80},{80,64},{96,112},{112,96},{1... | collective-permute-start | bytes 786440 | tf_op jit(solution)/shard_map/ppermute | solution.py:285
  21.0 9.9 %copy-start = (bf16[3,1024,256]{2,1,0:T(8,128)(2,1)S(1)}, bf16[3,1024,256]{2,1,0:T(8,128)(2,1)}, u32[]{:S(2)}) copy-start(bf16[3,1024,256]{2,1,0:T(8,128)(2,1)} %refs_3_.3) | copy-start | bytes 4718596
  21.0 9.9 %copy-start.1 = (bf16[256,1024]{1,0:T(8,128)(2,1)S(1)}, bf16[256,1024]{1,0:T(8,128)(2,1)}, u32[]{:S(2)}) copy-start(bf16[256,1024]{1,0:T(8,128)(2,1)} %refs_2_.5) | copy-start | bytes 1572868
  24.1 2.3 %collective-permute-start.6 = (bf16[2,256,256]{2,1,0:T(8,128)(2,1)S(1)}, bf16[2,256,256]{2,1,0:T(8,128)(2,1)S(1)}, u32[]{:S(2)}, u32[]{:S(2)}) collective-permute-start(bf16[2,256,256]{2,1,0:T(8,128)(2,1)S(1)} %shard_map.98.refs_2_.refs_1_), channel_id=1, source_target_pairs={{0,16},{16,0},{32,48},{48,32},{64,80},{80,64},{96,112},{112,96},{1... | collective-permute-start | bytes 786440 | tf_op jit(solution)/shard_map/ppermute | solution.py:285
  26.8 7.7 %collective-permute-start.9 = (bf16[128,1024]{1,0:T(8,128)(2,1)S(1)}, bf16[128,1024]{1,0:T(8,128)(2,1)S(1)}, u32[]{:S(2)}, u32[]{:S(2)}) collective-permute-start(bf16[128,1024]{1,0:T(8,128)(2,1)S(1)} %get-tuple-element.44), channel_id=1, source_target_pairs={{0,1},{1,0},{2,3},{3,2},{4,5},{5,4},{6,7},{7,6},{8,9},{9,8},{10,11... | collective-permute-start | bytes 786440 | tf_op jit(solution)/shard_map/ppermute | solution.py:369
  28.2 12.4 %collective-permute-start.10 = (bf16[128,1024]{1,0:T(8,128)(2,1)S(1)}, bf16[128,1024]{1,0:T(8,128)(2,1)S(1)}, u32[]{:S(2)}, u32[]{:S(2)}) collective-permute-start(bf16[128,1024]{1,0:T(8,128)(2,1)S(1)} %get-tuple-element.45), channel_id=1, source_target_pairs={{0,3},{1,2},{2,1},{3,0},{4,7},{5,6},{6,5},{7,4},{8,11},{9,10},{10,... | collective-permute-start | bytes 786440 | tf_op jit(solution)/shard_map/ppermute | solution.py:369
  30.1 12.4 %collective-permute-start.11 = (bf16[128,1024]{1,0:T(8,128)(2,1)S(1)}, bf16[128,1024]{1,0:T(8,128)(2,1)S(1)}, u32[]{:S(2)}, u32[]{:S(2)}) collective-permute-start(bf16[128,1024]{1,0:T(8,128)(2,1)S(1)} %get-tuple-element.46), channel_id=1, source_target_pairs={{0,2},{1,3},{2,0},{3,1},{4,6},{5,7},{6,4},{7,5},{8,10},{9,11},{10,... | collective-permute-start | bytes 786440 | tf_op jit(solution)/shard_map/ppermute | solution.py:369
  31.4 29.9 %collective-permute-start.7 = (bf16[2,256,256]{2,1,0:T(8,128)(2,1)S(1)}, bf16[2,256,256]{2,1,0:T(8,128)(2,1)S(1)}, u32[]{:S(2)}, u32[]{:S(2)}) collective-permute-start(bf16[2,256,256]{2,1,0:T(8,128)(2,1)S(1)} %get-tuple-element.42), channel_id=1, source_target_pairs={{0,4},{4,0},{8,12},{12,8},{1,5},{5,1},{9,13},{13,9},{2,6},{6,2},{1... | collective-permute-start | bytes 786440 | tf_op jit(solution)/shard_map/ppermute | solution.py:378
  32.7 28.6 %collective-permute-start.8 = (bf16[2,256,256]{2,1,0:T(8,128)(2,1)S(1)}, bf16[2,256,256]{2,1,0:T(8,128)(2,1)S(1)}, u32[]{:S(2)}, u32[]{:S(2)}) collective-permute-start(bf16[2,256,256]{2,1,0:T(8,128)(2,1)S(1)} %get-tuple-element.43), channel_id=1, source_target_pairs={{0,12},{4,8},{8,4},{12,0},{1,13},{5,9},{9,5},{13,1},{2,14},{6,10},... | collective-permute-start | bytes 786440 | tf_op jit(solution)/shard_map/ppermute | solution.py:378
  42.6 7.5 %collective-permute-start.12 = (bf16[32,1024]{1,0:T(8,128)(2,1)S(1)}, bf16[32,1024]{1,0:T(8,128)(2,1)S(1)}, u32[]{:S(2)}, u32[]{:S(2)}) collective-permute-start(bf16[32,1024]{1,0:T(8,128)(2,1)S(1)} %get-tuple-element.48), channel_id=1, source_target_pairs={{0,64},{16,80},{32,96},{48,112},{64,0},{80,16},{96,32},{112,48},{1... | collective-permute-start | bytes 196616 | tf_op jit(solution)/shard_map/ppermute | solution.py:386
  42.7 7.4 %collective-permute-start.13 = (bf16[32,1024]{1,0:T(8,128)(2,1)S(1)}, bf16[32,1024]{1,0:T(8,128)(2,1)S(1)}, u32[]{:S(2)}, u32[]{:S(2)}) collective-permute-start(bf16[32,1024]{1,0:T(8,128)(2,1)S(1)} %get-tuple-element.49), channel_id=1, source_target_pairs={{0,96},{16,112},{32,64},{48,80},{64,32},{80,48},{96,0},{112,16},{1... | collective-permute-start | bytes 196616 | tf_op jit(solution)/shard_map/ppermute | solution.py:386
  45.2 5.4 %collective-permute-start.14 = (bf16[32,1024]{1,0:T(8,128)(2,1)S(1)}, bf16[32,1024]{1,0:T(8,128)(2,1)S(1)}, u32[]{:S(2)}, u32[]{:S(2)}) collective-permute-start(bf16[32,1024]{1,0:T(8,128)(2,1)S(1)} %get-tuple-element.50), channel_id=1, source_target_pairs={{0,32},{16,48},{32,0},{48,16},{64,96},{80,112},{96,64},{112,80},{1... | collective-permute-start | bytes 196616 | tf_op jit(solution)/shard_map/ppermute | solution.py:386
  50.6 7.2 %collective-permute-start.15 = (bf16[32,1024]{1,0:T(8,128)(2,1)S(1)}, bf16[32,1024]{1,0:T(8,128)(2,1)S(1)}, u32[]{:S(2)}, u32[]{:S(2)}) collective-permute-start(bf16[32,1024]{1,0:T(8,128)(2,1)S(1)} %shard_map.102.refs_0_), channel_id=1, source_target_pairs={{0,128},{16,144},{32,160},{48,176},{64,192},{80,208},{96,224},{112... | collective-permute-start | bytes 196616 | tf_op jit(solution)/shard_map/ppermute | solution.py:388
  57.8 5.5 %collective-permute-start.18 = (bf16[32,1024]{1,0:T(8,128)(2,1)S(1)}, bf16[32,1024]{1,0:T(8,128)(2,1)S(1)}, u32[]{:S(2)}, u32[]{:S(2)}) collective-permute-start(bf16[32,1024]{1,0:T(8,128)(2,1)S(1)} %shard_map.103.refs_0_), channel_id=1, source_target_pairs={{0,64},{16,80},{32,96},{48,112},{64,0},{80,16},{96,32},{112,48},{1... | collective-permute-start | bytes 196616 | tf_op jit(solution)/shard_map/ppermute | solution.py:390
  60.9 5.4 %collective-permute-start.17 = (bf16[32,1024]{1,0:T(8,128)(2,1)S(1)}, bf16[32,1024]{1,0:T(8,128)(2,1)S(1)}, u32[]{:S(2)}, u32[]{:S(2)}) collective-permute-start(bf16[32,1024]{1,0:T(8,128)(2,1)S(1)} %shard_map.103.refs_0_), channel_id=1, source_target_pairs={{0,96},{16,112},{32,64},{48,80},{64,32},{80,48},{96,0},{112,16},{1... | collective-permute-start | bytes 196616 | tf_op jit(solution)/shard_map/ppermute | solution.py:390
  61.4 5.0 %collective-permute-start.16 = (bf16[32,1024]{1,0:T(8,128)(2,1)S(1)}, bf16[32,1024]{1,0:T(8,128)(2,1)S(1)}, u32[]{:S(2)}, u32[]{:S(2)}) collective-permute-start(bf16[32,1024]{1,0:T(8,128)(2,1)S(1)} %shard_map.103.refs_0_), channel_id=1, source_target_pairs={{0,32},{16,48},{32,0},{48,16},{64,96},{80,112},{96,64},{112,80},{1... | collective-permute-start | bytes 196616 | tf_op jit(solution)/shard_map/ppermute | solution.py:390
  66.3 10.2 %collective-permute-start.22 = (bf16[128,1024]{1,0:T(8,128)(2,1)S(1)}, bf16[128,1024]{1,0:T(8,128)(2,1)S(1)}, u32[]{:S(2)}, u32[]{:S(2)}) collective-permute-start(bf16[128,1024]{1,0:T(8,128)(2,1)S(1)} %shard_map.104.refs_4_.refs_0_), channel_id=1, source_target_pairs={{0,1},{1,0},{2,3},{3,2},{4,5},{5,4},{6,7},{7,6},{8,9},{9,8},{10,11... | collective-permute-start | bytes 786440 | tf_op jit(solution)/shard_map/ppermute | solution.py:398
  66.4 11.5 %collective-permute-start.21 = (bf16[128,1024]{1,0:T(8,128)(2,1)S(1)}, bf16[128,1024]{1,0:T(8,128)(2,1)S(1)}, u32[]{:S(2)}, u32[]{:S(2)}) collective-permute-start(bf16[128,1024]{1,0:T(8,128)(2,1)S(1)} %shard_map.104.refs_4_.refs_0_), channel_id=1, source_target_pairs={{0,3},{1,2},{2,1},{3,0},{4,7},{5,6},{6,5},{7,4},{8,11},{9,10},{10,... | collective-permute-start | bytes 786440 | tf_op jit(solution)/shard_map/ppermute | solution.py:398
  67.3 14.7 %collective-permute-start.20 = (bf16[128,1024]{1,0:T(8,128)(2,1)S(1)}, bf16[128,1024]{1,0:T(8,128)(2,1)S(1)}, u32[]{:S(2)}, u32[]{:S(2)}) collective-permute-start(bf16[128,1024]{1,0:T(8,128)(2,1)S(1)} %shard_map.104.refs_4_.refs_0_), channel_id=1, source_target_pairs={{0,2},{1,3},{2,0},{3,1},{4,6},{5,7},{6,4},{7,5},{8,10},{9,11},{10,... | collective-permute-start | bytes 786440 | tf_op jit(solution)/shard_map/ppermute | solution.py:398
  70.0 12.1 %collective-permute-start.19 = (bf16[2,256,256]{2,1,0:T(8,128)(2,1)S(1)}, bf16[2,256,256]{2,1,0:T(8,128)(2,1)S(1)}, u32[]{:S(2)}, u32[]{:S(2)}) collective-permute-start(bf16[2,256,256]{2,1,0:T(8,128)(2,1)S(1)} %shard_map.105), channel_id=1, source_target_pairs={{0,8},{4,12},{8,0},{12,4},{1,9},{5,13},{9,1},{13,5},{2,10},{6,14},... | collective-permute-start | bytes 786440 | tf_op jit(solution)/shard_map/ppermute | solution.py:406
  72.8 10.1 %collective-permute-start.23 = (bf16[128,1024]{1,0:T(8,128)(2,1)S(1)}, bf16[128,1024]{1,0:T(8,128)(2,1)S(1)}, u32[]{:S(2)}, u32[]{:S(2)}) collective-permute-start(bf16[128,1024]{1,0:T(8,128)(2,1)S(1)} %shard_map.104.refs_4_.refs_0_), channel_id=1, source_target_pairs={{0,16},{16,0},{32,48},{48,32},{64,80},{80,64},{96,112},{112,96},{1... | collective-permute-start | bytes 786440 | tf_op jit(solution)/shard_map/ppermute | solution.py:285
  76.6 6.3 %collective-permute-start.26 = (bf16[128,1024]{1,0:T(8,128)(2,1)S(1)}, bf16[128,1024]{1,0:T(8,128)(2,1)S(1)}, u32[]{:S(2)}, u32[]{:S(2)}) collective-permute-start(bf16[128,1024]{1,0:T(8,128)(2,1)S(1)} %collective-permute-done.22.refs_3_), channel_id=1, source_target_pairs={{0,16},{16,0},{32,48},{48,32},{64,80},{80,64},{96,112},{112,96},{1... | collective-permute-start | bytes 786440 | tf_op jit(solution)/shard_map/ppermute | solution.py:285
  78.0 5.3 %collective-permute-start.25 = (bf16[128,1024]{1,0:T(8,128)(2,1)S(1)}, bf16[128,1024]{1,0:T(8,128)(2,1)S(1)}, u32[]{:S(2)}, u32[]{:S(2)}) collective-permute-start(bf16[128,1024]{1,0:T(8,128)(2,1)S(1)} %collective-permute-done.21.refs_2_), channel_id=1, source_target_pairs={{0,16},{16,0},{32,48},{48,32},{64,80},{80,64},{96,112},{112,96},{1... | collective-permute-start | bytes 786440 | tf_op jit(solution)/shard_map/ppermute | solution.py:285
  82.1 1.5 %collective-permute-start.24 = (bf16[128,1024]{1,0:T(8,128)(2,1)S(1)}, bf16[128,1024]{1,0:T(8,128)(2,1)S(1)}, u32[]{:S(2)}, u32[]{:S(2)}) collective-permute-start(bf16[128,1024]{1,0:T(8,128)(2,1)S(1)} %collective-permute-done.20.refs_1_), channel_id=1, source_target_pairs={{0,16},{16,0},{32,48},{48,32},{64,80},{80,64},{96,112},{112,96},{1... | collective-permute-start | bytes 786440 | tf_op jit(solution)/shard_map/ppermute | solution.py:285

commit v5 on v4

--- a/solution.py
+++ b/solution.py
@@ -52,10 +52,6 @@
     return lax.dot_general(a, b, (((1,), (1,)), ((), ())), preferred_element_type=F32)
 
 
-def tn(a, b):
-    return lax.dot_general(a, b, (((0,), (0,)), ((), ())), preferred_element_type=F32)
-
-
 def place_of():
     spatial = lax.axis_index("spatial")
     return spatial >> 1, spatial & 1, lax.axis_index("dp"), lax.axis_index("head")
@@ -129,10 +125,10 @@
     pick_rows(place_of()[1], x_ref, cot_ref, xc_ref)
 
 
-def attention_kernel(q_ref, u_ref, mate_ref, own_ref, far_ref, bias_ref, acts_ref, gf_ref, go_ref, gm_ref):
+def attention_kernel(q_ref, u_ref, mate_ref, own_ref, far_ref, bias_ref, acts_ref, gf_ref, go_ref):
     factor = HD**-0.5
     window = (far_ref, own_ref, mate_ref)
-    grads = (gf_ref, go_ref, gm_ref)
+    grads = (gf_ref, go_ref, acts_ref.at[2:4])
     lane = lax.broadcasted_iota(jnp.int32, (1, 128), 1)
     picks = [(lane < HD).astype(F32).astype(BF), (lane >= HD).astype(F32).astype(BF)]
     first = lax.broadcasted_iota(jnp.int32, (ROWS, 128), 1) < HD
@@ -149,11 +145,13 @@
     for pair in range(WIDTH // 128):
         cols = slice(pair * 128, (pair + 1) * 128)
         q2, u2 = q_ref[:, cols], u_ref[:, cols]
+        q_turned, u_turned = q2.T, u2.T
         keys = [w[0, :, cols] for w in window]
         values = [w[1, :, cols] for w in window]
-        key_sum, value_sum = [None] * 3, [None] * 3
+        key_parts, value_parts = [[], [], []], [[], [], []]
         att, dq = [], []
-        for pick in picks:
+        for h, pick in enumerate(picks):
+            rows = slice(h * HD, (h + 1) * HD)
             qm, um = q2 * pick, u2 * pick
             weights = [jnp.exp2(nt(qm, keys[c]) * (factor * LOG2E) + bias[c]) for c in range(3)]
             total = sum(jnp.sum(w, axis=1, keepdims=True) for w in weights)
@@ -166,14 +164,13 @@
             att.append(sum(nn(low[c], values[c]) for c in range(3)))
             dq.append(sum(nn(dscore[c], keys[c]) for c in range(3)))
             for c in range(3):
-                dk, dv = tn(dscore[c], qm), tn(low[c], um)
-                key_sum[c] = dk if key_sum[c] is None else key_sum[c] + dk
-                value_sum[c] = dv if value_sum[c] is None else value_sum[c] + dv
+                key_parts[c].append(nn(q_turned[rows], dscore[c]))
+                value_parts[c].append(nn(u_turned[rows], low[c]))
         acts_ref[0, :, cols] = jnp.where(first, att[0], att[1]).astype(BF)
         acts_ref[1, :, cols] = jnp.where(first, dq[0], dq[1]).astype(BF)
         for c in range(3):
-            grads[c][0, :, cols] = key_sum[c].astype(grads[c].dtype)
-            grads[c][1, :, cols] = value_sum[c].astype(grads[c].dtype)
+            grads[c][0, :, cols] = jnp.concatenate(key_parts[c], axis=0).T.astype(grads[c].dtype)
+            grads[c][1, :, cols] = jnp.concatenate(value_parts[c], axis=0).T.astype(grads[c].dtype)
 
 
 def head_kernel(acts_ref, dkv_ref, wo_ref, w_ref, *outs, parts):
@@ -197,7 +194,7 @@
 
 
 def dkv_kernel(own_ref, a_ref, b_ref, out_ref):
-    out_ref[...] = (own_ref[...] + a_ref[...].astype(F32) + b_ref[...].astype(F32)).astype(BF)
+    out_ref[...] = (own_ref[...] + a_ref[...].astype(F32) + b_ref[2:4].astype(F32)).astype(BF)
 
 
 def early_kernel(mine_ref, other_ref, left_ref, right_ref, own_ref, rest_ref):
@@ -325,20 +322,18 @@
 
     xc_other = swapped(xc_sent)
 
-    acts, grad_far, grad_own, grad_mate = call(
+    acts, grad_far, grad_own = call(
         attention_kernel,
         [
-            shape((2, ROWS, WIDTH), BF),
+            shape((4, ROWS, WIDTH), BF),
             shape((2, ROWS, WIDTH), BF),
             shape((2, ROWS, WIDTH), F32),
-            shape((2, ROWS, WIDTH), BF),
         ],
         [q, u, mate_kv, kv, far_kv, bias],
         10 * 256 * 768 * 256,
         vmem=32,
     )
     from_far = lax.ppermute(grad_far, "spatial", cross)
-    from_mate = swapped(grad_mate)
     acts_other = swapped(acts)
     xc_mine = call(
         mine_kernel,
@@ -356,7 +351,7 @@
     dkv = call(
         dkv_kernel,
         [shape((2, ROWS, WIDTH), BF)],
-        [grad_own, from_far, from_mate],
+        [grad_own, from_far, acts_other],
         2**18,
         after=[early[0]],
     )[0]

time: 86.2 us -> 85.9 us (level)
  starting transfers between devices: 42.4 us -> 40.3 us
  waiting for transfers between devices: 27.1 us -> 29.2 us
    ppermute x9 -> x8, starting transfers between devices: 17.1 us -> 14.8 us  [swapped(): return lax.ppermute(a, 'spatial', swap)]
    ppermute x1, waiting for transfers between devices: 2.54 us -> 4.11 us  [per_device(): from_far = lax.ppermute(grad_far, 'spatial', cross)]
    ppermute x9 -> x8, waiting for transfers between devices: 1.89 us -> 2.63 us  [swapped(): return lax.ppermute(a, 'spatial', swap)]
  transfers between devices with their start and end apart: 27 -> 26, of which waited for: 11 -> 12; matrix products, arithmetic and copies ran while one was open for 1% -> 1% of each run, Pallas kernels for 12% -> 11%
where the time goes in v5:
time: 85.9 us; the launch traced here: 85.8 us
  starting transfers between devices  40.3 us (47%)
  waiting for transfers between devices  29.2 us (34%)
  Pallas kernels  14.6 us (17%)
  between operations  0.97 us (1%)
    ppermute x8, starting transfers between devices, swapped(): return lax.ppermute(a, 'spatial', swap)  14.8 us
    pallas_call x15, Pallas kernels, call(): pl.pallas_call(body, out_shape=outs, in_specs=(in_specs or [VMEM] * count...  14.6 us
    ppermute x3, waiting for transfers between devices, per_device(): from_y = [lax.ppermute(to_y[k - 1], 'dp', pair(k)) for k in (1, 3, 2)]  7.76 us
    ppermute x3, waiting for transfers between devices, per_device(): lax.ppermute(to_z[m - 1], 'spatial', pair_z(m))  5.18 us
    ppermute x3, waiting for transfers between devices, per_device(): lax.ppermute(chunk, 'spatial', pair_z(m))  4.94 us
    ppermute x1, waiting for transfers between devices, per_device(): far_part = lax.ppermute(part, 'spatial', pair_z(4))  4.56 us
    ppermute x1, waiting for transfers between devices, per_device(): from_far = lax.ppermute(grad_far, 'spatial', cross)  4.11 us
    ppermute x3, starting transfers between devices, per_device(): from_y = [lax.ppermute(to_y[k - 1], 'dp', pair(k)) for k in (1, 3, 2)]  4.01 us
  transfers between devices with their start and end apart: 26, of which 12 were waited for; matrix products, arithmetic and copies ran while one was open for 1% of the time, Pallas kernels for 11%

profile of v5, /device:TPU:1, one launch (start us, length us, event | category | flops | bytes accessed | tf_op | source)
XLA Modules:
  0.0 85.8 jit_solution(14659475131558788971)
XLA Ops:
  0.6 2.1 %shard_map.93.refs_5_.refs_3_ = bf16[2,256,256]{2,1,0:T(8,128)(2,1)S(1)} custom-call(bf16[256,1024]{1,0:T(8,128)(2,1)} %bitcast.5, bf16[3,1024,256]{2,1,0:T(8,128)(2,1)} %refs_3_.3), custom_call_target="tpu_custom_call" | custom-call | flops 268435456 | bytes 2359296 | tf_op jit(solution)/shard_map/pallas_call | solution.py:32
  2.7 0.0 copy-start.1
  2.7 0.0 copy-start.3
  2.7 3.1 %collective-permute-start.1 = (bf16[2,256,256]{2,1,0:T(8,128)(2,1)S(1)}, bf16[2,256,256]{2,1,0:T(8,128)(2,1)S(1)}, u32[]{:S(2)}, u32[]{:S(2)}) collective-permute-start(bf16[2,256,256]{2,1,0:T(8,128)(2,1)S(1)} %shard_map.93.refs_5_.refs_3_), channel_id=1, source_target_pairs={{0,240},{16,32},{32,16},{48,64},{64,48},{80,96},{96,80},{112,128},... | collective-permute-start | bytes 786440 | tf_op jit(solution)/shard_map/ppermute | solution.py:321
  5.8 3.8 %collective-permute-start = (bf16[2,256,256]{2,1,0:T(8,128)(2,1)S(1)}, bf16[2,256,256]{2,1,0:T(8,128)(2,1)S(1)}, u32[]{:S(2)}, u32[]{:S(2)}) collective-permute-start(bf16[2,256,256]{2,1,0:T(8,128)(2,1)S(1)} %shard_map.93.refs_5_.refs_3_), channel_id=1, source_target_pairs={{0,16},{16,0},{32,48},{48,32},{64,80},{80,64},{96,112},{112,96},{1... | collective-permute-start | bytes 786440 | tf_op jit(solution)/shard_map/ppermute | solution.py:282
  9.6 0.7 pad_add_fusion.refs_4_
  10.3 3.5 %shard_map.94 = (bf16[256,256]{1,0:T(8,128)(2,1)S(1)}, bf16[256,256]{1,0:T(8,128)(2,1)S(1)}, bf16[2,512,256]{2,1,0:T(8,128)(2,1)}, f32[4,768]{1,0:T(4,128)S(1)}) custom-call(bf16[256,1024]{1,0:T(8,128)(2,1)} %bitcast.6, bf16[3,1024,256]{2,1,0:T(8,128)(2,1)} %refs_3_.3, bf16[256,1024]{1,0:T(8,128)(2,1)} %refs_2_.5, bf16[256,1024]{1,0:T(8,128)(2,1)} %bitcast.9, ...), custom_call_target="tpu_custom_call" | custom-call | flops 536870912 | bytes 3947008 | tf_op jit(solution)/shard_map/pallas_call | solution.py:32
  13.8 0.1 collective-permute-start.4
  13.9 0.0 collective-permute-done.1.refs_4_
  13.9 0.0 collective-permute-done.refs_2_
  13.9 3.1 %shard_map.95 = (bf16[4,256,256]{2,1,0:T(8,128)(2,1)S(1)}, bf16[2,256,256]{2,1,0:T(8,128)(2,1)S(1)}, f32[2,256,256]{2,1,0:T(8,128)S(1)}) custom-call(bf16[256,256]{1,0:T(8,128)(2,1)S(1)} %get-tuple-element.29.refs_0_, bf16[256,256]{1,0:T(8,128)(2,1)S(1)} %get-tuple-element.30.refs_1_, bf16[2,256,256]{2,1,0:T(8,128)(2,1)S(1)} %collective-permute-done.refs_2_, ...), custom_call_target="tpu_custom_call" | custom-call | flops 503316480 | bytes 2371584 | tf_op jit(solution)/shard_map/pallas_call | solution.py:32
  17.1 0.6 collective-permute-start.3
  17.6 0.0 collective-permute-start.2
  17.6 0.7 shard_map.96.refs_0_
  18.4 0.0 copy-start
  18.4 0.0 copy-start.2
  18.4 0.7 collective-permute-done.3.refs_3_.refs_2_
  19.2 0.4 shard_map.97
  19.6 4.1 %collective-permute-done.2.refs_1_ = bf16[2,256,256]{2,1,0:T(8,128)(2,1)S(1)} collective-permute-done((bf16[2,256,256]{2,1,0:T(8,128)(2,1)S(1)}, bf16[2,256,256]{2,1,0:T(8,128)(2,1)S(1)}, u32[]{:S(2)}, u32[]{:S(2)}) %collective-permute-start.2) | collective-permute-done | bytes 262176 | tf_op jit(solution)/shard_map/ppermute | solution.py:336
  23.7 0.1 shard_map.98.refs_2_.refs_1_
  23.8 1.1 %collective-permute-start.5 = (bf16[2,256,256]{2,1,0:T(8,128)(2,1)S(1)}, bf16[2,256,256]{2,1,0:T(8,128)(2,1)S(1)}, u32[]{:S(2)}, u32[]{:S(2)}) collective-permute-start(bf16[2,256,256]{2,1,0:T(8,128)(2,1)S(1)} %shard_map.98.refs_2_.refs_1_), channel_id=1, source_target_pairs={{0,16},{16,0},{32,48},{48,32},{64,80},{80,64},{96,112},{112,96},{1... | collective-permute-start | bytes 786440 | tf_op jit(solution)/shard_map/ppermute | solution.py:282
  24.9 1.2 %collective-permute-done.5.refs_3_ = bf16[2,256,256]{2,1,0:T(8,128)(2,1)S(1)} collective-permute-done((bf16[2,256,256]{2,1,0:T(8,128)(2,1)S(1)}, bf16[2,256,256]{2,1,0:T(8,128)(2,1)S(1)}, u32[]{:S(2)}, u32[]{:S(2)}) %collective-permute-start.5) | collective-permute-done | bytes 262176 | tf_op jit(solution)/shard_map/ppermute | solution.py:282
  26.1 0.4 shard_map.99
  26.5 1.4 %collective-permute-start.8 = (bf16[128,1024]{1,0:T(8,128)(2,1)S(1)}, bf16[128,1024]{1,0:T(8,128)(2,1)S(1)}, u32[]{:S(2)}, u32[]{:S(2)}) collective-permute-start(bf16[128,1024]{1,0:T(8,128)(2,1)S(1)} %get-tuple-element.42), channel_id=1, source_target_pairs={{0,1},{1,0},{2,3},{3,2},{4,5},{5,4},{6,7},{7,6},{8,9},{9,8},{10,11... | collective-permute-start | bytes 786440 | tf_op jit(solution)/shard_map/ppermute | solution.py:364
  27.9 1.9 %collective-permute-start.9 = (bf16[128,1024]{1,0:T(8,128)(2,1)S(1)}, bf16[128,1024]{1,0:T(8,128)(2,1)S(1)}, u32[]{:S(2)}, u32[]{:S(2)}) collective-permute-start(bf16[128,1024]{1,0:T(8,128)(2,1)S(1)} %get-tuple-element.43), channel_id=1, source_target_pairs={{0,3},{1,2},{2,1},{3,0},{4,7},{5,6},{6,5},{7,4},{8,11},{9,10},{10,... | collective-permute-start | bytes 786440 | tf_op jit(solution)/shard_map/ppermute | solution.py:364
  29.8 0.7 collective-permute-start.10
  30.6 0.6 shard_map.100
  31.2 1.5 %collective-permute-start.6 = (bf16[2,256,256]{2,1,0:T(8,128)(2,1)S(1)}, bf16[2,256,256]{2,1,0:T(8,128)(2,1)S(1)}, u32[]{:S(2)}, u32[]{:S(2)}) collective-permute-start(bf16[2,256,256]{2,1,0:T(8,128)(2,1)S(1)} %get-tuple-element.40), channel_id=1, source_target_pairs={{0,4},{4,0},{8,12},{12,8},{1,5},{5,1},{9,13},{13,9},{2,6},{6,2},{1... | collective-permute-start | bytes 786440 | tf_op jit(solution)/shard_map/ppermute | solution.py:373
  32.6 1.8 %collective-permute-start.7 = (bf16[2,256,256]{2,1,0:T(8,128)(2,1)S(1)}, bf16[2,256,256]{2,1,0:T(8,128)(2,1)S(1)}, u32[]{:S(2)}, u32[]{:S(2)}) collective-permute-start(bf16[2,256,256]{2,1,0:T(8,128)(2,1)S(1)} %get-tuple-element.41), channel_id=1, source_target_pairs={{0,12},{4,8},{8,4},{12,0},{1,13},{5,9},{9,5},{13,1},{2,14},{6,10},... | collective-permute-start | bytes 786440 | tf_op jit(solution)/shard_map/ppermute | solution.py:373
  34.5 0.0 collective-permute-done.8.refs_1_
  34.5 5.8 %collective-permute-done.9.refs_2_ = bf16[128,1024]{1,0:T(8,128)(2,1)S(1)} collective-permute-done((bf16[128,1024]{1,0:T(8,128)(2,1)S(1)}, bf16[128,1024]{1,0:T(8,128)(2,1)S(1)}, u32[]{:S(2)}, u32[]{:S(2)}) %collective-permute-start.9) | collective-permute-done | bytes 262176 | tf_op jit(solution)/shard_map/ppermute | solution.py:364
  40.3 1.9 %collective-permute-done.10.refs_3_ = bf16[128,1024]{1,0:T(8,128)(2,1)S(1)} collective-permute-done((bf16[128,1024]{1,0:T(8,128)(2,1)S(1)}, bf16[128,1024]{1,0:T(8,128)(2,1)S(1)}, u32[]{:S(2)}, u32[]{:S(2)}) %collective-permute-start.10) | collective-permute-done | bytes 262176 | tf_op jit(solution)/shard_map/ppermute | solution.py:364
  42.2 0.1 shard_map.101
  42.3 0.1 collective-permute-start.11
  42.4 2.5 %collective-permute-start.12 = (bf16[32,1024]{1,0:T(8,128)(2,1)S(1)}, bf16[32,1024]{1,0:T(8,128)(2,1)S(1)}, u32[]{:S(2)}, u32[]{:S(2)}) collective-permute-start(bf16[32,1024]{1,0:T(8,128)(2,1)S(1)} %get-tuple-element.47), channel_id=1, source_target_pairs={{0,96},{16,112},{32,64},{48,80},{64,32},{80,48},{96,0},{112,16},{1... | collective-permute-start | bytes 196616 | tf_op jit(solution)/shard_map/ppermute | solution.py:381
  44.9 0.2 collective-permute-start.13
  45.1 4.7 %collective-permute-done.11.refs_1_ = bf16[32,1024]{1,0:T(8,128)(2,1)S(1)} collective-permute-done((bf16[32,1024]{1,0:T(8,128)(2,1)S(1)}, bf16[32,1024]{1,0:T(8,128)(2,1)S(1)}, u32[]{:S(2)}, u32[]{:S(2)}) %collective-permute-start.11) | collective-permute-done | bytes 65568 | tf_op jit(solution)/shard_map/ppermute | solution.py:381
  49.8 0.0 collective-permute-done.12.refs_2_
  49.8 0.5 collective-permute-done.13.refs_3_
  50.3 2.6 %collective-permute-start.14 = (bf16[32,1024]{1,0:T(8,128)(2,1)S(1)}, bf16[32,1024]{1,0:T(8,128)(2,1)S(1)}, u32[]{:S(2)}, u32[]{:S(2)}) collective-permute-start(bf16[32,1024]{1,0:T(8,128)(2,1)S(1)} %shard_map.102.refs_0_), channel_id=1, source_target_pairs={{0,128},{16,144},{32,160},{48,176},{64,192},{80,208},{96,224},{112... | collective-permute-start | bytes 196616 | tf_op jit(solution)/shard_map/ppermute | solution.py:383
  53.0 4.6 %collective-permute-done.14.refs_1_ = bf16[32,1024]{1,0:T(8,128)(2,1)S(1)} collective-permute-done((bf16[32,1024]{1,0:T(8,128)(2,1)S(1)}, bf16[32,1024]{1,0:T(8,128)(2,1)S(1)}, u32[]{:S(2)}, u32[]{:S(2)}) %collective-permute-start.14) | collective-permute-done | bytes 65568 | tf_op jit(solution)/shard_map/ppermute | solution.py:383
  57.5 3.1 %collective-permute-start.17 = (bf16[32,1024]{1,0:T(8,128)(2,1)S(1)}, bf16[32,1024]{1,0:T(8,128)(2,1)S(1)}, u32[]{:S(2)}, u32[]{:S(2)}) collective-permute-start(bf16[32,1024]{1,0:T(8,128)(2,1)S(1)} %shard_map.103.refs_0_), channel_id=1, source_target_pairs={{0,64},{16,80},{32,96},{48,112},{64,0},{80,16},{96,32},{112,48},{1... | collective-permute-start | bytes 196616 | tf_op jit(solution)/shard_map/ppermute | solution.py:385
  60.6 0.4 collective-permute-start.16
  61.1 0.0 collective-permute-start.15
  61.1 0.0 collective-permute-done.6.refs_4_.refs_1_
  61.1 0.0 collective-permute-done.7.refs_5_.refs_2_
  61.1 1.9 %collective-permute-done.17.refs_3_ = bf16[32,1024]{1,0:T(8,128)(2,1)S(1)} collective-permute-done((bf16[32,1024]{1,0:T(8,128)(2,1)S(1)}, bf16[32,1024]{1,0:T(8,128)(2,1)S(1)}, u32[]{:S(2)}, u32[]{:S(2)}) %collective-permute-start.17) | collective-permute-done | bytes 65568 | tf_op jit(solution)/shard_map/ppermute | solution.py:385
  63.0 3.0 %collective-permute-done.16.refs_2_ = bf16[32,1024]{1,0:T(8,128)(2,1)S(1)} collective-permute-done((bf16[32,1024]{1,0:T(8,128)(2,1)S(1)}, bf16[32,1024]{1,0:T(8,128)(2,1)S(1)}, u32[]{:S(2)}, u32[]{:S(2)}) %collective-permute-start.16) | collective-permute-done | bytes 65568 | tf_op jit(solution)/shard_map/ppermute | solution.py:385
  66.0 0.1 collective-permute-start.21
  66.1 0.9 %collective-permute-start.20 = (bf16[128,1024]{1,0:T(8,128)(2,1)S(1)}, bf16[128,1024]{1,0:T(8,128)(2,1)S(1)}, u32[]{:S(2)}, u32[]{:S(2)}) collective-permute-start(bf16[128,1024]{1,0:T(8,128)(2,1)S(1)} %shard_map.104.refs_4_.refs_0_), channel_id=1, source_target_pairs={{0,3},{1,2},{2,1},{3,0},{4,7},{5,6},{6,5},{7,4},{8,11},{9,10},{10,... | collective-permute-start | bytes 786440 | tf_op jit(solution)/shard_map/ppermute | solution.py:393
  67.1 2.3 %collective-permute-start.19 = (bf16[128,1024]{1,0:T(8,128)(2,1)S(1)}, bf16[128,1024]{1,0:T(8,128)(2,1)S(1)}, u32[]{:S(2)}, u32[]{:S(2)}) collective-permute-start(bf16[128,1024]{1,0:T(8,128)(2,1)S(1)} %shard_map.104.refs_4_.refs_0_), channel_id=1, source_target_pairs={{0,2},{1,3},{2,0},{3,1},{4,6},{5,7},{6,4},{7,5},{8,10},{9,11},{10,... | collective-permute-start | bytes 786440 | tf_op jit(solution)/shard_map/ppermute | solution.py:393
  69.4 0.3 shard_map.105
  69.7 2.8 %collective-permute-start.18 = (bf16[2,256,256]{2,1,0:T(8,128)(2,1)S(1)}, bf16[2,256,256]{2,1,0:T(8,128)(2,1)S(1)}, u32[]{:S(2)}, u32[]{:S(2)}) collective-permute-start(bf16[2,256,256]{2,1,0:T(8,128)(2,1)S(1)} %shard_map.105), channel_id=1, source_target_pairs={{0,8},{4,12},{8,0},{12,4},{1,9},{5,13},{9,1},{13,5},{2,10},{6,14},... | collective-permute-start | bytes 786440 | tf_op jit(solution)/shard_map/ppermute | solution.py:401
  72.6 3.7 %collective-permute-start.22 = (bf16[128,1024]{1,0:T(8,128)(2,1)S(1)}, bf16[128,1024]{1,0:T(8,128)(2,1)S(1)}, u32[]{:S(2)}, u32[]{:S(2)}) collective-permute-start(bf16[128,1024]{1,0:T(8,128)(2,1)S(1)} %shard_map.104.refs_4_.refs_0_), channel_id=1, source_target_pairs={{0,16},{16,0},{32,48},{48,32},{64,80},{80,64},{96,112},{112,96},{1... | collective-permute-start | bytes 786440 | tf_op jit(solution)/shard_map/ppermute | solution.py:282
  76.3 0.0 collective-permute-done.21.refs_3_
  76.3 1.4 %collective-permute-start.25 = (bf16[128,1024]{1,0:T(8,128)(2,1)S(1)}, bf16[128,1024]{1,0:T(8,128)(2,1)S(1)}, u32[]{:S(2)}, u32[]{:S(2)}) collective-permute-start(bf16[128,1024]{1,0:T(8,128)(2,1)S(1)} %collective-permute-done.21.refs_3_), channel_id=1, source_target_pairs={{0,16},{16,0},{32,48},{48,32},{64,80},{80,64},{96,112},{112,96},{1... | collective-permute-start | bytes 786440 | tf_op jit(solution)/shard_map/ppermute | solution.py:282
  77.7 0.0 collective-permute-done.20.refs_2_
  77.7 4.1 %collective-permute-start.24 = (bf16[128,1024]{1,0:T(8,128)(2,1)S(1)}, bf16[128,1024]{1,0:T(8,128)(2,1)S(1)}, u32[]{:S(2)}, u32[]{:S(2)}) collective-permute-start(bf16[128,1024]{1,0:T(8,128)(2,1)S(1)} %collective-permute-done.20.refs_2_), channel_id=1, source_target_pairs={{0,16},{16,0},{32,48},{48,32},{64,80},{80,64},{96,112},{112,96},{1... | collective-permute-start | bytes 786440 | tf_op jit(solution)/shard_map/ppermute | solution.py:282
  81.8 0.0 collective-permute-done.19.refs_1_
  81.8 0.0 collective-permute-start.23
  81.8 0.8 shard_map.106
  82.6 0.3 collective-permute-done.24.refs_6_
  82.9 0.4 collective-permute-done.23.refs_5_
  83.3 2.3 %shard_map.107 = (f32[3,1024,256]{2,1,0:T(8,128)}, f32[256,1024]{1,0:T(8,128)}) custom-call(bf16[128,1024]{1,0:T(8,128)(2,1)S(1)} %shard_map.104.refs_4_.refs_0_, bf16[128,1024]{1,0:T(8,128)(2,1)S(1)} %collective-permute-done.19.refs_1_, bf16[128,1024]{1,0:T(8,128)(2,1)S(1)} %collective-permute-done.20.refs_2_, ...), custom_call_target="tpu_custom_call" | custom-call | flops 1048576 | bytes 6291456 | tf_op jit(solution)/shard_map/pallas_call | solution.py:32
  (12 shorter events, 0.1 us)
Async XLA Ops:
  2.7 14.9 %copy-start.1 = (bf16[1,256,1024]{2,1,0:T(8,128)(2,1)S(1)}, bf16[1,256,1024]{2,1,0:T(8,128)(2,1)}, u32[]{:S(2)}) copy-start(bf16[1,256,1024]{2,1,0:T(8,128)(2,1)} %param.6) | copy-start | bytes 1572868
  2.7 14.9 %copy-start.3 = (bf16[1,256,1024]{2,1,0:T(8,128)(2,1)S(1)}, bf16[1,256,1024]{2,1,0:T(8,128)(2,1)}, u32[]{:S(2)}) copy-start(bf16[1,256,1024]{2,1,0:T(8,128)(2,1)} %param.11) | copy-start | bytes 1572868
  2.7 11.2 %collective-permute-start.1 = (bf16[2,256,256]{2,1,0:T(8,128)(2,1)S(1)}, bf16[2,256,256]{2,1,0:T(8,128)(2,1)S(1)}, u32[]{:S(2)}, u32[]{:S(2)}) collective-permute-start(bf16[2,256,256]{2,1,0:T(8,128)(2,1)S(1)} %shard_map.93.refs_5_.refs_3_), channel_id=1, source_target_pairs={{0,240},{16,32},{32,16},{48,64},{64,48},{80,96},{96,80},{112,128},... | collective-permute-start | bytes 786440 | tf_op jit(solution)/shard_map/ppermute | solution.py:321
  5.8 8.1 %collective-permute-start = (bf16[2,256,256]{2,1,0:T(8,128)(2,1)S(1)}, bf16[2,256,256]{2,1,0:T(8,128)(2,1)S(1)}, u32[]{:S(2)}, u32[]{:S(2)}) collective-permute-start(bf16[2,256,256]{2,1,0:T(8,128)(2,1)S(1)} %shard_map.93.refs_5_.refs_3_), channel_id=1, source_target_pairs={{0,16},{16,0},{32,48},{48,32},{64,80},{80,64},{96,112},{112,96},{1... | collective-permute-start | bytes 786440 | tf_op jit(solution)/shard_map/ppermute | solution.py:282
  13.8 4.6 %collective-permute-start.4 = (bf16[2,512,256]{2,1,0:T(8,128)(2,1)}, bf16[2,512,256]{2,1,0:T(8,128)(2,1)S(1)}, u32[]{:S(2)}, u32[]{:S(2)}) collective-permute-start(bf16[2,512,256]{2,1,0:T(8,128)(2,1)} %get-tuple-element.35), channel_id=1, source_target_pairs={{0,16},{16,0},{32,48},{48,32},{64,80},{80,64},{96,112},{112,96},{1... | collective-permute-start | bytes 1572872 | tf_op jit(solution)/shard_map/ppermute | solution.py:282
  17.1 2.1 %collective-permute-start.3 = (bf16[4,256,256]{2,1,0:T(8,128)(2,1)S(1)}, bf16[4,256,256]{2,1,0:T(8,128)(2,1)S(1)}, u32[]{:S(2)}, u32[]{:S(2)}) collective-permute-start(bf16[4,256,256]{2,1,0:T(8,128)(2,1)S(1)} %get-tuple-element.32.refs_2_.refs_0_), channel_id=1, source_target_pairs={{0,16},{16,0},{32,48},{48,32},{64,80},{80,64},{96,112},{112,96},{1... | collective-permute-start | bytes 1572872 | tf_op jit(solution)/shard_map/ppermute | solution.py:282
  17.6 6.1 %collective-permute-start.2 = (bf16[2,256,256]{2,1,0:T(8,128)(2,1)S(1)}, bf16[2,256,256]{2,1,0:T(8,128)(2,1)S(1)}, u32[]{:S(2)}, u32[]{:S(2)}) collective-permute-start(bf16[2,256,256]{2,1,0:T(8,128)(2,1)S(1)} %get-tuple-element.34), channel_id=1, source_target_pairs={{0,240},{16,32},{32,16},{48,64},{64,48},{80,96},{96,80},{112,128},... | collective-permute-start | bytes 786440 | tf_op jit(solution)/shard_map/ppermute | solution.py:336
  18.4 12.2 %copy-start = (bf16[3,1024,256]{2,1,0:T(8,128)(2,1)S(1)}, bf16[3,1024,256]{2,1,0:T(8,128)(2,1)}, u32[]{:S(2)}) copy-start(bf16[3,1024,256]{2,1,0:T(8,128)(2,1)} %refs_3_.3) | copy-start | bytes 4718596
  18.4 12.1 %copy-start.2 = (bf16[256,1024]{1,0:T(8,128)(2,1)S(1)}, bf16[256,1024]{1,0:T(8,128)(2,1)}, u32[]{:S(2)}) copy-start(bf16[256,1024]{1,0:T(8,128)(2,1)} %refs_2_.5) | copy-start | bytes 1572868
  23.8 2.3 %collective-permute-start.5 = (bf16[2,256,256]{2,1,0:T(8,128)(2,1)S(1)}, bf16[2,256,256]{2,1,0:T(8,128)(2,1)S(1)}, u32[]{:S(2)}, u32[]{:S(2)}) collective-permute-start(bf16[2,256,256]{2,1,0:T(8,128)(2,1)S(1)} %shard_map.98.refs_2_.refs_1_), channel_id=1, source_target_pairs={{0,16},{16,0},{32,48},{48,32},{64,80},{80,64},{96,112},{112,96},{1... | collective-permute-start | bytes 786440 | tf_op jit(solution)/shard_map/ppermute | solution.py:282
  26.5 7.9 %collective-permute-start.8 = (bf16[128,1024]{1,0:T(8,128)(2,1)S(1)}, bf16[128,1024]{1,0:T(8,128)(2,1)S(1)}, u32[]{:S(2)}, u32[]{:S(2)}) collective-permute-start(bf16[128,1024]{1,0:T(8,128)(2,1)S(1)} %get-tuple-element.42), channel_id=1, source_target_pairs={{0,1},{1,0},{2,3},{3,2},{4,5},{5,4},{6,7},{7,6},{8,9},{9,8},{10,11... | collective-permute-start | bytes 786440 | tf_op jit(solution)/shard_map/ppermute | solution.py:364
  27.9 12.4 %collective-permute-start.9 = (bf16[128,1024]{1,0:T(8,128)(2,1)S(1)}, bf16[128,1024]{1,0:T(8,128)(2,1)S(1)}, u32[]{:S(2)}, u32[]{:S(2)}) collective-permute-start(bf16[128,1024]{1,0:T(8,128)(2,1)S(1)} %get-tuple-element.43), channel_id=1, source_target_pairs={{0,3},{1,2},{2,1},{3,0},{4,7},{5,6},{6,5},{7,4},{8,11},{9,10},{10,... | collective-permute-start | bytes 786440 | tf_op jit(solution)/shard_map/ppermute | solution.py:364
  29.8 12.4 %collective-permute-start.10 = (bf16[128,1024]{1,0:T(8,128)(2,1)S(1)}, bf16[128,1024]{1,0:T(8,128)(2,1)S(1)}, u32[]{:S(2)}, u32[]{:S(2)}) collective-permute-start(bf16[128,1024]{1,0:T(8,128)(2,1)S(1)} %get-tuple-element.44), channel_id=1, source_target_pairs={{0,2},{1,3},{2,0},{3,1},{4,6},{5,7},{6,4},{7,5},{8,10},{9,11},{10,... | collective-permute-start | bytes 786440 | tf_op jit(solution)/shard_map/ppermute | solution.py:364
  31.2 29.9 %collective-permute-start.6 = (bf16[2,256,256]{2,1,0:T(8,128)(2,1)S(1)}, bf16[2,256,256]{2,1,0:T(8,128)(2,1)S(1)}, u32[]{:S(2)}, u32[]{:S(2)}) collective-permute-start(bf16[2,256,256]{2,1,0:T(8,128)(2,1)S(1)} %get-tuple-element.40), channel_id=1, source_target_pairs={{0,4},{4,0},{8,12},{12,8},{1,5},{5,1},{9,13},{13,9},{2,6},{6,2},{1... | collective-permute-start | bytes 786440 | tf_op jit(solution)/shard_map/ppermute | solution.py:373
  32.6 28.4 %collective-permute-start.7 = (bf16[2,256,256]{2,1,0:T(8,128)(2,1)S(1)}, bf16[2,256,256]{2,1,0:T(8,128)(2,1)S(1)}, u32[]{:S(2)}, u32[]{:S(2)}) collective-permute-start(bf16[2,256,256]{2,1,0:T(8,128)(2,1)S(1)} %get-tuple-element.41), channel_id=1, source_target_pairs={{0,12},{4,8},{8,4},{12,0},{1,13},{5,9},{9,5},{13,1},{2,14},{6,10},... | collective-permute-start | bytes 786440 | tf_op jit(solution)/shard_map/ppermute | solution.py:373
  42.3 7.5 %collective-permute-start.11 = (bf16[32,1024]{1,0:T(8,128)(2,1)S(1)}, bf16[32,1024]{1,0:T(8,128)(2,1)S(1)}, u32[]{:S(2)}, u32[]{:S(2)}) collective-permute-start(bf16[32,1024]{1,0:T(8,128)(2,1)S(1)} %get-tuple-element.46), channel_id=1, source_target_pairs={{0,64},{16,80},{32,96},{48,112},{64,0},{80,16},{96,32},{112,48},{1... | collective-permute-start | bytes 196616 | tf_op jit(solution)/shard_map/ppermute | solution.py:381
  42.4 7.4 %collective-permute-start.12 = (bf16[32,1024]{1,0:T(8,128)(2,1)S(1)}, bf16[32,1024]{1,0:T(8,128)(2,1)S(1)}, u32[]{:S(2)}, u32[]{:S(2)}) collective-permute-start(bf16[32,1024]{1,0:T(8,128)(2,1)S(1)} %get-tuple-element.47), channel_id=1, source_target_pairs={{0,96},{16,112},{32,64},{48,80},{64,32},{80,48},{96,0},{112,16},{1... | collective-permute-start | bytes 196616 | tf_op jit(solution)/shard_map/ppermute | solution.py:381
  44.9 5.4 %collective-permute-start.13 = (bf16[32,1024]{1,0:T(8,128)(2,1)S(1)}, bf16[32,1024]{1,0:T(8,128)(2,1)S(1)}, u32[]{:S(2)}, u32[]{:S(2)}) collective-permute-start(bf16[32,1024]{1,0:T(8,128)(2,1)S(1)} %get-tuple-element.48), channel_id=1, source_target_pairs={{0,32},{16,48},{32,0},{48,16},{64,96},{80,112},{96,64},{112,80},{1... | collective-permute-start | bytes 196616 | tf_op jit(solution)/shard_map/ppermute | solution.py:381
  50.3 7.2 %collective-permute-start.14 = (bf16[32,1024]{1,0:T(8,128)(2,1)S(1)}, bf16[32,1024]{1,0:T(8,128)(2,1)S(1)}, u32[]{:S(2)}, u32[]{:S(2)}) collective-permute-start(bf16[32,1024]{1,0:T(8,128)(2,1)S(1)} %shard_map.102.refs_0_), channel_id=1, source_target_pairs={{0,128},{16,144},{32,160},{48,176},{64,192},{80,208},{96,224},{112... | collective-permute-start | bytes 196616 | tf_op jit(solution)/shard_map/ppermute | solution.py:383
  57.5 5.5 %collective-permute-start.17 = (bf16[32,1024]{1,0:T(8,128)(2,1)S(1)}, bf16[32,1024]{1,0:T(8,128)(2,1)S(1)}, u32[]{:S(2)}, u32[]{:S(2)}) collective-permute-start(bf16[32,1024]{1,0:T(8,128)(2,1)S(1)} %shard_map.103.refs_0_), channel_id=1, source_target_pairs={{0,64},{16,80},{32,96},{48,112},{64,0},{80,16},{96,32},{112,48},{1... | collective-permute-start | bytes 196616 | tf_op jit(solution)/shard_map/ppermute | solution.py:385
  60.6 5.4 %collective-permute-start.16 = (bf16[32,1024]{1,0:T(8,128)(2,1)S(1)}, bf16[32,1024]{1,0:T(8,128)(2,1)S(1)}, u32[]{:S(2)}, u32[]{:S(2)}) collective-permute-start(bf16[32,1024]{1,0:T(8,128)(2,1)S(1)} %shard_map.103.refs_0_), channel_id=1, source_target_pairs={{0,96},{16,112},{32,64},{48,80},{64,32},{80,48},{96,0},{112,16},{1... | collective-permute-start | bytes 196616 | tf_op jit(solution)/shard_map/ppermute | solution.py:385
  61.1 5.0 %collective-permute-start.15 = (bf16[32,1024]{1,0:T(8,128)(2,1)S(1)}, bf16[32,1024]{1,0:T(8,128)(2,1)S(1)}, u32[]{:S(2)}, u32[]{:S(2)}) collective-permute-start(bf16[32,1024]{1,0:T(8,128)(2,1)S(1)} %shard_map.103.refs_0_), channel_id=1, source_target_pairs={{0,32},{16,48},{32,0},{48,16},{64,96},{80,112},{96,64},{112,80},{1... | collective-permute-start | bytes 196616 | tf_op jit(solution)/shard_map/ppermute | solution.py:385
  66.0 10.2 %collective-permute-start.21 = (bf16[128,1024]{1,0:T(8,128)(2,1)S(1)}, bf16[128,1024]{1,0:T(8,128)(2,1)S(1)}, u32[]{:S(2)}, u32[]{:S(2)}) collective-permute-start(bf16[128,1024]{1,0:T(8,128)(2,1)S(1)} %shard_map.104.refs_4_.refs_0_), channel_id=1, source_target_pairs={{0,1},{1,0},{2,3},{3,2},{4,5},{5,4},{6,7},{7,6},{8,9},{9,8},{10,11... | collective-permute-start | bytes 786440 | tf_op jit(solution)/shard_map/ppermute | solution.py:393
  66.1 11.5 %collective-permute-start.20 = (bf16[128,1024]{1,0:T(8,128)(2,1)S(1)}, bf16[128,1024]{1,0:T(8,128)(2,1)S(1)}, u32[]{:S(2)}, u32[]{:S(2)}) collective-permute-start(bf16[128,1024]{1,0:T(8,128)(2,1)S(1)} %shard_map.104.refs_4_.refs_0_), channel_id=1, source_target_pairs={{0,3},{1,2},{2,1},{3,0},{4,7},{5,6},{6,5},{7,4},{8,11},{9,10},{10,... | collective-permute-start | bytes 786440 | tf_op jit(solution)/shard_map/ppermute | solution.py:393
  67.1 14.7 %collective-permute-start.19 = (bf16[128,1024]{1,0:T(8,128)(2,1)S(1)}, bf16[128,1024]{1,0:T(8,128)(2,1)S(1)}, u32[]{:S(2)}, u32[]{:S(2)}) collective-permute-start(bf16[128,1024]{1,0:T(8,128)(2,1)S(1)} %shard_map.104.refs_4_.refs_0_), channel_id=1, source_target_pairs={{0,2},{1,3},{2,0},{3,1},{4,6},{5,7},{6,4},{7,5},{8,10},{9,11},{10,... | collective-permute-start | bytes 786440 | tf_op jit(solution)/shard_map/ppermute | solution.py:393
  69.7 12.1 %collective-permute-start.18 = (bf16[2,256,256]{2,1,0:T(8,128)(2,1)S(1)}, bf16[2,256,256]{2,1,0:T(8,128)(2,1)S(1)}, u32[]{:S(2)}, u32[]{:S(2)}) collective-permute-start(bf16[2,256,256]{2,1,0:T(8,128)(2,1)S(1)} %shard_map.105), channel_id=1, source_target_pairs={{0,8},{4,12},{8,0},{12,4},{1,9},{5,13},{9,1},{13,5},{2,10},{6,14},... | collective-permute-start | bytes 786440 | tf_op jit(solution)/shard_map/ppermute | solution.py:401
  72.6 10.1 %collective-permute-start.22 = (bf16[128,1024]{1,0:T(8,128)(2,1)S(1)}, bf16[128,1024]{1,0:T(8,128)(2,1)S(1)}, u32[]{:S(2)}, u32[]{:S(2)}) collective-permute-start(bf16[128,1024]{1,0:T(8,128)(2,1)S(1)} %shard_map.104.refs_4_.refs_0_), channel_id=1, source_target_pairs={{0,16},{16,0},{32,48},{48,32},{64,80},{80,64},{96,112},{112,96},{1... | collective-permute-start | bytes 786440 | tf_op jit(solution)/shard_map/ppermute | solution.py:282
  76.3 6.3 %collective-permute-start.25 = (bf16[128,1024]{1,0:T(8,128)(2,1)S(1)}, bf16[128,1024]{1,0:T(8,128)(2,1)S(1)}, u32[]{:S(2)}, u32[]{:S(2)}) collective-permute-start(bf16[128,1024]{1,0:T(8,128)(2,1)S(1)} %collective-permute-done.21.refs_3_), channel_id=1, source_target_pairs={{0,16},{16,0},{32,48},{48,32},{64,80},{80,64},{96,112},{112,96},{1... | collective-permute-start | bytes 786440 | tf_op jit(solution)/shard_map/ppermute | solution.py:282
  77.7 5.3 %collective-permute-start.24 = (bf16[128,1024]{1,0:T(8,128)(2,1)S(1)}, bf16[128,1024]{1,0:T(8,128)(2,1)S(1)}, u32[]{:S(2)}, u32[]{:S(2)}) collective-permute-start(bf16[128,1024]{1,0:T(8,128)(2,1)S(1)} %collective-permute-done.20.refs_2_), channel_id=1, source_target_pairs={{0,16},{16,0},{32,48},{48,32},{64,80},{80,64},{96,112},{112,96},{1... | collective-permute-start | bytes 786440 | tf_op jit(solution)/shard_map/ppermute | solution.py:282
  81.8 1.5 %collective-permute-start.23 = (bf16[128,1024]{1,0:T(8,128)(2,1)S(1)}, bf16[128,1024]{1,0:T(8,128)(2,1)S(1)}, u32[]{:S(2)}, u32[]{:S(2)}) collective-permute-start(bf16[128,1024]{1,0:T(8,128)(2,1)S(1)} %collective-permute-done.19.refs_1_), channel_id=1, source_target_pairs={{0,16},{16,0},{32,48},{48,32},{64,80},{80,64},{96,112},{112,96},{1... | collective-permute-start | bytes 786440 | tf_op jit(solution)/shard_map/ppermute | solution.py:282

commit v6 on v5

--- a/solution.py
+++ b/solution.py
@@ -66,8 +66,7 @@
     return (feature == row).astype(F32).astype(BF)
 
 
-def pick_rows(side, x_ref, cot_ref, out_ref):
-    pick = picker(side)
+def pick_rows(pick, x_ref, cot_ref, out_ref):
     out_ref[0] = nt(pick, x_ref[...]).astype(BF)
     out_ref[1] = nt(pick, cot_ref[...]).astype(BF)
 
@@ -96,6 +95,7 @@
     x_load, w_load, cot_load, wo_load = fetch(pairs, sems)
 
     z, core, _, _ = place_of()
+    pick = picker(1 - core)
     base = (z * 2 + core) * 4
     starts = (base - 4 + 8 * core, base, base + 4 - 8 * core)
     lane = lax.broadcasted_iota(jnp.int32, (4, 128), 1)
@@ -118,11 +118,11 @@
     cot_load.wait()
     wo_load.wait()
     u_ref[...] = nt(cot_ref[...], wo_ref[...]).astype(BF)
-    pick_rows(1 - core, x_ref, cot_ref, xc_ref)
+    pick_rows(pick, x_ref, cot_ref, xc_ref)
 
 
 def mine_kernel(x_ref, cot_ref, xc_ref):
-    pick_rows(place_of()[1], x_ref, cot_ref, xc_ref)
+    pick_rows(picker(place_of()[1]), x_ref, cot_ref, xc_ref)
 
 
 def attention_kernel(q_ref, u_ref, mate_ref, own_ref, far_ref, bias_ref, acts_ref, gf_ref, go_ref):
@@ -247,7 +247,7 @@
     copies = []
     for n, k in enumerate(PLACE_ORDER):
         block = pl.ds(pl.multiple_of((y ^ k) * 256, 256), 256)
-        for array, column in ((3, 1), (0, 0), (1, 2), (2, 3)):
+        for array, column in ((0, 0), (1, 2), (2, 3), (3, 1)):
             cols = slice(column * WIDTH, (column + 1) * WIDTH)
             for side, blocks in ((core, mine), (1 - core, other)):
                 for m in range(4):

time: 85.9 us -> 85.8 us (level)
  no operation moved by 1% of the time
where the time goes in v6:
time: 85.8 us; the launch traced here: 85.6 us
  starting transfers between devices  40.3 us (47%)
  waiting for transfers between devices  29.2 us (34%)
  Pallas kernels  14.5 us (17%)
  between operations  0.97 us (1%)
    ppermute x8, starting transfers between devices, swapped(): return lax.ppermute(a, 'spatial', swap)  14.8 us
    pallas_call x15, Pallas kernels, call(): pl.pallas_call(body, out_shape=outs, in_specs=(in_specs or [VMEM] * count...  14.5 us
    ppermute x3, waiting for transfers between devices, per_device(): from_y = [lax.ppermute(to_y[k - 1], 'dp', pair(k)) for k in (1, 3, 2)]  7.76 us
    ppermute x3, waiting for transfers between devices, per_device(): lax.ppermute(to_z[m - 1], 'spatial', pair_z(m))  5.18 us
    ppermute x3, waiting for transfers between devices, per_device(): lax.ppermute(chunk, 'spatial', pair_z(m))  4.94 us
    ppermute x1, waiting for transfers between devices, per_device(): far_part = lax.ppermute(part, 'spatial', pair_z(4))  4.56 us
    ppermute x1, waiting for transfers between devices, per_device(): from_far = lax.ppermute(grad_far, 'spatial', cross)  4.11 us
    ppermute x3, starting transfers between devices, per_device(): from_y = [lax.ppermute(to_y[k - 1], 'dp', pair(k)) for k in (1, 3, 2)]  4 us
  transfers between devices with their start and end apart: 26, of which 12 were waited for; matrix products, arithmetic and copies ran while one was open for 1% of the time, Pallas kernels for 11%

profile of v6, /device:TPU:1, one launch (start us, length us, event | category | flops | bytes accessed | tf_op | source)
XLA Modules:
  0.0 85.6 jit_solution(594633312350128534)
XLA Ops:
  0.6 2.1 %shard_map.93.refs_5_.refs_3_ = bf16[2,256,256]{2,1,0:T(8,128)(2,1)S(1)} custom-call(bf16[256,1024]{1,0:T(8,128)(2,1)} %bitcast.5, bf16[3,1024,256]{2,1,0:T(8,128)(2,1)} %refs_3_.3), custom_call_target="tpu_custom_call" | custom-call | flops 268435456 | bytes 2359296 | tf_op jit(solution)/shard_map/pallas_call | solution.py:32
  2.7 0.0 copy-start.1
  2.7 0.0 copy-start.3
  2.7 3.1 %collective-permute-start.1 = (bf16[2,256,256]{2,1,0:T(8,128)(2,1)S(1)}, bf16[2,256,256]{2,1,0:T(8,128)(2,1)S(1)}, u32[]{:S(2)}, u32[]{:S(2)}) collective-permute-start(bf16[2,256,256]{2,1,0:T(8,128)(2,1)S(1)} %shard_map.93.refs_5_.refs_3_), channel_id=1, source_target_pairs={{0,240},{16,32},{32,16},{48,64},{64,48},{80,96},{96,80},{112,128},... | collective-permute-start | bytes 786440 | tf_op jit(solution)/shard_map/ppermute | solution.py:321
  5.8 3.8 %collective-permute-start = (bf16[2,256,256]{2,1,0:T(8,128)(2,1)S(1)}, bf16[2,256,256]{2,1,0:T(8,128)(2,1)S(1)}, u32[]{:S(2)}, u32[]{:S(2)}) collective-permute-start(bf16[2,256,256]{2,1,0:T(8,128)(2,1)S(1)} %shard_map.93.refs_5_.refs_3_), channel_id=1, source_target_pairs={{0,16},{16,0},{32,48},{48,32},{64,80},{80,64},{96,112},{112,96},{1... | collective-permute-start | bytes 786440 | tf_op jit(solution)/shard_map/ppermute | solution.py:282
  9.6 0.7 pad_add_fusion.refs_4_
  10.3 3.5 %shard_map.94 = (bf16[256,256]{1,0:T(8,128)(2,1)S(1)}, bf16[256,256]{1,0:T(8,128)(2,1)S(1)}, bf16[2,512,256]{2,1,0:T(8,128)(2,1)}, f32[4,768]{1,0:T(4,128)S(1)}) custom-call(bf16[256,1024]{1,0:T(8,128)(2,1)} %bitcast.6, bf16[3,1024,256]{2,1,0:T(8,128)(2,1)} %refs_3_.3, bf16[256,1024]{1,0:T(8,128)(2,1)} %refs_2_.5, bf16[256,1024]{1,0:T(8,128)(2,1)} %bitcast.9, ...), custom_call_target="tpu_custom_call" | custom-call | flops 536870912 | bytes 3947008 | tf_op jit(solution)/shard_map/pallas_call | solution.py:32
  13.8 0.1 collective-permute-start.4
  13.9 0.0 collective-permute-done.1.refs_4_
  13.9 0.0 collective-permute-done.refs_2_
  13.9 3.1 %shard_map.95 = (bf16[4,256,256]{2,1,0:T(8,128)(2,1)S(1)}, bf16[2,256,256]{2,1,0:T(8,128)(2,1)S(1)}, f32[2,256,256]{2,1,0:T(8,128)S(1)}) custom-call(bf16[256,256]{1,0:T(8,128)(2,1)S(1)} %get-tuple-element.29.refs_0_, bf16[256,256]{1,0:T(8,128)(2,1)S(1)} %get-tuple-element.30.refs_1_, bf16[2,256,256]{2,1,0:T(8,128)(2,1)S(1)} %collective-permute-done.refs_2_, ...), custom_call_target="tpu_custom_call" | custom-call | flops 503316480 | bytes 2371584 | tf_op jit(solution)/shard_map/pallas_call | solution.py:32
  17.1 0.6 collective-permute-start.3
  17.6 0.0 collective-permute-start.2
  17.6 0.7 shard_map.96.refs_0_
  18.4 0.0 copy-start
  18.4 0.0 copy-start.2
  18.4 0.0 collective-permute-done.4.refs_1_
  18.4 0.7 collective-permute-done.3.refs_3_.refs_2_
  19.2 0.4 shard_map.97
  19.6 4.1 %collective-permute-done.2.refs_1_ = bf16[2,256,256]{2,1,0:T(8,128)(2,1)S(1)} collective-permute-done((bf16[2,256,256]{2,1,0:T(8,128)(2,1)S(1)}, bf16[2,256,256]{2,1,0:T(8,128)(2,1)S(1)}, u32[]{:S(2)}, u32[]{:S(2)}) %collective-permute-start.2) | collective-permute-done | bytes 262176 | tf_op jit(solution)/shard_map/ppermute | solution.py:336
  23.7 0.1 shard_map.98.refs_2_.refs_1_
  23.8 1.1 %collective-permute-start.5 = (bf16[2,256,256]{2,1,0:T(8,128)(2,1)S(1)}, bf16[2,256,256]{2,1,0:T(8,128)(2,1)S(1)}, u32[]{:S(2)}, u32[]{:S(2)}) collective-permute-start(bf16[2,256,256]{2,1,0:T(8,128)(2,1)S(1)} %shard_map.98.refs_2_.refs_1_), channel_id=1, source_target_pairs={{0,16},{16,0},{32,48},{48,32},{64,80},{80,64},{96,112},{112,96},{1... | collective-permute-start | bytes 786440 | tf_op jit(solution)/shard_map/ppermute | solution.py:282
  24.9 1.2 %collective-permute-done.5.refs_3_ = bf16[2,256,256]{2,1,0:T(8,128)(2,1)S(1)} collective-permute-done((bf16[2,256,256]{2,1,0:T(8,128)(2,1)S(1)}, bf16[2,256,256]{2,1,0:T(8,128)(2,1)S(1)}, u32[]{:S(2)}, u32[]{:S(2)}) %collective-permute-start.5) | collective-permute-done | bytes 262176 | tf_op jit(solution)/shard_map/ppermute | solution.py:282
  26.1 0.4 shard_map.99
  26.5 1.4 %collective-permute-start.8 = (bf16[128,1024]{1,0:T(8,128)(2,1)S(1)}, bf16[128,1024]{1,0:T(8,128)(2,1)S(1)}, u32[]{:S(2)}, u32[]{:S(2)}) collective-permute-start(bf16[128,1024]{1,0:T(8,128)(2,1)S(1)} %get-tuple-element.42), channel_id=1, source_target_pairs={{0,1},{1,0},{2,3},{3,2},{4,5},{5,4},{6,7},{7,6},{8,9},{9,8},{10,11... | collective-permute-start | bytes 786440 | tf_op jit(solution)/shard_map/ppermute | solution.py:364
  27.9 1.9 %collective-permute-start.9 = (bf16[128,1024]{1,0:T(8,128)(2,1)S(1)}, bf16[128,1024]{1,0:T(8,128)(2,1)S(1)}, u32[]{:S(2)}, u32[]{:S(2)}) collective-permute-start(bf16[128,1024]{1,0:T(8,128)(2,1)S(1)} %get-tuple-element.43), channel_id=1, source_target_pairs={{0,3},{1,2},{2,1},{3,0},{4,7},{5,6},{6,5},{7,4},{8,11},{9,10},{10,... | collective-permute-start | bytes 786440 | tf_op jit(solution)/shard_map/ppermute | solution.py:364
  29.8 0.7 collective-permute-start.10
  30.5 0.6 shard_map.100
  31.1 1.5 %collective-permute-start.6 = (bf16[2,256,256]{2,1,0:T(8,128)(2,1)S(1)}, bf16[2,256,256]{2,1,0:T(8,128)(2,1)S(1)}, u32[]{:S(2)}, u32[]{:S(2)}) collective-permute-start(bf16[2,256,256]{2,1,0:T(8,128)(2,1)S(1)} %get-tuple-element.40), channel_id=1, source_target_pairs={{0,4},{4,0},{8,12},{12,8},{1,5},{5,1},{9,13},{13,9},{2,6},{6,2},{1... | collective-permute-start | bytes 786440 | tf_op jit(solution)/shard_map/ppermute | solution.py:373
  32.6 1.8 %collective-permute-start.7 = (bf16[2,256,256]{2,1,0:T(8,128)(2,1)S(1)}, bf16[2,256,256]{2,1,0:T(8,128)(2,1)S(1)}, u32[]{:S(2)}, u32[]{:S(2)}) collective-permute-start(bf16[2,256,256]{2,1,0:T(8,128)(2,1)S(1)} %get-tuple-element.41), channel_id=1, source_target_pairs={{0,12},{4,8},{8,4},{12,0},{1,13},{5,9},{9,5},{13,1},{2,14},{6,10},... | collective-permute-start | bytes 786440 | tf_op jit(solution)/shard_map/ppermute | solution.py:373
  34.4 0.0 collective-permute-done.8.refs_1_
  34.5 5.8 %collective-permute-done.9.refs_2_ = bf16[128,1024]{1,0:T(8,128)(2,1)S(1)} collective-permute-done((bf16[128,1024]{1,0:T(8,128)(2,1)S(1)}, bf16[128,1024]{1,0:T(8,128)(2,1)S(1)}, u32[]{:S(2)}, u32[]{:S(2)}) %collective-permute-start.9) | collective-permute-done | bytes 262176 | tf_op jit(solution)/shard_map/ppermute | solution.py:364
  40.3 1.9 %collective-permute-done.10.refs_3_ = bf16[128,1024]{1,0:T(8,128)(2,1)S(1)} collective-permute-done((bf16[128,1024]{1,0:T(8,128)(2,1)S(1)}, bf16[128,1024]{1,0:T(8,128)(2,1)S(1)}, u32[]{:S(2)}, u32[]{:S(2)}) %collective-permute-start.10) | collective-permute-done | bytes 262176 | tf_op jit(solution)/shard_map/ppermute | solution.py:364
  42.2 0.1 shard_map.101
  42.3 0.1 collective-permute-start.11
  42.4 2.5 %collective-permute-start.12 = (bf16[32,1024]{1,0:T(8,128)(2,1)S(1)}, bf16[32,1024]{1,0:T(8,128)(2,1)S(1)}, u32[]{:S(2)}, u32[]{:S(2)}) collective-permute-start(bf16[32,1024]{1,0:T(8,128)(2,1)S(1)} %get-tuple-element.47), channel_id=1, source_target_pairs={{0,96},{16,112},{32,64},{48,80},{64,32},{80,48},{96,0},{112,16},{1... | collective-permute-start | bytes 196616 | tf_op jit(solution)/shard_map/ppermute | solution.py:381
  44.9 0.2 collective-permute-start.13
  45.1 4.7 %collective-permute-done.11.refs_1_ = bf16[32,1024]{1,0:T(8,128)(2,1)S(1)} collective-permute-done((bf16[32,1024]{1,0:T(8,128)(2,1)S(1)}, bf16[32,1024]{1,0:T(8,128)(2,1)S(1)}, u32[]{:S(2)}, u32[]{:S(2)}) %collective-permute-start.11) | collective-permute-done | bytes 65568 | tf_op jit(solution)/shard_map/ppermute | solution.py:381
  49.8 0.0 collective-permute-done.12.refs_2_
  49.8 0.5 collective-permute-done.13.refs_3_
  50.3 2.6 %collective-permute-start.14 = (bf16[32,1024]{1,0:T(8,128)(2,1)S(1)}, bf16[32,1024]{1,0:T(8,128)(2,1)S(1)}, u32[]{:S(2)}, u32[]{:S(2)}) collective-permute-start(bf16[32,1024]{1,0:T(8,128)(2,1)S(1)} %shard_map.102.refs_0_), channel_id=1, source_target_pairs={{0,128},{16,144},{32,160},{48,176},{64,192},{80,208},{96,224},{112... | collective-permute-start | bytes 196616 | tf_op jit(solution)/shard_map/ppermute | solution.py:383
  53.0 4.6 %collective-permute-done.14.refs_1_ = bf16[32,1024]{1,0:T(8,128)(2,1)S(1)} collective-permute-done((bf16[32,1024]{1,0:T(8,128)(2,1)S(1)}, bf16[32,1024]{1,0:T(8,128)(2,1)S(1)}, u32[]{:S(2)}, u32[]{:S(2)}) %collective-permute-start.14) | collective-permute-done | bytes 65568 | tf_op jit(solution)/shard_map/ppermute | solution.py:383
  57.5 3.1 %collective-permute-start.17 = (bf16[32,1024]{1,0:T(8,128)(2,1)S(1)}, bf16[32,1024]{1,0:T(8,128)(2,1)S(1)}, u32[]{:S(2)}, u32[]{:S(2)}) collective-permute-start(bf16[32,1024]{1,0:T(8,128)(2,1)S(1)} %shard_map.103.refs_0_), channel_id=1, source_target_pairs={{0,64},{16,80},{32,96},{48,112},{64,0},{80,16},{96,32},{112,48},{1... | collective-permute-start | bytes 196616 | tf_op jit(solution)/shard_map/ppermute | solution.py:385
  60.7 0.4 collective-permute-start.16
  61.1 0.0 collective-permute-start.15
  61.1 0.0 collective-permute-done.6.refs_4_.refs_1_
  61.1 1.9 %collective-permute-done.17.refs_3_ = bf16[32,1024]{1,0:T(8,128)(2,1)S(1)} collective-permute-done((bf16[32,1024]{1,0:T(8,128)(2,1)S(1)}, bf16[32,1024]{1,0:T(8,128)(2,1)S(1)}, u32[]{:S(2)}, u32[]{:S(2)}) %collective-permute-start.17) | collective-permute-done | bytes 65568 | tf_op jit(solution)/shard_map/ppermute | solution.py:385
  63.0 3.0 %collective-permute-done.16.refs_2_ = bf16[32,1024]{1,0:T(8,128)(2,1)S(1)} collective-permute-done((bf16[32,1024]{1,0:T(8,128)(2,1)S(1)}, bf16[32,1024]{1,0:T(8,128)(2,1)S(1)}, u32[]{:S(2)}, u32[]{:S(2)}) %collective-permute-start.16) | collective-permute-done | bytes 65568 | tf_op jit(solution)/shard_map/ppermute | solution.py:385
  66.0 0.0 collective-permute-done.15.refs_1_
  66.0 0.1 collective-permute-start.21
  66.1 0.9 %collective-permute-start.20 = (bf16[128,1024]{1,0:T(8,128)(2,1)S(1)}, bf16[128,1024]{1,0:T(8,128)(2,1)S(1)}, u32[]{:S(2)}, u32[]{:S(2)}) collective-permute-start(bf16[128,1024]{1,0:T(8,128)(2,1)S(1)} %shard_map.104.refs_4_.refs_0_), channel_id=1, source_target_pairs={{0,3},{1,2},{2,1},{3,0},{4,7},{5,6},{6,5},{7,4},{8,11},{9,10},{10,... | collective-permute-start | bytes 786440 | tf_op jit(solution)/shard_map/ppermute | solution.py:393
  67.0 2.3 %collective-permute-start.19 = (bf16[128,1024]{1,0:T(8,128)(2,1)S(1)}, bf16[128,1024]{1,0:T(8,128)(2,1)S(1)}, u32[]{:S(2)}, u32[]{:S(2)}) collective-permute-start(bf16[128,1024]{1,0:T(8,128)(2,1)S(1)} %shard_map.104.refs_4_.refs_0_), channel_id=1, source_target_pairs={{0,2},{1,3},{2,0},{3,1},{4,6},{5,7},{6,4},{7,5},{8,10},{9,11},{10,... | collective-permute-start | bytes 786440 | tf_op jit(solution)/shard_map/ppermute | solution.py:393
  69.4 0.3 shard_map.105
  69.7 2.8 %collective-permute-start.18 = (bf16[2,256,256]{2,1,0:T(8,128)(2,1)S(1)}, bf16[2,256,256]{2,1,0:T(8,128)(2,1)S(1)}, u32[]{:S(2)}, u32[]{:S(2)}) collective-permute-start(bf16[2,256,256]{2,1,0:T(8,128)(2,1)S(1)} %shard_map.105), channel_id=1, source_target_pairs={{0,8},{4,12},{8,0},{12,4},{1,9},{5,13},{9,1},{13,5},{2,10},{6,14},... | collective-permute-start | bytes 786440 | tf_op jit(solution)/shard_map/ppermute | solution.py:401
  72.5 3.7 %collective-permute-start.22 = (bf16[128,1024]{1,0:T(8,128)(2,1)S(1)}, bf16[128,1024]{1,0:T(8,128)(2,1)S(1)}, u32[]{:S(2)}, u32[]{:S(2)}) collective-permute-start(bf16[128,1024]{1,0:T(8,128)(2,1)S(1)} %shard_map.104.refs_4_.refs_0_), channel_id=1, source_target_pairs={{0,16},{16,0},{32,48},{48,32},{64,80},{80,64},{96,112},{112,96},{1... | collective-permute-start | bytes 786440 | tf_op jit(solution)/shard_map/ppermute | solution.py:282
  76.3 0.0 collective-permute-done.21.refs_3_
  76.3 1.4 %collective-permute-start.25 = (bf16[128,1024]{1,0:T(8,128)(2,1)S(1)}, bf16[128,1024]{1,0:T(8,128)(2,1)S(1)}, u32[]{:S(2)}, u32[]{:S(2)}) collective-permute-start(bf16[128,1024]{1,0:T(8,128)(2,1)S(1)} %collective-permute-done.21.refs_3_), channel_id=1, source_target_pairs={{0,16},{16,0},{32,48},{48,32},{64,80},{80,64},{96,112},{112,96},{1... | collective-permute-start | bytes 786440 | tf_op jit(solution)/shard_map/ppermute | solution.py:282
  77.7 4.1 %collective-permute-start.24 = (bf16[128,1024]{1,0:T(8,128)(2,1)S(1)}, bf16[128,1024]{1,0:T(8,128)(2,1)S(1)}, u32[]{:S(2)}, u32[]{:S(2)}) collective-permute-start(bf16[128,1024]{1,0:T(8,128)(2,1)S(1)} %collective-permute-done.20.refs_2_), channel_id=1, source_target_pairs={{0,16},{16,0},{32,48},{48,32},{64,80},{80,64},{96,112},{112,96},{1... | collective-permute-start | bytes 786440 | tf_op jit(solution)/shard_map/ppermute | solution.py:282
  81.8 0.0 collective-permute-start.23
  81.8 0.0 collective-permute-done.18.refs_3_
  81.8 0.8 shard_map.106
  82.6 0.3 collective-permute-done.24.refs_6_
  82.9 0.4 collective-permute-done.23.refs_5_
  83.3 2.2 %shard_map.107 = (f32[3,1024,256]{2,1,0:T(8,128)}, f32[256,1024]{1,0:T(8,128)}) custom-call(bf16[128,1024]{1,0:T(8,128)(2,1)S(1)} %shard_map.104.refs_4_.refs_0_, bf16[128,1024]{1,0:T(8,128)(2,1)S(1)} %collective-permute-done.19.refs_1_, bf16[128,1024]{1,0:T(8,128)(2,1)S(1)} %collective-permute-done.20.refs_2_, ...), custom_call_target="tpu_custom_call" | custom-call | flops 1048576 | bytes 6291456 | tf_op jit(solution)/shard_map/pallas_call | solution.py:32
  (12 shorter events, 0.1 us)
Async XLA Ops:
  2.7 14.9 %copy-start.1 = (bf16[1,256,1024]{2,1,0:T(8,128)(2,1)S(1)}, bf16[1,256,1024]{2,1,0:T(8,128)(2,1)}, u32[]{:S(2)}) copy-start(bf16[1,256,1024]{2,1,0:T(8,128)(2,1)} %param.6) | copy-start | bytes 1572868
  2.7 14.9 %copy-start.3 = (bf16[1,256,1024]{2,1,0:T(8,128)(2,1)S(1)}, bf16[1,256,1024]{2,1,0:T(8,128)(2,1)}, u32[]{:S(2)}) copy-start(bf16[1,256,1024]{2,1,0:T(8,128)(2,1)} %param.11) | copy-start | bytes 1572868
  2.7 11.2 %collective-permute-start.1 = (bf16[2,256,256]{2,1,0:T(8,128)(2,1)S(1)}, bf16[2,256,256]{2,1,0:T(8,128)(2,1)S(1)}, u32[]{:S(2)}, u32[]{:S(2)}) collective-permute-start(bf16[2,256,256]{2,1,0:T(8,128)(2,1)S(1)} %shard_map.93.refs_5_.refs_3_), channel_id=1, source_target_pairs={{0,240},{16,32},{32,16},{48,64},{64,48},{80,96},{96,80},{112,128},... | collective-permute-start | bytes 786440 | tf_op jit(solution)/shard_map/ppermute | solution.py:321
  5.8 8.1 %collective-permute-start = (bf16[2,256,256]{2,1,0:T(8,128)(2,1)S(1)}, bf16[2,256,256]{2,1,0:T(8,128)(2,1)S(1)}, u32[]{:S(2)}, u32[]{:S(2)}) collective-permute-start(bf16[2,256,256]{2,1,0:T(8,128)(2,1)S(1)} %shard_map.93.refs_5_.refs_3_), channel_id=1, source_target_pairs={{0,16},{16,0},{32,48},{48,32},{64,80},{80,64},{96,112},{112,96},{1... | collective-permute-start | bytes 786440 | tf_op jit(solution)/shard_map/ppermute | solution.py:282
  13.8 4.6 %collective-permute-start.4 = (bf16[2,512,256]{2,1,0:T(8,128)(2,1)}, bf16[2,512,256]{2,1,0:T(8,128)(2,1)S(1)}, u32[]{:S(2)}, u32[]{:S(2)}) collective-permute-start(bf16[2,512,256]{2,1,0:T(8,128)(2,1)} %get-tuple-element.35), channel_id=1, source_target_pairs={{0,16},{16,0},{32,48},{48,32},{64,80},{80,64},{96,112},{112,96},{1... | collective-permute-start | bytes 1572872 | tf_op jit(solution)/shard_map/ppermute | solution.py:282
  17.1 2.1 %collective-permute-start.3 = (bf16[4,256,256]{2,1,0:T(8,128)(2,1)S(1)}, bf16[4,256,256]{2,1,0:T(8,128)(2,1)S(1)}, u32[]{:S(2)}, u32[]{:S(2)}) collective-permute-start(bf16[4,256,256]{2,1,0:T(8,128)(2,1)S(1)} %get-tuple-element.32.refs_2_.refs_0_), channel_id=1, source_target_pairs={{0,16},{16,0},{32,48},{48,32},{64,80},{80,64},{96,112},{112,96},{1... | collective-permute-start | bytes 1572872 | tf_op jit(solution)/shard_map/ppermute | solution.py:282
  17.6 6.1 %collective-permute-start.2 = (bf16[2,256,256]{2,1,0:T(8,128)(2,1)S(1)}, bf16[2,256,256]{2,1,0:T(8,128)(2,1)S(1)}, u32[]{:S(2)}, u32[]{:S(2)}) collective-permute-start(bf16[2,256,256]{2,1,0:T(8,128)(2,1)S(1)} %get-tuple-element.34), channel_id=1, source_target_pairs={{0,240},{16,32},{32,16},{48,64},{64,48},{80,96},{96,80},{112,128},... | collective-permute-start | bytes 786440 | tf_op jit(solution)/shard_map/ppermute | solution.py:336
  18.4 12.1 %copy-start = (bf16[3,1024,256]{2,1,0:T(8,128)(2,1)S(1)}, bf16[3,1024,256]{2,1,0:T(8,128)(2,1)}, u32[]{:S(2)}) copy-start(bf16[3,1024,256]{2,1,0:T(8,128)(2,1)} %refs_3_.3) | copy-start | bytes 4718596
  18.4 12.1 %copy-start.2 = (bf16[256,1024]{1,0:T(8,128)(2,1)S(1)}, bf16[256,1024]{1,0:T(8,128)(2,1)}, u32[]{:S(2)}) copy-start(bf16[256,1024]{1,0:T(8,128)(2,1)} %refs_2_.5) | copy-start | bytes 1572868
  23.8 2.3 %collective-permute-start.5 = (bf16[2,256,256]{2,1,0:T(8,128)(2,1)S(1)}, bf16[2,256,256]{2,1,0:T(8,128)(2,1)S(1)}, u32[]{:S(2)}, u32[]{:S(2)}) collective-permute-start(bf16[2,256,256]{2,1,0:T(8,128)(2,1)S(1)} %shard_map.98.refs_2_.refs_1_), channel_id=1, source_target_pairs={{0,16},{16,0},{32,48},{48,32},{64,80},{80,64},{96,112},{112,96},{1... | collective-permute-start | bytes 786440 | tf_op jit(solution)/shard_map/ppermute | solution.py:282
  26.5 7.9 %collective-permute-start.8 = (bf16[128,1024]{1,0:T(8,128)(2,1)S(1)}, bf16[128,1024]{1,0:T(8,128)(2,1)S(1)}, u32[]{:S(2)}, u32[]{:S(2)}) collective-permute-start(bf16[128,1024]{1,0:T(8,128)(2,1)S(1)} %get-tuple-element.42), channel_id=1, source_target_pairs={{0,1},{1,0},{2,3},{3,2},{4,5},{5,4},{6,7},{7,6},{8,9},{9,8},{10,11... | collective-permute-start | bytes 786440 | tf_op jit(solution)/shard_map/ppermute | solution.py:364
  27.9 12.4 %collective-permute-start.9 = (bf16[128,1024]{1,0:T(8,128)(2,1)S(1)}, bf16[128,1024]{1,0:T(8,128)(2,1)S(1)}, u32[]{:S(2)}, u32[]{:S(2)}) collective-permute-start(bf16[128,1024]{1,0:T(8,128)(2,1)S(1)} %get-tuple-element.43), channel_id=1, source_target_pairs={{0,3},{1,2},{2,1},{3,0},{4,7},{5,6},{6,5},{7,4},{8,11},{9,10},{10,... | collective-permute-start | bytes 786440 | tf_op jit(solution)/shard_map/ppermute | solution.py:364
  29.8 12.4 %collective-permute-start.10 = (bf16[128,1024]{1,0:T(8,128)(2,1)S(1)}, bf16[128,1024]{1,0:T(8,128)(2,1)S(1)}, u32[]{:S(2)}, u32[]{:S(2)}) collective-permute-start(bf16[128,1024]{1,0:T(8,128)(2,1)S(1)} %get-tuple-element.44), channel_id=1, source_target_pairs={{0,2},{1,3},{2,0},{3,1},{4,6},{5,7},{6,4},{7,5},{8,10},{9,11},{10,... | collective-permute-start | bytes 786440 | tf_op jit(solution)/shard_map/ppermute | solution.py:364
  31.1 29.9 %collective-permute-start.6 = (bf16[2,256,256]{2,1,0:T(8,128)(2,1)S(1)}, bf16[2,256,256]{2,1,0:T(8,128)(2,1)S(1)}, u32[]{:S(2)}, u32[]{:S(2)}) collective-permute-start(bf16[2,256,256]{2,1,0:T(8,128)(2,1)S(1)} %get-tuple-element.40), channel_id=1, source_target_pairs={{0,4},{4,0},{8,12},{12,8},{1,5},{5,1},{9,13},{13,9},{2,6},{6,2},{1... | collective-permute-start | bytes 786440 | tf_op jit(solution)/shard_map/ppermute | solution.py:373
  32.6 28.4 %collective-permute-start.7 = (bf16[2,256,256]{2,1,0:T(8,128)(2,1)S(1)}, bf16[2,256,256]{2,1,0:T(8,128)(2,1)S(1)}, u32[]{:S(2)}, u32[]{:S(2)}) collective-permute-start(bf16[2,256,256]{2,1,0:T(8,128)(2,1)S(1)} %get-tuple-element.41), channel_id=1, source_target_pairs={{0,12},{4,8},{8,4},{12,0},{1,13},{5,9},{9,5},{13,1},{2,14},{6,10},... | collective-permute-start | bytes 786440 | tf_op jit(solution)/shard_map/ppermute | solution.py:373
  42.3 7.5 %collective-permute-start.11 = (bf16[32,1024]{1,0:T(8,128)(2,1)S(1)}, bf16[32,1024]{1,0:T(8,128)(2,1)S(1)}, u32[]{:S(2)}, u32[]{:S(2)}) collective-permute-start(bf16[32,1024]{1,0:T(8,128)(2,1)S(1)} %get-tuple-element.46), channel_id=1, source_target_pairs={{0,64},{16,80},{32,96},{48,112},{64,0},{80,16},{96,32},{112,48},{1... | collective-permute-start | bytes 196616 | tf_op jit(solution)/shard_map/ppermute | solution.py:381
  42.4 7.4 %collective-permute-start.12 = (bf16[32,1024]{1,0:T(8,128)(2,1)S(1)}, bf16[32,1024]{1,0:T(8,128)(2,1)S(1)}, u32[]{:S(2)}, u32[]{:S(2)}) collective-permute-start(bf16[32,1024]{1,0:T(8,128)(2,1)S(1)} %get-tuple-element.47), channel_id=1, source_target_pairs={{0,96},{16,112},{32,64},{48,80},{64,32},{80,48},{96,0},{112,16},{1... | collective-permute-start | bytes 196616 | tf_op jit(solution)/shard_map/ppermute | solution.py:381
  44.9 5.4 %collective-permute-start.13 = (bf16[32,1024]{1,0:T(8,128)(2,1)S(1)}, bf16[32,1024]{1,0:T(8,128)(2,1)S(1)}, u32[]{:S(2)}, u32[]{:S(2)}) collective-permute-start(bf16[32,1024]{1,0:T(8,128)(2,1)S(1)} %get-tuple-element.48), channel_id=1, source_target_pairs={{0,32},{16,48},{32,0},{48,16},{64,96},{80,112},{96,64},{112,80},{1... | collective-permute-start | bytes 196616 | tf_op jit(solution)/shard_map/ppermute | solution.py:381
  50.3 7.2 %collective-permute-start.14 = (bf16[32,1024]{1,0:T(8,128)(2,1)S(1)}, bf16[32,1024]{1,0:T(8,128)(2,1)S(1)}, u32[]{:S(2)}, u32[]{:S(2)}) collective-permute-start(bf16[32,1024]{1,0:T(8,128)(2,1)S(1)} %shard_map.102.refs_0_), channel_id=1, source_target_pairs={{0,128},{16,144},{32,160},{48,176},{64,192},{80,208},{96,224},{112... | collective-permute-start | bytes 196616 | tf_op jit(solution)/shard_map/ppermute | solution.py:383
  57.5 5.5 %collective-permute-start.17 = (bf16[32,1024]{1,0:T(8,128)(2,1)S(1)}, bf16[32,1024]{1,0:T(8,128)(2,1)S(1)}, u32[]{:S(2)}, u32[]{:S(2)}) collective-permute-start(bf16[32,1024]{1,0:T(8,128)(2,1)S(1)} %shard_map.103.refs_0_), channel_id=1, source_target_pairs={{0,64},{16,80},{32,96},{48,112},{64,0},{80,16},{96,32},{112,48},{1... | collective-permute-start | bytes 196616 | tf_op jit(solution)/shard_map/ppermute | solution.py:385
  60.7 5.4 %collective-permute-start.16 = (bf16[32,1024]{1,0:T(8,128)(2,1)S(1)}, bf16[32,1024]{1,0:T(8,128)(2,1)S(1)}, u32[]{:S(2)}, u32[]{:S(2)}) collective-permute-start(bf16[32,1024]{1,0:T(8,128)(2,1)S(1)} %shard_map.103.refs_0_), channel_id=1, source_target_pairs={{0,96},{16,112},{32,64},{48,80},{64,32},{80,48},{96,0},{112,16},{1... | collective-permute-start | bytes 196616 | tf_op jit(solution)/shard_map/ppermute | solution.py:385
  61.1 5.0 %collective-permute-start.15 = (bf16[32,1024]{1,0:T(8,128)(2,1)S(1)}, bf16[32,1024]{1,0:T(8,128)(2,1)S(1)}, u32[]{:S(2)}, u32[]{:S(2)}) collective-permute-start(bf16[32,1024]{1,0:T(8,128)(2,1)S(1)} %shard_map.103.refs_0_), channel_id=1, source_target_pairs={{0,32},{16,48},{32,0},{48,16},{64,96},{80,112},{96,64},{112,80},{1... | collective-permute-start | bytes 196616 | tf_op jit(solution)/shard_map/ppermute | solution.py:385
  66.0 10.2 %collective-permute-start.21 = (bf16[128,1024]{1,0:T(8,128)(2,1)S(1)}, bf16[128,1024]{1,0:T(8,128)(2,1)S(1)}, u32[]{:S(2)}, u32[]{:S(2)}) collective-permute-start(bf16[128,1024]{1,0:T(8,128)(2,1)S(1)} %shard_map.104.refs_4_.refs_0_), channel_id=1, source_target_pairs={{0,1},{1,0},{2,3},{3,2},{4,5},{5,4},{6,7},{7,6},{8,9},{9,8},{10,11... | collective-permute-start | bytes 786440 | tf_op jit(solution)/shard_map/ppermute | solution.py:393
  66.1 11.5 %collective-permute-start.20 = (bf16[128,1024]{1,0:T(8,128)(2,1)S(1)}, bf16[128,1024]{1,0:T(8,128)(2,1)S(1)}, u32[]{:S(2)}, u32[]{:S(2)}) collective-permute-start(bf16[128,1024]{1,0:T(8,128)(2,1)S(1)} %shard_map.104.refs_4_.refs_0_), channel_id=1, source_target_pairs={{0,3},{1,2},{2,1},{3,0},{4,7},{5,6},{6,5},{7,4},{8,11},{9,10},{10,... | collective-permute-start | bytes 786440 | tf_op jit(solution)/shard_map/ppermute | solution.py:393
  67.0 14.7 %collective-permute-start.19 = (bf16[128,1024]{1,0:T(8,128)(2,1)S(1)}, bf16[128,1024]{1,0:T(8,128)(2,1)S(1)}, u32[]{:S(2)}, u32[]{:S(2)}) collective-permute-start(bf16[128,1024]{1,0:T(8,128)(2,1)S(1)} %shard_map.104.refs_4_.refs_0_), channel_id=1, source_target_pairs={{0,2},{1,3},{2,0},{3,1},{4,6},{5,7},{6,4},{7,5},{8,10},{9,11},{10,... | collective-permute-start | bytes 786440 | tf_op jit(solution)/shard_map/ppermute | solution.py:393
  69.7 12.1 %collective-permute-start.18 = (bf16[2,256,256]{2,1,0:T(8,128)(2,1)S(1)}, bf16[2,256,256]{2,1,0:T(8,128)(2,1)S(1)}, u32[]{:S(2)}, u32[]{:S(2)}) collective-permute-start(bf16[2,256,256]{2,1,0:T(8,128)(2,1)S(1)} %shard_map.105), channel_id=1, source_target_pairs={{0,8},{4,12},{8,0},{12,4},{1,9},{5,13},{9,1},{13,5},{2,10},{6,14},... | collective-permute-start | bytes 786440 | tf_op jit(solution)/shard_map/ppermute | solution.py:401
  72.5 10.1 %collective-permute-start.22 = (bf16[128,1024]{1,0:T(8,128)(2,1)S(1)}, bf16[128,1024]{1,0:T(8,128)(2,1)S(1)}, u32[]{:S(2)}, u32[]{:S(2)}) collective-permute-start(bf16[128,1024]{1,0:T(8,128)(2,1)S(1)} %shard_map.104.refs_4_.refs_0_), channel_id=1, source_target_pairs={{0,16},{16,0},{32,48},{48,32},{64,80},{80,64},{96,112},{112,96},{1... | collective-permute-start | bytes 786440 | tf_op jit(solution)/shard_map/ppermute | solution.py:282
  76.3 6.3 %collective-permute-start.25 = (bf16[128,1024]{1,0:T(8,128)(2,1)S(1)}, bf16[128,1024]{1,0:T(8,128)(2,1)S(1)}, u32[]{:S(2)}, u32[]{:S(2)}) collective-permute-start(bf16[128,1024]{1,0:T(8,128)(2,1)S(1)} %collective-permute-done.21.refs_3_), channel_id=1, source_target_pairs={{0,16},{16,0},{32,48},{48,32},{64,80},{80,64},{96,112},{112,96},{1... | collective-permute-start | bytes 786440 | tf_op jit(solution)/shard_map/ppermute | solution.py:282
  77.7 5.3 %collective-permute-start.24 = (bf16[128,1024]{1,0:T(8,128)(2,1)S(1)}, bf16[128,1024]{1,0:T(8,128)(2,1)S(1)}, u32[]{:S(2)}, u32[]{:S(2)}) collective-permute-start(bf16[128,1024]{1,0:T(8,128)(2,1)S(1)} %collective-permute-done.20.refs_2_), channel_id=1, source_target_pairs={{0,16},{16,0},{32,48},{48,32},{64,80},{80,64},{96,112},{112,96},{1... | collective-permute-start | bytes 786440 | tf_op jit(solution)/shard_map/ppermute | solution.py:282
  81.8 1.5 %collective-permute-start.23 = (bf16[128,1024]{1,0:T(8,128)(2,1)S(1)}, bf16[128,1024]{1,0:T(8,128)(2,1)S(1)}, u32[]{:S(2)}, u32[]{:S(2)}) collective-permute-start(bf16[128,1024]{1,0:T(8,128)(2,1)S(1)} %collective-permute-done.19.refs_1_), channel_id=1, source_target_pairs={{0,16},{16,0},{32,48},{48,32},{64,80},{80,64},{96,112},{112,96},{1... | collective-permute-start | bytes 786440 | tf_op jit(solution)/shard_map/ppermute | solution.py:282

commit v7 on v5

--- a/solution.py
+++ b/solution.py
@@ -364,22 +364,23 @@
     from_y = [lax.ppermute(to_y[k - 1], "dp", pair(k)) for k in (1, 3, 2)]
 
     head_own, *to_head = call(
-        functools.partial(head_kernel, parts=(0, 1, 3)),
-        [shape((2, ROWS, WIDTH), F32)] + [shape((2, ROWS, WIDTH), BF)] * 2,
+        functools.partial(head_kernel, parts=(0, 1, 3, 2)),
+        [shape((2, ROWS, WIDTH), F32)] + [shape((2, ROWS, WIDTH), BF)] * 3,
         [acts, dkv, w_out, w_qkv],
-        6 * ROWS * WIDTH * D,
+        8 * ROWS * WIDTH * D,
         after=[own],
     )
-    from_head = [lax.ppermute(a, "head", pair(k)) for k, a in zip((1, 3), to_head)]
+    from_head = [lax.ppermute(a, "head", pair(k)) for k, a in zip((1, 3, 2), to_head)]
 
     own, *to_z = call(
         ysum_kernel,
         [shape((32, D), F32)] + [shape((32, D), BF)] * 3,
         [own] + from_y,
         2**20,
+        after=from_head[:2],
     )
     from_z = [lax.ppermute(to_z[m - 1], "spatial", pair_z(m)) for m in (2, 3, 1)]
-    part = call(sum_kernel, [shape((32, D), BF)], [own] + from_z, 2**18)[0]
+    part = call(sum_kernel, [shape((32, D), BF)], [own] + from_z, 2**18, after=from_head[2:])[0]
     far_part = lax.ppermute(part, "spatial", pair_z(4))
     chunk = call(sum_kernel, [shape((32, D), BF)], [part, far_part], 2**16)[0]
     pieces = [chunk] + [lax.ppermute(chunk, "spatial", pair_z(m)) for m in (1, 3, 2)]
@@ -388,17 +389,8 @@
         [shape((128, D), BF)],
         pieces,
         2**16,
-        after=from_head,
     )[0]
     mine = [column] + [lax.ppermute(column, "dp", pair(k)) for k in PLACE_ORDER[1:]]
-    last = call(
-        functools.partial(head_kernel, parts=(2,)),
-        [shape((2, ROWS, WIDTH), BF)],
-        [acts, dkv, w_out, w_qkv],
-        2 * ROWS * WIDTH * D,
-        after=[column],
-    )[0]
-    from_head.append(lax.ppermute(last, "head", pair(2)))
     layer_out, grad_tokens, token = call(
         head_sum_kernel,
         [shape((ROWS, WIDTH), BF)] * 2 + [shape((8, 128), F32)],

time: 85.9 us -> 90.7 us (1.056)
  starting transfers between devices: 40.3 us -> 48.6 us
  waiting for transfers between devices: 29.2 us -> 25.8 us
    ppermute x8, starting transfers between devices: 14.8 us -> 23.5 us  [swapped(): return lax.ppermute(a, 'spatial', swap)]
    ppermute x3, waiting for transfers between devices: 5.18 us -> 2.25 us  [per_device(): lax.ppermute(to_z[m - 1], 'spatial', pair_z(m))]
    ppermute x1 -> x0, starting transfers between devices: 2.84 us -> none  [per_device(): from_head.append(lax.ppermute(last, 'head', pair(2)))]
    ppermute x3, waiting for transfers between devices: 7.76 us -> 5.32 us  [per_device(): from_y = [lax.ppermute(to_y[k - 1], 'dp', pair(k)) for k in (1, 3, 2)]]
    ppermute x2 -> x3, starting transfers between devices: 3.29 us -> 5.6 us  [per_device(): lax.ppermute(a, 'head', pair(k))]
    ppermute x2 -> x3, waiting for transfers between devices: 0.01 us -> 1.18 us  [per_device(): lax.ppermute(a, 'head', pair(k))]
    ppermute x3, waiting for transfers between devices: 4.94 us -> 5.89 us  [per_device(): lax.ppermute(chunk, 'spatial', pair_z(m))]
    pallas_call x15 -> x14, Pallas kernels: 14.6 us -> 14.4 us  [call(): pl.pallas_call(body, out_shape=outs, in_specs=(in_specs or [VMEM] * count...]
  transfers between devices with their start and end apart: 26 -> 26, of which waited for: 12 -> 13; matrix products, arithmetic and copies ran while one was open for 1% -> 1% of each run, Pallas kernels for 11% -> 10%
where the time goes in v7:
time: 90.7 us; the launch traced here: 90.5 us
  starting transfers between devices  48.6 us (54%)
  waiting for transfers between devices  25.8 us (28%)
  Pallas kernels  14.4 us (16%)
  between operations  0.97 us (1%)
    ppermute x8, starting transfers between devices, swapped(): return lax.ppermute(a, 'spatial', swap)  23.5 us
    pallas_call x14, Pallas kernels, call(): pl.pallas_call(body, out_shape=outs, in_specs=(in_specs or [VMEM] * count...  14.4 us
    ppermute x3, waiting for transfers between devices, per_device(): lax.ppermute(chunk, 'spatial', pair_z(m))  5.89 us
    ppermute x3, starting transfers between devices, per_device(): lax.ppermute(a, 'head', pair(k))  5.6 us
    ppermute x3, waiting for transfers between devices, per_device(): from_y = [lax.ppermute(to_y[k - 1], 'dp', pair(k)) for k in (1, 3, 2)]  5.32 us
    ppermute x1, waiting for transfers between devices, per_device(): far_part = lax.ppermute(part, 'spatial', pair_z(4))  4.39 us
    ppermute x1, waiting for transfers between devices, per_device(): from_far = lax.ppermute(grad_far, 'spatial', cross)  4.11 us
    ppermute x3, starting transfers between devices, per_device(): from_y = [lax.ppermute(to_y[k - 1], 'dp', pair(k)) for k in (1, 3, 2)]  4.01 us
  transfers between devices with their start and end apart: 26, of which 13 were waited for; matrix products, arithmetic and copies ran while one was open for 1% of the time, Pallas kernels for 10%

profile of v7, /device:TPU:1, one launch (start us, length us, event | category | flops | bytes accessed | tf_op | source)
XLA Modules:
  0.0 90.5 jit_solution(6573982683675639503)
XLA Ops:
  0.6 2.1 %shard_map.93.refs_5_.refs_3_ = bf16[2,256,256]{2,1,0:T(8,128)(2,1)S(1)} custom-call(bf16[256,1024]{1,0:T(8,128)(2,1)} %bitcast.5, bf16[3,1024,256]{2,1,0:T(8,128)(2,1)} %refs_3_.1), custom_call_target="tpu_custom_call" | custom-call | flops 268435456 | bytes 2359296 | tf_op jit(solution)/shard_map/pallas_call | solution.py:32
  2.7 0.0 copy-start.1
  2.7 0.0 copy-start.2
  2.7 3.1 %collective-permute-start.1 = (bf16[2,256,256]{2,1,0:T(8,128)(2,1)S(1)}, bf16[2,256,256]{2,1,0:T(8,128)(2,1)S(1)}, u32[]{:S(2)}, u32[]{:S(2)}) collective-permute-start(bf16[2,256,256]{2,1,0:T(8,128)(2,1)S(1)} %shard_map.93.refs_5_.refs_3_), channel_id=1, source_target_pairs={{0,240},{16,32},{32,16},{48,64},{64,48},{80,96},{96,80},{112,128},... | collective-permute-start | bytes 786440 | tf_op jit(solution)/shard_map/ppermute | solution.py:321
  5.8 3.8 %collective-permute-start = (bf16[2,256,256]{2,1,0:T(8,128)(2,1)S(1)}, bf16[2,256,256]{2,1,0:T(8,128)(2,1)S(1)}, u32[]{:S(2)}, u32[]{:S(2)}) collective-permute-start(bf16[2,256,256]{2,1,0:T(8,128)(2,1)S(1)} %shard_map.93.refs_5_.refs_3_), channel_id=1, source_target_pairs={{0,16},{16,0},{32,48},{48,32},{64,80},{80,64},{96,112},{112,96},{1... | collective-permute-start | bytes 786440 | tf_op jit(solution)/shard_map/ppermute | solution.py:282
  9.6 0.7 pad_add_fusion.refs_4_
  10.3 3.5 %shard_map.94 = (bf16[256,256]{1,0:T(8,128)(2,1)S(1)}, bf16[256,256]{1,0:T(8,128)(2,1)S(1)}, bf16[2,512,256]{2,1,0:T(8,128)(2,1)}, f32[4,768]{1,0:T(4,128)S(1)}) custom-call(bf16[256,1024]{1,0:T(8,128)(2,1)} %bitcast.6, bf16[3,1024,256]{2,1,0:T(8,128)(2,1)} %refs_3_.1, bf16[256,1024]{1,0:T(8,128)(2,1)} %refs_2_.3, bf16[256,1024]{1,0:T(8,128)(2,1)} %bitcast.9, ...), custom_call_target="tpu_custom_call" | custom-call | flops 536870912 | bytes 3947008 | tf_op jit(solution)/shard_map/pallas_call | solution.py:32
  13.8 0.1 collective-permute-start.4
  13.9 0.0 collective-permute-done.1.refs_4_
  13.9 0.0 collective-permute-done.refs_2_
  13.9 3.1 %shard_map.95 = (bf16[4,256,256]{2,1,0:T(8,128)(2,1)S(1)}, bf16[2,256,256]{2,1,0:T(8,128)(2,1)S(1)}, f32[2,256,256]{2,1,0:T(8,128)S(1)}) custom-call(bf16[256,256]{1,0:T(8,128)(2,1)S(1)} %get-tuple-element.30.refs_0_, bf16[256,256]{1,0:T(8,128)(2,1)S(1)} %get-tuple-element.31.refs_1_, bf16[2,256,256]{2,1,0:T(8,128)(2,1)S(1)} %collective-permute-done.refs_2_, ...), custom_call_target="tpu_custom_call" | custom-call | flops 503316480 | bytes 2371584 | tf_op jit(solution)/shard_map/pallas_call | solution.py:32
  17.1 0.6 collective-permute-start.3
  17.6 0.7 shard_map.96.refs_0_
  18.4 0.0 copy-start
  18.4 0.0 copy-start.3
  18.4 0.7 collective-permute-done.3.refs_3_.refs_2_
  19.2 0.4 shard_map.97
  19.6 4.1 %collective-permute-done.2.refs_1_ = bf16[2,256,256]{2,1,0:T(8,128)(2,1)S(1)} collective-permute-done((bf16[2,256,256]{2,1,0:T(8,128)(2,1)S(1)}, bf16[2,256,256]{2,1,0:T(8,128)(2,1)S(1)}, u32[]{:S(2)}, u32[]{:S(2)}) %collective-permute-start.2) | collective-permute-done | bytes 262176 | tf_op jit(solution)/shard_map/ppermute | solution.py:336
  23.7 0.1 shard_map.98.refs_2_.refs_1_
  23.8 1.1 %collective-permute-start.5 = (bf16[2,256,256]{2,1,0:T(8,128)(2,1)S(1)}, bf16[2,256,256]{2,1,0:T(8,128)(2,1)S(1)}, u32[]{:S(2)}, u32[]{:S(2)}) collective-permute-start(bf16[2,256,256]{2,1,0:T(8,128)(2,1)S(1)} %shard_map.98.refs_2_.refs_1_), channel_id=1, source_target_pairs={{0,16},{16,0},{32,48},{48,32},{64,80},{80,64},{96,112},{112,96},{1... | collective-permute-start | bytes 786440 | tf_op jit(solution)/shard_map/ppermute | solution.py:282
  24.9 1.2 %collective-permute-done.5.refs_3_ = bf16[2,256,256]{2,1,0:T(8,128)(2,1)S(1)} collective-permute-done((bf16[2,256,256]{2,1,0:T(8,128)(2,1)S(1)}, bf16[2,256,256]{2,1,0:T(8,128)(2,1)S(1)}, u32[]{:S(2)}, u32[]{:S(2)}) %collective-permute-start.5) | collective-permute-done | bytes 262176 | tf_op jit(solution)/shard_map/ppermute | solution.py:282
  26.1 0.4 shard_map.99
  26.5 1.4 %collective-permute-start.9 = (bf16[128,1024]{1,0:T(8,128)(2,1)S(1)}, bf16[128,1024]{1,0:T(8,128)(2,1)S(1)}, u32[]{:S(2)}, u32[]{:S(2)}) collective-permute-start(bf16[128,1024]{1,0:T(8,128)(2,1)S(1)} %get-tuple-element.46), channel_id=1, source_target_pairs={{0,1},{1,0},{2,3},{3,2},{4,5},{5,4},{6,7},{7,6},{8,9},{9,8},{10,11... | collective-permute-start | bytes 786440 | tf_op jit(solution)/shard_map/ppermute | solution.py:364
  27.9 1.9 %collective-permute-start.10 = (bf16[128,1024]{1,0:T(8,128)(2,1)S(1)}, bf16[128,1024]{1,0:T(8,128)(2,1)S(1)}, u32[]{:S(2)}, u32[]{:S(2)}) collective-permute-start(bf16[128,1024]{1,0:T(8,128)(2,1)S(1)} %get-tuple-element.47), channel_id=1, source_target_pairs={{0,3},{1,2},{2,1},{3,0},{4,7},{5,6},{6,5},{7,4},{8,11},{9,10},{10,... | collective-permute-start | bytes 786440 | tf_op jit(solution)/shard_map/ppermute | solution.py:364
  29.8 0.7 collective-permute-start.11
  30.6 0.7 shard_map.100
  31.3 1.5 %collective-permute-start.6 = (bf16[2,256,256]{2,1,0:T(8,128)(2,1)S(1)}, bf16[2,256,256]{2,1,0:T(8,128)(2,1)S(1)}, u32[]{:S(2)}, u32[]{:S(2)}) collective-permute-start(bf16[2,256,256]{2,1,0:T(8,128)(2,1)S(1)} %get-tuple-element.41), channel_id=1, source_target_pairs={{0,4},{4,0},{8,12},{12,8},{1,5},{5,1},{9,13},{13,9},{2,6},{6,2},{1... | collective-permute-start | bytes 786440 | tf_op jit(solution)/shard_map/ppermute | solution.py:373
  32.8 1.8 %collective-permute-start.7 = (bf16[2,256,256]{2,1,0:T(8,128)(2,1)S(1)}, bf16[2,256,256]{2,1,0:T(8,128)(2,1)S(1)}, u32[]{:S(2)}, u32[]{:S(2)}) collective-permute-start(bf16[2,256,256]{2,1,0:T(8,128)(2,1)S(1)} %get-tuple-element.42), channel_id=1, source_target_pairs={{0,12},{4,8},{8,4},{12,0},{1,13},{5,9},{9,5},{13,1},{2,14},{6,10},... | collective-permute-start | bytes 786440 | tf_op jit(solution)/shard_map/ppermute | solution.py:373
  34.6 0.0 collective-permute-done.9.refs_1_
  34.6 2.3 %collective-permute-start.8 = (bf16[2,256,256]{2,1,0:T(8,128)(2,1)S(1)}, bf16[2,256,256]{2,1,0:T(8,128)(2,1)S(1)}, u32[]{:S(2)}, u32[]{:S(2)}) collective-permute-start(bf16[2,256,256]{2,1,0:T(8,128)(2,1)S(1)} %get-tuple-element.43), channel_id=1, source_target_pairs={{0,8},{4,12},{8,0},{12,4},{1,9},{5,13},{9,1},{13,5},{2,10},{6,14},... | collective-permute-start | bytes 786440 | tf_op jit(solution)/shard_map/ppermute | solution.py:373
  36.9 3.4 %collective-permute-done.10.refs_2_ = bf16[128,1024]{1,0:T(8,128)(2,1)S(1)} collective-permute-done((bf16[128,1024]{1,0:T(8,128)(2,1)S(1)}, bf16[128,1024]{1,0:T(8,128)(2,1)S(1)}, u32[]{:S(2)}, u32[]{:S(2)}) %collective-permute-start.10) | collective-permute-done | bytes 262176 | tf_op jit(solution)/shard_map/ppermute | solution.py:364
  40.3 1.9 %collective-permute-done.11.refs_3_ = bf16[128,1024]{1,0:T(8,128)(2,1)S(1)} collective-permute-done((bf16[128,1024]{1,0:T(8,128)(2,1)S(1)}, bf16[128,1024]{1,0:T(8,128)(2,1)S(1)}, u32[]{:S(2)}, u32[]{:S(2)}) %collective-permute-start.11) | collective-permute-done | bytes 262176 | tf_op jit(solution)/shard_map/ppermute | solution.py:364
  42.2 0.0 collective-permute-done.7.refs_2_.refs_5_
  42.2 0.1 shard_map.102
  42.3 0.1 collective-permute-start.12
  42.5 2.5 %collective-permute-start.13 = (bf16[32,1024]{1,0:T(8,128)(2,1)S(1)}, bf16[32,1024]{1,0:T(8,128)(2,1)S(1)}, u32[]{:S(2)}, u32[]{:S(2)}) collective-permute-start(bf16[32,1024]{1,0:T(8,128)(2,1)S(1)} %get-tuple-element.51), channel_id=1, source_target_pairs={{0,96},{16,112},{32,64},{48,80},{64,32},{80,48},{96,0},{112,16},{1... | collective-permute-start | bytes 196616 | tf_op jit(solution)/shard_map/ppermute | solution.py:382
  44.9 0.2 collective-permute-start.14
  45.1 1.2 %collective-permute-done.8.refs_3_.refs_4_ = bf16[2,256,256]{2,1,0:T(8,128)(2,1)S(1)} collective-permute-done((bf16[2,256,256]{2,1,0:T(8,128)(2,1)S(1)}, bf16[2,256,256]{2,1,0:T(8,128)(2,1)S(1)}, u32[]{:S(2)}, u32[]{:S(2)}) %collective-permute-start.8) | collective-permute-done | bytes 262176 | tf_op jit(solution)/shard_map/ppermute | solution.py:373
  46.3 1.6 %collective-permute-done.12.refs_1_ = bf16[32,1024]{1,0:T(8,128)(2,1)S(1)} collective-permute-done((bf16[32,1024]{1,0:T(8,128)(2,1)S(1)}, bf16[32,1024]{1,0:T(8,128)(2,1)S(1)}, u32[]{:S(2)}, u32[]{:S(2)}) %collective-permute-start.12) | collective-permute-done | bytes 65568 | tf_op jit(solution)/shard_map/ppermute | solution.py:382
  47.9 0.6 collective-permute-done.14.refs_3_
  48.6 3.3 %collective-permute-start.15 = (bf16[32,1024]{1,0:T(8,128)(2,1)S(1)}, bf16[32,1024]{1,0:T(8,128)(2,1)S(1)}, u32[]{:S(2)}, u32[]{:S(2)}) collective-permute-start(bf16[32,1024]{1,0:T(8,128)(2,1)S(1)} %shard_map.103.refs_0_), channel_id=1, source_target_pairs={{0,128},{16,144},{32,160},{48,176},{64,192},{80,208},{96,224},{112... | collective-permute-start | bytes 196616 | tf_op jit(solution)/shard_map/ppermute | solution.py:384
  51.9 4.4 %collective-permute-done.15.refs_1_ = bf16[32,1024]{1,0:T(8,128)(2,1)S(1)} collective-permute-done((bf16[32,1024]{1,0:T(8,128)(2,1)S(1)}, bf16[32,1024]{1,0:T(8,128)(2,1)S(1)}, u32[]{:S(2)}, u32[]{:S(2)}) %collective-permute-start.15) | collective-permute-done | bytes 65568 | tf_op jit(solution)/shard_map/ppermute | solution.py:384
  56.3 2.6 %collective-permute-start.18 = (bf16[32,1024]{1,0:T(8,128)(2,1)S(1)}, bf16[32,1024]{1,0:T(8,128)(2,1)S(1)}, u32[]{:S(2)}, u32[]{:S(2)}) collective-permute-start(bf16[32,1024]{1,0:T(8,128)(2,1)S(1)} %shard_map.104.refs_0_), channel_id=1, source_target_pairs={{0,64},{16,80},{32,96},{48,112},{64,0},{80,16},{96,32},{112,48},{1... | collective-permute-start | bytes 196616 | tf_op jit(solution)/shard_map/ppermute | solution.py:386
  58.9 0.0 collective-permute-start.17
  58.9 0.4 collective-permute-start.16
  59.3 1.4 %collective-permute-done.18.refs_3_ = bf16[32,1024]{1,0:T(8,128)(2,1)S(1)} collective-permute-done((bf16[32,1024]{1,0:T(8,128)(2,1)S(1)}, bf16[32,1024]{1,0:T(8,128)(2,1)S(1)}, u32[]{:S(2)}, u32[]{:S(2)}) %collective-permute-start.18) | collective-permute-done | bytes 65568 | tf_op jit(solution)/shard_map/ppermute | solution.py:386
  60.7 4.4 %collective-permute-done.17.refs_2_ = bf16[32,1024]{1,0:T(8,128)(2,1)S(1)} collective-permute-done((bf16[32,1024]{1,0:T(8,128)(2,1)S(1)}, bf16[32,1024]{1,0:T(8,128)(2,1)S(1)}, u32[]{:S(2)}, u32[]{:S(2)}) %collective-permute-start.17) | collective-permute-done | bytes 65568 | tf_op jit(solution)/shard_map/ppermute | solution.py:386
  65.2 0.0 collective-permute-done.16.refs_1_
  65.2 0.1 collective-permute-start.21
  65.3 0.1 collective-permute-start.20
  65.4 3.1 %collective-permute-start.19 = (bf16[128,1024]{1,0:T(8,128)(2,1)S(1)}, bf16[128,1024]{1,0:T(8,128)(2,1)S(1)}, u32[]{:S(2)}, u32[]{:S(2)}) collective-permute-start(bf16[128,1024]{1,0:T(8,128)(2,1)S(1)} %shard_map.105.refs_0_), channel_id=1, source_target_pairs={{0,2},{1,3},{2,0},{3,1},{4,6},{5,7},{6,4},{7,5},{8,10},{9,11},{10,... | collective-permute-start | bytes 786440 | tf_op jit(solution)/shard_map/ppermute | solution.py:393
  68.5 9.8 %collective-permute-start.22 = (bf16[128,1024]{1,0:T(8,128)(2,1)S(1)}, bf16[128,1024]{1,0:T(8,128)(2,1)S(1)}, u32[]{:S(2)}, u32[]{:S(2)}) collective-permute-start(bf16[128,1024]{1,0:T(8,128)(2,1)S(1)} %shard_map.105.refs_0_), channel_id=1, source_target_pairs={{0,16},{16,0},{32,48},{48,32},{64,80},{80,64},{96,112},{112,96},{1... | collective-permute-start | bytes 786440 | tf_op jit(solution)/shard_map/ppermute | solution.py:282
  78.3 0.0 collective-permute-done.21.refs_3_
  78.3 2.2 %collective-permute-start.25 = (bf16[128,1024]{1,0:T(8,128)(2,1)S(1)}, bf16[128,1024]{1,0:T(8,128)(2,1)S(1)}, u32[]{:S(2)}, u32[]{:S(2)}) collective-permute-start(bf16[128,1024]{1,0:T(8,128)(2,1)S(1)} %collective-permute-done.21.refs_3_), channel_id=1, source_target_pairs={{0,16},{16,0},{32,48},{48,32},{64,80},{80,64},{96,112},{112,96},{1... | collective-permute-start | bytes 786440 | tf_op jit(solution)/shard_map/ppermute | solution.py:282
  80.5 0.0 collective-permute-done.20.refs_2_
  80.5 6.0 %collective-permute-start.24 = (bf16[128,1024]{1,0:T(8,128)(2,1)S(1)}, bf16[128,1024]{1,0:T(8,128)(2,1)S(1)}, u32[]{:S(2)}, u32[]{:S(2)}) collective-permute-start(bf16[128,1024]{1,0:T(8,128)(2,1)S(1)} %collective-permute-done.20.refs_2_), channel_id=1, source_target_pairs={{0,16},{16,0},{32,48},{48,32},{64,80},{80,64},{96,112},{112,96},{1... | collective-permute-start | bytes 786440 | tf_op jit(solution)/shard_map/ppermute | solution.py:282
  86.5 0.0 collective-permute-done.19.refs_1_
  86.5 0.0 collective-permute-start.23
  86.5 0.8 shard_map.101
  87.3 0.0 collective-permute-done.22.refs_4_
  87.3 0.0 collective-permute-done.25.refs_7_
  87.3 0.3 collective-permute-done.24.refs_6_
  87.7 0.4 collective-permute-done.23.refs_5_
  88.1 2.3 %shard_map.106 = (f32[3,1024,256]{2,1,0:T(8,128)}, f32[256,1024]{1,0:T(8,128)}) custom-call(bf16[128,1024]{1,0:T(8,128)(2,1)S(1)} %shard_map.105.refs_0_, bf16[128,1024]{1,0:T(8,128)(2,1)S(1)} %collective-permute-done.19.refs_1_, bf16[128,1024]{1,0:T(8,128)(2,1)S(1)} %collective-permute-done.20.refs_2_, ...), custom_call_target="tpu_custom_call" | custom-call | flops 1048576 | bytes 6291456 | tf_op jit(solution)/shard_map/pallas_call | solution.py:32
  (11 shorter events, 0.1 us)
Async XLA Ops:
  2.7 14.9 %copy-start.1 = (bf16[1,256,1024]{2,1,0:T(8,128)(2,1)S(1)}, bf16[1,256,1024]{2,1,0:T(8,128)(2,1)}, u32[]{:S(2)}) copy-start(bf16[1,256,1024]{2,1,0:T(8,128)(2,1)} %param.6) | copy-start | bytes 1572868
  2.7 14.9 %copy-start.2 = (bf16[1,256,1024]{2,1,0:T(8,128)(2,1)S(1)}, bf16[1,256,1024]{2,1,0:T(8,128)(2,1)}, u32[]{:S(2)}) copy-start(bf16[1,256,1024]{2,1,0:T(8,128)(2,1)} %param.11) | copy-start | bytes 1572868
  2.7 11.2 %collective-permute-start.1 = (bf16[2,256,256]{2,1,0:T(8,128)(2,1)S(1)}, bf16[2,256,256]{2,1,0:T(8,128)(2,1)S(1)}, u32[]{:S(2)}, u32[]{:S(2)}) collective-permute-start(bf16[2,256,256]{2,1,0:T(8,128)(2,1)S(1)} %shard_map.93.refs_5_.refs_3_), channel_id=1, source_target_pairs={{0,240},{16,32},{32,16},{48,64},{64,48},{80,96},{96,80},{112,128},... | collective-permute-start | bytes 786440 | tf_op jit(solution)/shard_map/ppermute | solution.py:321
  5.8 8.1 %collective-permute-start = (bf16[2,256,256]{2,1,0:T(8,128)(2,1)S(1)}, bf16[2,256,256]{2,1,0:T(8,128)(2,1)S(1)}, u32[]{:S(2)}, u32[]{:S(2)}) collective-permute-start(bf16[2,256,256]{2,1,0:T(8,128)(2,1)S(1)} %shard_map.93.refs_5_.refs_3_), channel_id=1, source_target_pairs={{0,16},{16,0},{32,48},{48,32},{64,80},{80,64},{96,112},{112,96},{1... | collective-permute-start | bytes 786440 | tf_op jit(solution)/shard_map/ppermute | solution.py:282
  13.8 4.6 %collective-permute-start.4 = (bf16[2,512,256]{2,1,0:T(8,128)(2,1)}, bf16[2,512,256]{2,1,0:T(8,128)(2,1)S(1)}, u32[]{:S(2)}, u32[]{:S(2)}) collective-permute-start(bf16[2,512,256]{2,1,0:T(8,128)(2,1)} %get-tuple-element.36), channel_id=1, source_target_pairs={{0,16},{16,0},{32,48},{48,32},{64,80},{80,64},{96,112},{112,96},{1... | collective-permute-start | bytes 1572872 | tf_op jit(solution)/shard_map/ppermute | solution.py:282
  17.1 2.1 %collective-permute-start.3 = (bf16[4,256,256]{2,1,0:T(8,128)(2,1)S(1)}, bf16[4,256,256]{2,1,0:T(8,128)(2,1)S(1)}, u32[]{:S(2)}, u32[]{:S(2)}) collective-permute-start(bf16[4,256,256]{2,1,0:T(8,128)(2,1)S(1)} %get-tuple-element.33.refs_2_.refs_0_), channel_id=1, source_target_pairs={{0,16},{16,0},{32,48},{48,32},{64,80},{80,64},{96,112},{112,96},{1... | collective-permute-start | bytes 1572872 | tf_op jit(solution)/shard_map/ppermute | solution.py:282
  17.6 6.1 %collective-permute-start.2 = (bf16[2,256,256]{2,1,0:T(8,128)(2,1)S(1)}, bf16[2,256,256]{2,1,0:T(8,128)(2,1)S(1)}, u32[]{:S(2)}, u32[]{:S(2)}) collective-permute-start(bf16[2,256,256]{2,1,0:T(8,128)(2,1)S(1)} %get-tuple-element.35), channel_id=1, source_target_pairs={{0,240},{16,32},{32,16},{48,64},{64,48},{80,96},{96,80},{112,128},... | collective-permute-start | bytes 786440 | tf_op jit(solution)/shard_map/ppermute | solution.py:336
  18.4 12.2 %copy-start = (bf16[3,1024,256]{2,1,0:T(8,128)(2,1)S(1)}, bf16[3,1024,256]{2,1,0:T(8,128)(2,1)}, u32[]{:S(2)}) copy-start(bf16[3,1024,256]{2,1,0:T(8,128)(2,1)} %refs_3_.1) | copy-start | bytes 4718596
  18.4 12.1 %copy-start.3 = (bf16[256,1024]{1,0:T(8,128)(2,1)S(1)}, bf16[256,1024]{1,0:T(8,128)(2,1)}, u32[]{:S(2)}) copy-start(bf16[256,1024]{1,0:T(8,128)(2,1)} %refs_2_.3) | copy-start | bytes 1572868
  23.8 2.3 %collective-permute-start.5 = (bf16[2,256,256]{2,1,0:T(8,128)(2,1)S(1)}, bf16[2,256,256]{2,1,0:T(8,128)(2,1)S(1)}, u32[]{:S(2)}, u32[]{:S(2)}) collective-permute-start(bf16[2,256,256]{2,1,0:T(8,128)(2,1)S(1)} %shard_map.98.refs_2_.refs_1_), channel_id=1, source_target_pairs={{0,16},{16,0},{32,48},{48,32},{64,80},{80,64},{96,112},{112,96},{1... | collective-permute-start | bytes 786440 | tf_op jit(solution)/shard_map/ppermute | solution.py:282
  26.5 8.1 %collective-permute-start.9 = (bf16[128,1024]{1,0:T(8,128)(2,1)S(1)}, bf16[128,1024]{1,0:T(8,128)(2,1)S(1)}, u32[]{:S(2)}, u32[]{:S(2)}) collective-permute-start(bf16[128,1024]{1,0:T(8,128)(2,1)S(1)} %get-tuple-element.46), channel_id=1, source_target_pairs={{0,1},{1,0},{2,3},{3,2},{4,5},{5,4},{6,7},{7,6},{8,9},{9,8},{10,11... | collective-permute-start | bytes 786440 | tf_op jit(solution)/shard_map/ppermute | solution.py:364
  27.9 12.4 %collective-permute-start.10 = (bf16[128,1024]{1,0:T(8,128)(2,1)S(1)}, bf16[128,1024]{1,0:T(8,128)(2,1)S(1)}, u32[]{:S(2)}, u32[]{:S(2)}) collective-permute-start(bf16[128,1024]{1,0:T(8,128)(2,1)S(1)} %get-tuple-element.47), channel_id=1, source_target_pairs={{0,3},{1,2},{2,1},{3,0},{4,7},{5,6},{6,5},{7,4},{8,11},{9,10},{10,... | collective-permute-start | bytes 786440 | tf_op jit(solution)/shard_map/ppermute | solution.py:364
  29.8 12.4 %collective-permute-start.11 = (bf16[128,1024]{1,0:T(8,128)(2,1)S(1)}, bf16[128,1024]{1,0:T(8,128)(2,1)S(1)}, u32[]{:S(2)}, u32[]{:S(2)}) collective-permute-start(bf16[128,1024]{1,0:T(8,128)(2,1)S(1)} %get-tuple-element.48), channel_id=1, source_target_pairs={{0,2},{1,3},{2,0},{3,1},{4,6},{5,7},{6,4},{7,5},{8,10},{9,11},{10,... | collective-permute-start | bytes 786440 | tf_op jit(solution)/shard_map/ppermute | solution.py:364
  31.3 10.9 %collective-permute-start.6 = (bf16[2,256,256]{2,1,0:T(8,128)(2,1)S(1)}, bf16[2,256,256]{2,1,0:T(8,128)(2,1)S(1)}, u32[]{:S(2)}, u32[]{:S(2)}) collective-permute-start(bf16[2,256,256]{2,1,0:T(8,128)(2,1)S(1)} %get-tuple-element.41), channel_id=1, source_target_pairs={{0,4},{4,0},{8,12},{12,8},{1,5},{5,1},{9,13},{13,9},{2,6},{6,2},{1... | collective-permute-start | bytes 786440 | tf_op jit(solution)/shard_map/ppermute | solution.py:373
  32.8 9.5 %collective-permute-start.7 = (bf16[2,256,256]{2,1,0:T(8,128)(2,1)S(1)}, bf16[2,256,256]{2,1,0:T(8,128)(2,1)S(1)}, u32[]{:S(2)}, u32[]{:S(2)}) collective-permute-start(bf16[2,256,256]{2,1,0:T(8,128)(2,1)S(1)} %get-tuple-element.42), channel_id=1, source_target_pairs={{0,12},{4,8},{8,4},{12,0},{1,13},{5,9},{9,5},{13,1},{2,14},{6,10},... | collective-permute-start | bytes 786440 | tf_op jit(solution)/shard_map/ppermute | solution.py:373
  34.6 11.7 %collective-permute-start.8 = (bf16[2,256,256]{2,1,0:T(8,128)(2,1)S(1)}, bf16[2,256,256]{2,1,0:T(8,128)(2,1)S(1)}, u32[]{:S(2)}, u32[]{:S(2)}) collective-permute-start(bf16[2,256,256]{2,1,0:T(8,128)(2,1)S(1)} %get-tuple-element.43), channel_id=1, source_target_pairs={{0,8},{4,12},{8,0},{12,4},{1,9},{5,13},{9,1},{13,5},{2,10},{6,14},... | collective-permute-start | bytes 786440 | tf_op jit(solution)/shard_map/ppermute | solution.py:373
  42.3 5.6 %collective-permute-start.12 = (bf16[32,1024]{1,0:T(8,128)(2,1)S(1)}, bf16[32,1024]{1,0:T(8,128)(2,1)S(1)}, u32[]{:S(2)}, u32[]{:S(2)}) collective-permute-start(bf16[32,1024]{1,0:T(8,128)(2,1)S(1)} %get-tuple-element.50), channel_id=1, source_target_pairs={{0,64},{16,80},{32,96},{48,112},{64,0},{80,16},{96,32},{112,48},{1... | collective-permute-start | bytes 196616 | tf_op jit(solution)/shard_map/ppermute | solution.py:382
  42.5 5.5 %collective-permute-start.13 = (bf16[32,1024]{1,0:T(8,128)(2,1)S(1)}, bf16[32,1024]{1,0:T(8,128)(2,1)S(1)}, u32[]{:S(2)}, u32[]{:S(2)}) collective-permute-start(bf16[32,1024]{1,0:T(8,128)(2,1)S(1)} %get-tuple-element.51), channel_id=1, source_target_pairs={{0,96},{16,112},{32,64},{48,80},{64,32},{80,48},{96,0},{112,16},{1... | collective-permute-start | bytes 196616 | tf_op jit(solution)/shard_map/ppermute | solution.py:382
  44.9 3.6 %collective-permute-start.14 = (bf16[32,1024]{1,0:T(8,128)(2,1)S(1)}, bf16[32,1024]{1,0:T(8,128)(2,1)S(1)}, u32[]{:S(2)}, u32[]{:S(2)}) collective-permute-start(bf16[32,1024]{1,0:T(8,128)(2,1)S(1)} %get-tuple-element.52), channel_id=1, source_target_pairs={{0,32},{16,48},{32,0},{48,16},{64,96},{80,112},{96,64},{112,80},{1... | collective-permute-start | bytes 196616 | tf_op jit(solution)/shard_map/ppermute | solution.py:382
  48.6 7.7 %collective-permute-start.15 = (bf16[32,1024]{1,0:T(8,128)(2,1)S(1)}, bf16[32,1024]{1,0:T(8,128)(2,1)S(1)}, u32[]{:S(2)}, u32[]{:S(2)}) collective-permute-start(bf16[32,1024]{1,0:T(8,128)(2,1)S(1)} %shard_map.103.refs_0_), channel_id=1, source_target_pairs={{0,128},{16,144},{32,160},{48,176},{64,192},{80,208},{96,224},{112... | collective-permute-start | bytes 196616 | tf_op jit(solution)/shard_map/ppermute | solution.py:384
  56.3 4.4 %collective-permute-start.18 = (bf16[32,1024]{1,0:T(8,128)(2,1)S(1)}, bf16[32,1024]{1,0:T(8,128)(2,1)S(1)}, u32[]{:S(2)}, u32[]{:S(2)}) collective-permute-start(bf16[32,1024]{1,0:T(8,128)(2,1)S(1)} %shard_map.104.refs_0_), channel_id=1, source_target_pairs={{0,64},{16,80},{32,96},{48,112},{64,0},{80,16},{96,32},{112,48},{1... | collective-permute-start | bytes 196616 | tf_op jit(solution)/shard_map/ppermute | solution.py:386
  58.9 6.3 %collective-permute-start.17 = (bf16[32,1024]{1,0:T(8,128)(2,1)S(1)}, bf16[32,1024]{1,0:T(8,128)(2,1)S(1)}, u32[]{:S(2)}, u32[]{:S(2)}) collective-permute-start(bf16[32,1024]{1,0:T(8,128)(2,1)S(1)} %shard_map.104.refs_0_), channel_id=1, source_target_pairs={{0,96},{16,112},{32,64},{48,80},{64,32},{80,48},{96,0},{112,16},{1... | collective-permute-start | bytes 196616 | tf_op jit(solution)/shard_map/ppermute | solution.py:386
  58.9 6.3 %collective-permute-start.16 = (bf16[32,1024]{1,0:T(8,128)(2,1)S(1)}, bf16[32,1024]{1,0:T(8,128)(2,1)S(1)}, u32[]{:S(2)}, u32[]{:S(2)}) collective-permute-start(bf16[32,1024]{1,0:T(8,128)(2,1)S(1)} %shard_map.104.refs_0_), channel_id=1, source_target_pairs={{0,32},{16,48},{32,0},{48,16},{64,96},{80,112},{96,64},{112,80},{1... | collective-permute-start | bytes 196616 | tf_op jit(solution)/shard_map/ppermute | solution.py:386
  65.2 13.1 %collective-permute-start.21 = (bf16[128,1024]{1,0:T(8,128)(2,1)S(1)}, bf16[128,1024]{1,0:T(8,128)(2,1)S(1)}, u32[]{:S(2)}, u32[]{:S(2)}) collective-permute-start(bf16[128,1024]{1,0:T(8,128)(2,1)S(1)} %shard_map.105.refs_0_), channel_id=1, source_target_pairs={{0,1},{1,0},{2,3},{3,2},{4,5},{5,4},{6,7},{7,6},{8,9},{9,8},{10,11... | collective-permute-start | bytes 786440 | tf_op jit(solution)/shard_map/ppermute | solution.py:393
  65.3 15.2 %collective-permute-start.20 = (bf16[128,1024]{1,0:T(8,128)(2,1)S(1)}, bf16[128,1024]{1,0:T(8,128)(2,1)S(1)}, u32[]{:S(2)}, u32[]{:S(2)}) collective-permute-start(bf16[128,1024]{1,0:T(8,128)(2,1)S(1)} %shard_map.105.refs_0_), channel_id=1, source_target_pairs={{0,3},{1,2},{2,1},{3,0},{4,7},{5,6},{6,5},{7,4},{8,11},{9,10},{10,... | collective-permute-start | bytes 786440 | tf_op jit(solution)/shard_map/ppermute | solution.py:393
  65.4 21.1 %collective-permute-start.19 = (bf16[128,1024]{1,0:T(8,128)(2,1)S(1)}, bf16[128,1024]{1,0:T(8,128)(2,1)S(1)}, u32[]{:S(2)}, u32[]{:S(2)}) collective-permute-start(bf16[128,1024]{1,0:T(8,128)(2,1)S(1)} %shard_map.105.refs_0_), channel_id=1, source_target_pairs={{0,2},{1,3},{2,0},{3,1},{4,6},{5,7},{6,4},{7,5},{8,10},{9,11},{10,... | collective-permute-start | bytes 786440 | tf_op jit(solution)/shard_map/ppermute | solution.py:393
  68.5 18.8 %collective-permute-start.22 = (bf16[128,1024]{1,0:T(8,128)(2,1)S(1)}, bf16[128,1024]{1,0:T(8,128)(2,1)S(1)}, u32[]{:S(2)}, u32[]{:S(2)}) collective-permute-start(bf16[128,1024]{1,0:T(8,128)(2,1)S(1)} %shard_map.105.refs_0_), channel_id=1, source_target_pairs={{0,16},{16,0},{32,48},{48,32},{64,80},{80,64},{96,112},{112,96},{1... | collective-permute-start | bytes 786440 | tf_op jit(solution)/shard_map/ppermute | solution.py:282
  78.3 9.0 %collective-permute-start.25 = (bf16[128,1024]{1,0:T(8,128)(2,1)S(1)}, bf16[128,1024]{1,0:T(8,128)(2,1)S(1)}, u32[]{:S(2)}, u32[]{:S(2)}) collective-permute-start(bf16[128,1024]{1,0:T(8,128)(2,1)S(1)} %collective-permute-done.21.refs_3_), channel_id=1, source_target_pairs={{0,16},{16,0},{32,48},{48,32},{64,80},{80,64},{96,112},{112,96},{1... | collective-permute-start | bytes 786440 | tf_op jit(solution)/shard_map/ppermute | solution.py:282
  80.5 7.2 %collective-permute-start.24 = (bf16[128,1024]{1,0:T(8,128)(2,1)S(1)}, bf16[128,1024]{1,0:T(8,128)(2,1)S(1)}, u32[]{:S(2)}, u32[]{:S(2)}) collective-permute-start(bf16[128,1024]{1,0:T(8,128)(2,1)S(1)} %collective-permute-done.20.refs_2_), channel_id=1, source_target_pairs={{0,16},{16,0},{32,48},{48,32},{64,80},{80,64},{96,112},{112,96},{1... | collective-permute-start | bytes 786440 | tf_op jit(solution)/shard_map/ppermute | solution.py:282
  86.5 1.5 %collective-permute-start.23 = (bf16[128,1024]{1,0:T(8,128)(2,1)S(1)}, bf16[128,1024]{1,0:T(8,128)(2,1)S(1)}, u32[]{:S(2)}, u32[]{:S(2)}) collective-permute-start(bf16[128,1024]{1,0:T(8,128)(2,1)S(1)} %collective-permute-done.19.refs_1_), channel_id=1, source_target_pairs={{0,16},{16,0},{32,48},{48,32},{64,80},{80,64},{96,112},{112,96},{1... | collective-permute-start | bytes 786440 | tf_op jit(solution)/shard_map/ppermute | solution.py:282
